TPU v7x, 32 devices: a whole 2x2x4 slice. The times are simulated.
32 devices in a mesh: rep: 4 (over y, x), fsdp: 8 (over z, core).
Axes of the slice: x: 2, y: 2, z: 4, core: 2. Of those that a mesh axis runs over, the one named last changes fastest.
Arguments:
- tokens: bfloat16 [4, 2048, 768], P('rep', 'fsdp'), may hold values from -6 to 6
- cotangent: bfloat16 [4, 2048, 768], P('rep', 'fsdp'), may hold values from -6 to 6
- lengths: int32 [4], P('rep'), may hold values from 1024 to 2048, as said below
- routes: int32 [4, 2048, 2], P('rep', 'fsdp'), may hold values from 0 to 3, all different within a row; in each aligned block of 256 rows (0 to 255, 256 to 511, ..., all dimensions but the last counted through in order) at most 160 rows name the same one
- gain_attn: bfloat16 [768], P('fsdp'), may hold values from 0.25 to 1.75
- gain_ffn: bfloat16 [768], P('fsdp'), may hold values from 0.25 to 1.75
- w_query: bfloat16 [768, 768], P('fsdp'), may hold values from -0.21875 to 0.21875
- w_key: bfloat16 [768, 768], P('fsdp'), may hold values from -0.21875 to 0.21875
- w_value: bfloat16 [768, 768], P('fsdp'), may hold values from -0.21875 to 0.21875
- w_out: bfloat16 [768, 768], P('fsdp'), may hold values from -1.75 to 1.75
- w_router: bfloat16 [768, 4], P('fsdp'), may hold values from -0.21875 to 0.21875
- shared_gate: bfloat16 [768, 2048], P('fsdp'), may hold values from -0.21875 to 0.21875
- shared_up: bfloat16 [768, 2048], P('fsdp'), may hold values from -0.21875 to 0.21875
- shared_down: bfloat16 [2048, 768], P('fsdp'), may hold values from -0.125 to 0.125
- expert_gate: bfloat16 [768, 8192], P(None, 'fsdp'), may hold values from -0.21875 to 0.21875
- expert_up: bfloat16 [768, 8192], P(None, 'fsdp'), may hold values from -0.21875 to 0.21875
- expert_down: bfloat16 [8192, 768], P('fsdp'), may hold values from -0.5 to 0.5
Outputs:
- output: bfloat16 [4, 2048, 768], P('rep', 'fsdp')
- input_grad: float32 [4, 2048, 768], P('rep', 'fsdp')
- grad_gain_attn: float32 [768], P('fsdp')
- grad_gain_ffn: float32 [768], P('fsdp')
- grad_w_query: float32 [768, 768], P('fsdp')
- grad_w_key: float32 [768, 768], P('fsdp')
- grad_w_value: float32 [768, 768], P('fsdp')
- grad_w_out: float32 [768, 768], P('fsdp')
- grad_w_router: float32 [768, 4], P('fsdp')
- grad_shared_gate: float32 [768, 2048], P('fsdp')
- grad_shared_up: float32 [768, 2048], P('fsdp')
- grad_shared_down: float32 [2048, 768], P('fsdp')
- grad_expert_gate: float32 [768, 8192], P(None, 'fsdp')
- grad_expert_up: float32 [768, 8192], P(None, 'fsdp')
- grad_expert_down: float32 [8192, 768], P('fsdp')
Inputs may be any that keep to these rules, and one draw needn't show every extreme that they name: `lengths`: each slot's live positions come first and its padded positions after them; in every draw one slot, drawn from the seed, is full. `routes`: each position names two different experts; in each aligned block of 256 positions of a slot no expert is named by more than 160 of them, and in some block one is named by exactly 160. Routes of padded positions are ignored.
All inputs are finite; a program needn't handle non-finite values.
Results may differ from a plain program's by a relative error of at most 0.02.
Values may be sent and summed in bfloat16 or wider, within the bound.
No kernel may reach another device: no remote copies, remote signals or barrier semaphores. Data moves between devices by JAX's collectives and lax.ppermute only.
A program may use at most 256 MiB of HBM per device.

v0:
```python
import jax
import jax.numpy as jnp
from jax import lax
from jax.sharding import PartitionSpec as P

HEADS = 12
HEAD_DIM = 64


EPSILON = 1e-06
ROPE_BASE = 10000.0
NEG_FILL = -1e30


def rms_norm(values, gain_vec):
    return (
        values * lax.rsqrt(jnp.mean(values * values, axis=-1, keepdims=True) + EPSILON) * gain_vec
    )


def rotate(values, positions, direction):
    half_dim = values.shape[-1] // 2
    frequency = ROPE_BASE ** (-jnp.arange(half_dim, dtype=jnp.float32) / half_dim)
    angles = positions.astype(jnp.float32)[:, None] * frequency[None, :]
    cosine = jnp.cos(angles)[:, None, :]
    sine_part = direction * jnp.sin(angles)[:, None, :]
    first_half = values[..., :half_dim]
    second = values[..., half_dim:]
    return jnp.concatenate(
        [first_half * cosine - second * sine_part, second * cosine + first_half * sine_part],
        axis=-1,
    )


def matmul(first_op, second_op):
    return jnp.dot(first_op, second_op, preferred_element_type=jnp.float32)


def matmul_tn(first_op, second_op):
    return lax.dot_general(
        first_op, second_op, (((0,), (0,)), ((), ())), preferred_element_type=jnp.float32
    )


def product_transposed_right(first_op, second_op):
    return lax.dot_general(
        first_op, second_op, (((1,), (1,)), ((), ())), preferred_element_type=jnp.float32
    )


def swiglu_grad(grad_inner, gate_act, up_act):
    _, pullback = jax.vjp(lambda gate_in, up_in: jax.nn.silu(gate_in) * up_in, gate_act, up_act)
    grad_gate, grad_up = pullback(grad_inner.astype(jnp.float32))
    return (grad_gate.astype(jnp.bfloat16), grad_up.astype(jnp.bfloat16))


def masked_scores(queries, key_blk, query_pos, key_pos, length):
    scores = (
        jnp.einsum("qhd,khd->hqk", queries, key_blk, preferred_element_type=jnp.float32) * 0.125
    )
    allowed = (key_pos[None, :] <= query_pos[:, None]) & (key_pos[None, :] < length)
    return (jnp.where(allowed[None], scores, NEG_FILL), allowed)


def score_grads(
    queries, grad_mixed, log_norm, row_delta, key_blk, value_blk, query_pos, key_pos, length
):
    scores, allowed = masked_scores(queries, key_blk, query_pos, key_pos, length)
    attention_weights_soft = jnp.exp(scores - log_norm[..., None])
    grad_probs = jnp.einsum(
        "qhd,khd->hqk", grad_mixed, value_blk, preferred_element_type=jnp.float32
    )
    grad_scores = jnp.where(
        allowed[None], attention_weights_soft * (grad_probs - row_delta[..., None]), 0.0
    )
    return (attention_weights_soft.astype(jnp.bfloat16), grad_scores.astype(jnp.bfloat16))


def block_rows(array_in, block_idx, rows_block, axis_num):
    return lax.dynamic_slice_in_dim(array_in, block_idx * rows_block, rows_block, axis_num)


def attention_forward(queries, key_all, value_all, query_pos, length, rows_block, block_count):

    def attention_block_pos(block_idx):
        return block_idx * rows_block + jnp.arange(rows_block, dtype=jnp.int32)

    def stats_step(block_idx, state_pair):
        running_maximum, run_sum = state_pair
        scores, _ = masked_scores(
            queries,
            block_rows(key_all, block_idx, rows_block, 0),
            query_pos,
            attention_block_pos(block_idx),
            length,
        )
        new_max = jnp.maximum(running_maximum, jnp.max(scores, axis=-1))
        run_sum = run_sum * jnp.exp(running_maximum - new_max) + jnp.sum(
            jnp.exp(scores - new_max[..., None]), axis=-1
        )
        return (new_max, run_sum)

    start_max = jnp.full((HEADS, queries.shape[0]), NEG_FILL, jnp.float32)
    running_maximum, run_sum = lax.fori_loop(
        0, block_count, stats_step, (start_max, jnp.zeros_like(start_max))
    )
    log_norm = running_maximum + jnp.log(run_sum)

    def value_step(block_idx, running):
        scores, _ = masked_scores(
            queries,
            block_rows(key_all, block_idx, rows_block, 0),
            query_pos,
            attention_block_pos(block_idx),
            length,
        )
        attention_weights_soft = jnp.exp(scores - log_norm[..., None]).astype(jnp.bfloat16)
        return running + jnp.einsum(
            "hqk,khd->qhd",
            attention_weights_soft,
            block_rows(value_all, block_idx, rows_block, 0),
            preferred_element_type=jnp.float32,
        )

    mixed_heads = lax.fori_loop(0, block_count, value_step, jnp.zeros(queries.shape, jnp.float32))
    return (mixed_heads, log_norm)


def on_device(
    tokens,
    cotangent,
    lengths,
    routes,
    gain_attn,
    gain_ffn,
    w_query,
    w_key,
    w_value,
    w_out,
    w_router,
    shared_gate,
    shared_up,
    shared_down,
    expert_gate,
    expert_up,
    expert_down,
):
    rows_dev = tokens.shape[1]
    width = tokens.shape[2]
    groups = lax.axis_size("fsdp")
    experts = w_router.shape[1]
    capacity = min(rows_dev, 5 * rows_dev // (2 * experts))
    length = lengths[0]
    first_row = lax.axis_index("fsdp") * rows_dev
    positions = first_row + jnp.arange(rows_dev, dtype=jnp.int32)
    token_live = positions < length
    live_col = token_live.astype(jnp.float32)[:, None]
    inputs = tokens[0].astype(jnp.float32)
    full_weights = (
        lax.all_gather(gain_attn, "fsdp", axis=0, tiled=True),
        lax.all_gather(gain_ffn, "fsdp", axis=0, tiled=True),
        lax.all_gather(w_query, "fsdp", axis=0, tiled=True),
        lax.all_gather(w_key, "fsdp", axis=0, tiled=True),
        lax.all_gather(w_value, "fsdp", axis=0, tiled=True),
        lax.all_gather(w_out, "fsdp", axis=0, tiled=True),
        lax.all_gather(w_router, "fsdp", axis=0, tiled=True),
        lax.all_gather(shared_gate, "fsdp", axis=0, tiled=True),
        lax.all_gather(shared_up, "fsdp", axis=0, tiled=True),
        lax.all_gather(shared_down, "fsdp", axis=0, tiled=True),
    )
    (
        full_gain_attn,
        full_gain_ffn,
        full_query,
        full_key,
        full_value,
        full_out,
        full_router,
        full_gate,
        full_up,
        full_down,
    ) = full_weights
    gain_one = full_gain_attn.astype(jnp.float32)
    gain_two = full_gain_ffn.astype(jnp.float32)
    normed = rms_norm(inputs, gain_one).astype(jnp.bfloat16)
    queries = rotate(
        matmul(normed, full_query).reshape(rows_dev, HEADS, HEAD_DIM), positions, 1.0
    ).astype(jnp.bfloat16)
    key_rows = rotate(
        matmul(normed, full_key).reshape(rows_dev, HEADS, HEAD_DIM), positions, 1.0
    ).astype(jnp.bfloat16)
    value_rows = matmul(normed, full_value).astype(jnp.bfloat16)
    key_all, value_all = (
        lax.all_gather(key_rows.reshape(rows_dev, width), "fsdp", axis=0, tiled=True),
        lax.all_gather(value_rows, "fsdp", axis=0, tiled=True),
    )
    seq_len = key_all.shape[0]
    key_all = key_all.reshape(seq_len, HEADS, HEAD_DIM)
    value_all = value_all.reshape(seq_len, HEADS, HEAD_DIM)
    rows_block = min(512, seq_len)
    block_count = (first_row + rows_dev - 1) // rows_block + 1
    mixed_heads, log_norm = attention_forward(
        queries, key_all, value_all, positions, length, rows_block, block_count
    )
    mixed_b = mixed_heads.reshape(rows_dev, width).astype(jnp.bfloat16)
    hidden = inputs + matmul(mixed_b, full_out)
    normed_ffn = rms_norm(hidden, gain_two).astype(jnp.bfloat16)
    router_probs = jax.nn.softmax(matmul(normed_ffn, full_router), axis=-1)
    shared_gate_act = matmul(normed_ffn, full_gate)
    shared_up_act = matmul(normed_ffn, full_up)
    shared_inner = (jax.nn.silu(shared_gate_act) * shared_up_act).astype(jnp.bfloat16)
    shared_result = matmul(shared_inner, full_down)
    route_rows = routes[0]
    flat_expert = route_rows.reshape(-1)
    flat_token = jnp.arange(2 * rows_dev, dtype=jnp.int32) // 2
    flat_live = jnp.repeat(token_live, 2)
    expert_ids = jnp.arange(experts, dtype=jnp.int32)
    onehot = ((flat_expert[:, None] == expert_ids[None, :]) & flat_live[:, None]).astype(jnp.int32)
    slot_rank = jnp.sum(jnp.cumsum(onehot, axis=0) * onehot, axis=1) - 1
    slot_index = jnp.where(flat_live, flat_expert * capacity + slot_rank, experts * capacity)
    slot_fetch = jnp.minimum(slot_index, experts * capacity - 1)
    flat_gate = jnp.take_along_axis(router_probs, route_rows, axis=1).reshape(-1) * flat_live

    def to_experts(rows_flat):
        packed = (
            jnp.zeros((experts * capacity, width), jnp.bfloat16)
            .at[slot_index]
            .set(rows_flat, mode="drop")
        )
        packed = jnp.broadcast_to(
            packed.reshape(experts, 1, capacity, width), (experts, 2, capacity, width)
        )
        return packed.reshape(groups, capacity, width)

    def from_experts(split_parts_pair):
        summed_halves = jnp.sum(
            split_parts_pair.reshape(experts, 2, capacity, width).astype(jnp.float32), axis=1
        )
        return summed_halves.reshape(experts * capacity, width)[slot_fetch]

    received = lax.all_to_all(
        to_experts(normed_ffn[flat_token]), "fsdp", split_axis=0, concat_axis=0, tiled=True
    )
    rows_in = received.reshape(groups * capacity, width)
    expert_gate_act = matmul(rows_in, expert_gate)
    expert_up_act = matmul(rows_in, expert_up)
    expert_inner = (jax.nn.silu(expert_gate_act) * expert_up_act).astype(jnp.bfloat16)
    half_out = (
        matmul(expert_inner, expert_down).astype(jnp.bfloat16).reshape(groups, capacity, width)
    )
    returned = lax.all_to_all(half_out, "fsdp", split_axis=0, concat_axis=0, tiled=True)
    expert_rows = from_experts(returned)
    moe_result = jnp.sum((flat_gate[:, None] * expert_rows).reshape(rows_dev, 2, width), axis=1)
    output = (
        (live_col * (hidden + shared_result + moe_result))
        .astype(jnp.bfloat16)
        .reshape(1, rows_dev, width)
    )
    back_weights = (
        lax.all_gather(gain_attn, "fsdp", axis=0, tiled=True),
        lax.all_gather(gain_ffn, "fsdp", axis=0, tiled=True),
        lax.all_gather(w_query, "fsdp", axis=0, tiled=True),
        lax.all_gather(w_key, "fsdp", axis=0, tiled=True),
        lax.all_gather(w_value, "fsdp", axis=0, tiled=True),
        lax.all_gather(w_out, "fsdp", axis=0, tiled=True),
        lax.all_gather(w_router, "fsdp", axis=0, tiled=True),
        lax.all_gather(shared_gate, "fsdp", axis=0, tiled=True),
        lax.all_gather(shared_up, "fsdp", axis=0, tiled=True),
        lax.all_gather(shared_down, "fsdp", axis=0, tiled=True),
    )
    (
        back_gain_attn,
        back_gain_ffn,
        back_query,
        back_key,
        back_value,
        back_out,
        back_router,
        back_gate,
        back_up,
        back_down,
    ) = back_weights
    grad_out = live_col * cotangent[0].astype(jnp.float32)
    grad_out_b = grad_out.astype(jnp.bfloat16)
    grad_shared_down = matmul_tn(shared_inner, grad_out_b)
    gate_in_grad, up_in_grad = swiglu_grad(
        product_transposed_right(grad_out_b, back_down).astype(jnp.bfloat16),
        shared_gate_act,
        shared_up_act,
    )
    grad_shared_gate = matmul_tn(normed_ffn, gate_in_grad)
    grad_shared_up = matmul_tn(normed_ffn, up_in_grad)
    grad_normed_ffn = product_transposed_right(gate_in_grad, back_gate) + product_transposed_right(
        up_in_grad, back_up
    )
    token_grads = grad_out[flat_token]
    grad_gates = jnp.sum(expert_rows * token_grads, axis=1) * flat_live
    grad_rows_out = (flat_gate[:, None] * token_grads).astype(jnp.bfloat16)
    grad_received = lax.all_to_all(
        to_experts(grad_rows_out), "fsdp", split_axis=0, concat_axis=0, tiled=True
    )
    grad_half = grad_received.reshape(groups * capacity, width)
    grad_expert_down = matmul_tn(expert_inner, grad_half)
    expert_gate_in_grad, expert_up_in_grad = swiglu_grad(
        product_transposed_right(grad_half, expert_down).astype(jnp.bfloat16),
        expert_gate_act,
        expert_up_act,
    )
    grad_expert_gate = matmul_tn(rows_in, expert_gate_in_grad)
    grad_expert_up = matmul_tn(rows_in, expert_up_in_grad)
    rows_grad = (
        (
            product_transposed_right(expert_gate_in_grad, expert_gate)
            + product_transposed_right(expert_up_in_grad, expert_up)
        )
        .astype(jnp.bfloat16)
        .reshape(groups, capacity, width)
    )
    grad_back = lax.all_to_all(rows_grad, "fsdp", split_axis=0, concat_axis=0, tiled=True)
    routed_grad = from_experts(grad_back) * flat_live[:, None]
    grad_normed_ffn = grad_normed_ffn + jnp.sum(routed_grad.reshape(rows_dev, 2, width), axis=1)
    route_hot = (route_rows[:, :, None] == expert_ids[None, None, :]).astype(jnp.float32)
    grad_rprobs = jnp.sum(route_hot * grad_gates.reshape(rows_dev, 2)[:, :, None], axis=1)
    grad_logits = (
        router_probs * (grad_rprobs - jnp.sum(router_probs * grad_rprobs, axis=1, keepdims=True))
    ).astype(jnp.bfloat16)
    grad_w_router = matmul_tn(normed_ffn, grad_logits)
    grad_normed_ffn = grad_normed_ffn + product_transposed_right(grad_logits, back_router)
    _, second_pullback = jax.vjp(rms_norm, hidden, back_gain_ffn.astype(jnp.float32))
    hidden_part, grad_gain_ffn = second_pullback(grad_normed_ffn)
    grad_hidden = grad_out + hidden_part
    grad_hidden_b = grad_hidden.astype(jnp.bfloat16)
    grad_w_out = matmul_tn(mixed_b, grad_hidden_b)
    grad_mixed = (
        product_transposed_right(grad_hidden_b, back_out)
        .astype(jnp.bfloat16)
        .reshape(rows_dev, HEADS, HEAD_DIM)
    )
    row_delta = jnp.sum(grad_mixed.astype(jnp.float32) * mixed_heads, axis=-1).T

    def body_block_pos(block_idx):
        return block_idx * rows_block + jnp.arange(rows_block, dtype=jnp.int32)

    query_zero = jnp.zeros((rows_dev, HEADS, HEAD_DIM), jnp.float32)
    full_zero = jnp.zeros((seq_len, HEADS, HEAD_DIM), jnp.float32)

    def key_step(block_idx, state_set):
        grad_queries, key_full, value_full = state_set
        key_blk = block_rows(key_all, block_idx, rows_block, 0)
        value_blk = block_rows(value_all, block_idx, rows_block, 0)
        probs_b, scores_b = score_grads(
            queries,
            grad_mixed,
            log_norm,
            row_delta,
            key_blk,
            value_blk,
            positions,
            body_block_pos(block_idx),
            length,
        )
        grad_queries = grad_queries + jnp.einsum(
            "hqk,khd->qhd", scores_b, key_blk, preferred_element_type=jnp.float32
        )
        key_part = jnp.einsum("hqk,qhd->khd", scores_b, queries, preferred_element_type=jnp.float32)
        value_part = jnp.einsum(
            "hqk,qhd->khd", probs_b, grad_mixed, preferred_element_type=jnp.float32
        )
        key_full = lax.dynamic_update_slice_in_dim(key_full, key_part, block_idx * rows_block, 0)
        value_full = lax.dynamic_update_slice_in_dim(
            value_full, value_part, block_idx * rows_block, 0
        )
        return (grad_queries, key_full, value_full)

    grad_queries, key_full, value_full = lax.fori_loop(
        0, block_count, key_step, (query_zero, full_zero, full_zero)
    )
    grad_keys, grad_values = (
        lax.psum_scatter(key_full.reshape(seq_len, width), "fsdp", scatter_dimension=0, tiled=True),
        lax.psum_scatter(
            value_full.reshape(seq_len, width), "fsdp", scatter_dimension=0, tiled=True
        ),
    )
    query_grad_b = (
        rotate(grad_queries * 0.125, positions, -1.0).reshape(rows_dev, width).astype(jnp.bfloat16)
    )
    key_grad_b = (
        rotate(grad_keys.reshape(rows_dev, HEADS, HEAD_DIM) * 0.125, positions, -1.0)
        .reshape(rows_dev, width)
        .astype(jnp.bfloat16)
    )
    value_grad_b = grad_values.astype(jnp.bfloat16)
    grad_w_query = matmul_tn(normed, query_grad_b)
    grad_w_key = matmul_tn(normed, key_grad_b)
    grad_w_value = matmul_tn(normed, value_grad_b)
    grad_normed = (
        product_transposed_right(query_grad_b, back_query)
        + product_transposed_right(key_grad_b, back_key)
        + product_transposed_right(value_grad_b, back_value)
    )
    _, first_pullback = jax.vjp(rms_norm, inputs, back_gain_attn.astype(jnp.float32))
    input_part, grad_gain_attn = first_pullback(grad_normed)
    input_grad = (grad_hidden + input_part).reshape(1, rows_dev, width)
    (
        shard_gain_attn,
        shard_gain_ffn,
        shard_query,
        shard_key,
        shard_value,
        shard_out,
        shard_router,
        shard_gate,
        shard_up,
        shard_down,
    ) = (
        lax.psum_scatter(grad_gain_attn, "fsdp", scatter_dimension=0, tiled=True),
        lax.psum_scatter(grad_gain_ffn, "fsdp", scatter_dimension=0, tiled=True),
        lax.psum_scatter(grad_w_query, "fsdp", scatter_dimension=0, tiled=True),
        lax.psum_scatter(grad_w_key, "fsdp", scatter_dimension=0, tiled=True),
        lax.psum_scatter(grad_w_value, "fsdp", scatter_dimension=0, tiled=True),
        lax.psum_scatter(grad_w_out, "fsdp", scatter_dimension=0, tiled=True),
        lax.psum_scatter(grad_w_router, "fsdp", scatter_dimension=0, tiled=True),
        lax.psum_scatter(grad_shared_gate, "fsdp", scatter_dimension=0, tiled=True),
        lax.psum_scatter(grad_shared_up, "fsdp", scatter_dimension=0, tiled=True),
        lax.psum_scatter(grad_shared_down, "fsdp", scatter_dimension=0, tiled=True),
    )
    (
        sum_gain_attn,
        sum_gain_ffn,
        sum_query,
        sum_key,
        sum_value,
        sum_out,
        sum_router,
        sum_gate,
        sum_up,
        sum_down,
        sum_egate,
        summed_expert_up_weight,
        sum_edown,
    ) = lax.psum(
        (
            shard_gain_attn,
            shard_gain_ffn,
            shard_query,
            shard_key,
            shard_value,
            shard_out,
            shard_router,
            shard_gate,
            shard_up,
            shard_down,
            grad_expert_gate,
            grad_expert_up,
            grad_expert_down,
        ),
        "rep",
    )
    return (
        output,
        input_grad,
        sum_gain_attn,
        sum_gain_ffn,
        sum_query,
        sum_key,
        sum_value,
        sum_out,
        sum_router,
        sum_gate,
        sum_up,
        sum_down,
        sum_egate,
        summed_expert_up_weight,
        sum_edown,
    )


def solution(mesh):
    in_specs = (
        P("rep", "fsdp", None),
        P("rep", "fsdp", None),
        P("rep"),
        P("rep", "fsdp", None),
        P("fsdp"),
        P("fsdp"),
        P("fsdp", None),
        P("fsdp", None),
        P("fsdp", None),
        P("fsdp", None),
        P("fsdp", None),
        P("fsdp", None),
        P("fsdp", None),
        P("fsdp", None),
        P(None, "fsdp"),
        P(None, "fsdp"),
        P("fsdp", None),
    )
    out_specs = (
        P("rep", "fsdp", None),
        P("rep", "fsdp", None),
        P("fsdp"),
        P("fsdp"),
        P("fsdp", None),
        P("fsdp", None),
        P("fsdp", None),
        P("fsdp", None),
        P("fsdp", None),
        P("fsdp", None),
        P("fsdp", None),
        P("fsdp", None),
        P(None, "fsdp"),
        P(None, "fsdp"),
        P("fsdp", None),
    )
    return jax.shard_map(
        on_device, mesh=mesh, in_specs=in_specs, out_specs=out_specs, check_vma=False
    )
```

profile of v0, /device:TPU:0, one launch (start us, length us, event | category | flops | bytes accessed | tf_op | source)
XLA Modules:
  0.0 1417.6 jit_solution(5288683629052058043)
XLA Ops:
  13.3 18.2 %all-reduce.7 = (bf16[768]{0:T(1024)(128)(2,1)S(1)}, bf16[768]{0:T(1024)(128)(2,1)S(1)}) all-reduce(bf16[768]{0:T(1024)(128)(2,1)S(1)} %dynamic-update-slice, bf16[768]{0:T(1024)(128)(2,1)S(1)} %dynamic-update-slice.1), channel_id=1, replica_groups=mesh['rep'=4,'fsdp'=8] {'fsdp'}, use_global_device_ids=true, to_apply=%add | all-reduce | flops 1536 | bytes 6144
  36.8 22.4 %all-gather.15.cloned.1.call-done = bf16[768,768]{1,0:T(8,128)(2,1)} async-done(((bf16[96,768]{1,0:T(8,128)(2,1)}), bf16[768,768]{1,0:T(8,128)(2,1)}) %all-gather.15.cloned.1.call-update) | async-done | bytes 1179664 | tf_op jit(solution)/shard_map/all_gather | solution.py:163
  64.5 18.8 %all-gather.11.cloned.1.call-done = bf16[768,768]{1,0:T(8,128)(2,1)} async-done(((bf16[96,768]{1,0:T(8,128)(2,1)}), bf16[768,768]{1,0:T(8,128)(2,1)}) %all-gather.11.cloned.1.call-update) | async-done | bytes 1179664 | tf_op jit(solution)/shard_map/all_gather | solution.py:164
  83.3 2.5 convolution_convert_fusion.4
  91.1 33.2 %all-gather.17.cloned.1.call-done = bf16[2048,768]{0,1:T(8,128)(2,1)} async-done(((bf16[256,768]{0,1:T(8,128)(2,1)}), bf16[2048,768]{0,1:T(8,128)(2,1)}) %all-gather.17.cloned.1.call-update) | async-done | bytes 3145744 | tf_op jit(solution)/shard_map/all_gather | solution.py:194
  124.3 4.5 while.39
  128.9 34.1 %all-gather.13.cloned.1.call-done = bf16[2048,768]{1,0:T(8,128)(2,1)} async-done(((bf16[256,768]{1,0:T(8,128)(2,1)}), bf16[2048,768]{1,0:T(8,128)(2,1)}) %all-gather.13.cloned.1.call-update) | async-done | bytes 3145744 | tf_op jit(solution)/shard_map/all_gather | solution.py:195
  162.9 4.6 copy.79
  167.6 4.7 while.40
  168.6 3.6 fusion.231
  173.0 13.0 all-gather.21.cloned.1.call-done
  188.9 6.7 scatter_custom_fusion
  195.6 2.6 broadcast_in_dim.93
  198.2 3.6 all-to-all-start
  202.6 70.8 %all-to-all-done = bf16[8,160,768]{2,1,0:T(8,128)(2,1)S(1)} async-done(((bf16[8,160,768]{2,1,0:T(8,128)(2,1)}), bf16[8,160,768]{2,1,0:T(8,128)(2,1)S(1)}, u32[]{:S(2)}, u32[]{:S(2)}) %all-to-all-start) | async-done | bytes 1966112 | tf_op jit(solution)/shard_map/all_to_all | solution.py:241
  273.4 4.4 fusion.136
  277.8 4.9 multiply_convert_fusion
  282.7 3.5 convolution_convert_fusion.1
  286.2 4.5 all-to-all-start.1
  291.6 2.6 gather_fusion.1
  294.9 56.0 %all-gather = bf16[8,96,4]{1,2,0:T(4,128)(2,1)S(1)} all-gather(bf16[1,96,4]{1,2,0:T(4,128)(2,1)S(1)} %bitcast.307), channel_id=1, replica_groups=mesh['rep'=4,'fsdp'=8] {'fsdp'}, dimensions={0}, use_global_device_ids=true | all-gather | bytes 6912 | tf_op jit(solution)/shard_map/all_gather | solution.py:166
  352.2 10.1 all-to-all-done.1
  364.4 2.6 gather_fusion
  370.1 4.8 gather_fusion.3
  375.0 4.0 scatter_custom_fusion.1
  379.0 2.6 broadcast_in_dim.146
  381.6 6.9 all-to-all-start.2
  389.2 70.8 %all-to-all-done.2 = bf16[8,160,768]{2,1,0:T(8,128)(2,1)S(1)} async-done(((bf16[8,160,768]{2,1,0:T(8,128)(2,1)}), bf16[8,160,768]{2,1,0:T(8,128)(2,1)S(1)}, u32[]{:S(2)}, u32[]{:S(2)}) %all-to-all-start.2) | async-done | bytes 1966112 | tf_op jit(solution)/shard_map/all_to_all | solution.py:299
  460.1 7.6 fusion.54
  470.3 3.6 add_convert_fusion
  473.9 4.5 all-to-all-start.3
  478.5 3.0 convolution_convert_fusion.2
  481.5 4.5 fusion.135
  486.1 6.1 fusion.62
  494.1 30.5 %all-to-all-done.3 = bf16[8,160,768]{2,1,0:T(8,128)(2,1)} async-done(((bf16[8,160,768]{2,1,0:T(8,128)(2,1)}), bf16[8,160,768]{2,1,0:T(8,128)(2,1)}, u32[]{:S(2)}, u32[]{:S(2)}) %all-to-all-start.3) | async-done | bytes 1966112 | tf_op jit(solution)/shard_map/all_to_all | solution.py:319
  526.7 2.6 gather_fusion.2
  533.5 4.4 fusion.64
  541.0 3.5 broadcast_in_dim.148
  544.5 3.5 broadcast_in_dim.148.clone
  547.9 13.9 while.41
  551.4 3.4 fusion.243
  559.0 2.9 bitcast_dynamic-update-slice_fusion.5
  563.2 3.7 fusion.141
  568.1 5.4 fusion.127
  574.8 3.7 fusion.104
  581.6 89.5 %reduce-scatter.13.cloned.1.call-done = f32[256,768]{0,1:T(8,128)} async-done(((f32[2048,768]{0,1:T(8,128)}), f32[256,768]{0,1:T(8,128)}) %reduce-scatter.13.cloned.1.call-update) | async-done | bytes 786448 | tf_op jit(solution)/shard_map/reduce_scatter | solution.py:379
  677.0 64.7 %reduce-scatter.15.cloned.1.call-done = f32[256,768]{0,1:T(8,128)} async-done(((f32[2048,768]{0,1:T(8,128)}), f32[256,768]{0,1:T(8,128)}) %reduce-scatter.15.cloned.1.call-update) | async-done | bytes 786448 | tf_op jit(solution)/shard_map/reduce_scatter | solution.py:380
  741.7 3.2 fusion.98
  746.4 6.0 fusion.142
  752.4 3.9 fusion.143
  756.4 4.0 fusion.144
  760.4 51.7 %reduce-scatter.25.cloned.1.call-done = f32[96,2048]{1,0:T(8,128)} async-done(((f32[768,2048]{1,0:T(8,128)}), f32[96,2048]{1,0:T(8,128)}) %reduce-scatter.25.cloned.1.call-update) | async-done | bytes 786448 | tf_op jit(solution)/shard_map/reduce_scatter | solution.py:423
  812.0 70.5 %reduce-scatter.27.cloned.1.call-done = f32[96,2048]{1,0:T(8,128)} async-done(((f32[768,2048]{1,0:T(8,128)}), f32[96,2048]{1,0:T(8,128)}) %reduce-scatter.27.cloned.1.call-update) | async-done | bytes 786448 | tf_op jit(solution)/shard_map/reduce_scatter | solution.py:424
  882.5 70.3 %reduce-scatter.29.cloned.1.call-done = f32[256,768]{1,0:T(8,128)} async-done(((f32[2048,768]{1,0:T(8,128)}), f32[256,768]{1,0:T(8,128)}) %reduce-scatter.29.cloned.1.call-update) | async-done | bytes 786448 | tf_op jit(solution)/shard_map/reduce_scatter | solution.py:425
  952.9 36.8 %reduce-scatter.23.cloned.1.call-done = f32[96,768]{1,0:T(8,128)} async-done(((f32[768,768]{1,0:T(8,128)}), f32[96,768]{1,0:T(8,128)}) %reduce-scatter.23.cloned.1.call-update) | async-done | bytes 294928 | tf_op jit(solution)/shard_map/reduce_scatter | solution.py:421
  989.7 37.6 %reduce-scatter.17.cloned.1.call-done = f32[96,768]{1,0:T(8,128)} async-done(((f32[768,768]{1,0:T(8,128)}), f32[96,768]{1,0:T(8,128)}) %reduce-scatter.17.cloned.1.call-update) | async-done | bytes 294928 | tf_op jit(solution)/shard_map/reduce_scatter | solution.py:418
  1027.3 37.8 %reduce-scatter.19.cloned.1.call-done = f32[96,768]{1,0:T(8,128)} async-done(((f32[768,768]{1,0:T(8,128)}), f32[96,768]{1,0:T(8,128)}) %reduce-scatter.19.cloned.1.call-update) | async-done | bytes 294928 | tf_op jit(solution)/shard_map/reduce_scatter | solution.py:419
  1065.1 37.8 %reduce-scatter.21.cloned.1.call-done = f32[96,768]{1,0:T(8,128)} async-done(((f32[768,768]{1,0:T(8,128)}), f32[96,768]{1,0:T(8,128)}) %reduce-scatter.21.cloned.1.call-update) | async-done | bytes 294928 | tf_op jit(solution)/shard_map/reduce_scatter | solution.py:420
  1106.6 3.5 multiply_reduce_fusion.2
  1110.1 3.7 fusion.68
  1113.9 21.3 %reduce-scatter.31.cloned.1.call-done = f32[96,4]{1,0:T(8,128)} async-done(((f32[768,4]{1,0:T(8,128)}), f32[96,4]{1,0:T(8,128)}) %reduce-scatter.31.cloned.1.call-update) | async-done | bytes 1552
  1138.3 14.1 all-reduce.4
  1152.6 10.8 all-reduce.5
  1164.5 228.7 %all-reduce.10.cloned.1.call-done = (f32[96,768]{1,0:T(8,128)}, f32[96,768]{1,0:T(8,128)}, f32[96,768]{1,0:T(8,128)}, f32[96,768]{1,0:T(8,128)}, f32[96,2048]{1,...) async-done(((f32[96,768]{1,0:T(8,128)}, f32[96,768]{1,0:T(8,128)}, ...) | async-done | bytes 12976144 | tf_op jit(solution)/shard_map/psum | solution.py:441
  (382 shorter events, 98.4 us)
Async XLA Ops:
  7.2 275.5 %copy-start = (bf16[1024,768]{1,0:T(8,128)(2,1)S(1)}, bf16[1024,768]{1,0:T(8,128)(2,1)}, u32[]{:S(2)}) copy-start(bf16[1024,768]{1,0:T(8,128)(2,1)} %param.39) | copy-start | bytes 4718596
  7.2 28.0 %all-gather.19.cloned.1.call-start = ((), (), s32[]{:S(2)}) async-start(), calls=%async_computation.18 | async-start | bytes 1327104 | tf_op jit(solution)/shard_map/all_gather | solution.py:162
  7.9 51.2 %all-gather.15.cloned.1.call-start = ((), (), s32[]{:S(2)}) async-start(), calls=%async_computation.16 | async-start | bytes 1327104 | tf_op jit(solution)/shard_map/all_gather | solution.py:163
  8.7 74.6 %all-gather.11.cloned.1.call-start = ((), (), s32[]{:S(2)}) async-start(), calls=%async_computation.14 | async-start | bytes 1327104 | tf_op jit(solution)/shard_map/all_gather | solution.py:164
  9.4 114.9 %all-gather.17.cloned.1.call-start = ((), (), s32[]{:S(2)}) async-start(), calls=%async_computation.17 | async-start | bytes 3538944 | tf_op jit(solution)/shard_map/all_gather | solution.py:194
  12.4 49.1 %copy-start.4 = (bf16[1,256,768]{2,1,0:T(8,128)(2,1)S(1)}, bf16[1,256,768]{2,1,0:T(8,128)(2,1)}, u32[]{:S(2)}) copy-start(bf16[1,256,768]{2,1,0:T(8,128)(2,1)} %param.23) | copy-start | bytes 1179652
  31.5 51.7 %copy-start.57 = (f32[768]{0:T(1024)}, f32[768]{0:T(1024)S(1)}, u32[]{:S(2)}) copy-start(f32[768]{0:T(1024)S(1)} %convert_element_type.197) | copy-start | bytes 9220
  33.2 50.0 %copy-start.60 = (f32[256]{0:T(256)}, f32[256]{0:T(256)S(1)}, u32[]{:S(2)}) copy-start(f32[256]{0:T(256)S(1)} %fusion.121) | copy-start | bytes 3076
  34.1 29.3 %copy-start.55 = (f32[256,32]{0,1:T(8,128)}, f32[256,32]{0,1:T(8,128)S(1)}, u32[]{:S(2)}) copy-start(f32[256,32]{0,1:T(8,128)S(1)} %get-tuple-element.393) | copy-start | bytes 98308
  63.4 23.0 %copy-start.68 = (s32[1,256,2]{1,2,0:T(2,128)S(1)}, s32[1,256,2]{1,2,0:T(2,128)}, u32[]{:S(2)}) copy-start(s32[1,256,2]{1,2,0:T(2,128)} %param.26) | copy-start | bytes 6148
  64.4 98.5 %all-gather.13.cloned.1.call-start = ((), (), s32[]{:S(2)}) async-start(), calls=%async_computation.15 | async-start | bytes 3538944 | tf_op jit(solution)/shard_map/all_gather | solution.py:195
  85.8 100.2 %all-gather.21.cloned.1.call-start = ((), (), s32[]{:S(2)}) async-start(), calls=%async_computation.19 | async-start | bytes 1327104 | tf_op jit(solution)/shard_map/all_gather | solution.py:165
  87.5 203.9 %copy-start.64 = (f32[256]{0:T(256)}, f32[256]{0:T(256)S(1)}, u32[]{:S(2)}) copy-start(f32[256]{0:T(256)S(1)} %get-tuple-element.369) | copy-start | bytes 3076
  172.9 22.7 %copy-start.2 = (bf16[256,12,64]{0,2,1:T(8,128)(2,1)}, bf16[256,12,64]{0,2,1:T(8,128)(2,1)S(1)}, u32[]{:S(2)}) copy-start(bf16[256,12,64]{0,2,1:T(8,128)(2,1)S(1)} %get-tuple-element.778) | copy-start | bytes 1179652
  172.9 22.7 %copy-start.21 = (f32[256,12,64]{0,2,1:T(8,128)}, f32[256,12,64]{0,2,1:T(8,128)S(1)}, u32[]{:S(2)}) copy-start(f32[256,12,64]{0,2,1:T(8,128)S(1)} %get-tuple-element.179) | copy-start | bytes 2359300
  173.0 25.2 %copy-start.29 = (bf16[256,12,64]{0,2,1:T(8,128)(2,1)}, bf16[256,12,64]{0,2,1:T(8,128)(2,1)S(1)}, u32[]{:S(2)}) copy-start(bf16[256,12,64]{0,2,1:T(8,128)(2,1)S(1)} %convert_element_type.205) | copy-start | bytes 1179652
  188.9 9.3 copy-start.15
  198.2 75.2 %all-to-all-start = ((bf16[8,160,768]{2,1,0:T(8,128)(2,1)}), bf16[8,160,768]{2,1,0:T(8,128)(2,1)S(1)}, u32[]{:S(2)}, u32[]{:S(2)}) async-start(bf16[8,160,768]{2,1,0:T(8,128)(2,1)} %bitcast.279), calls=%async_computation | async-start | bytes 3932160 | tf_op jit(solution)/shard_map/all_to_all | solution.py:241
  201.8 276.6 %all-gather.27.cloned.1.call-start = ((), (), s32[]{:S(2)}) async-start(), calls=%async_computation.22 | async-start | bytes 3538944 | tf_op jit(solution)/shard_map/all_gather | solution.py:169
  286.2 5.2 copy-start.26
  286.2 76.1 %all-to-all-start.1 = ((bf16[8,160,768]{2,1,0:T(8,128)(2,1)}), bf16[8,160,768]{2,1,0:T(8,128)(2,1)}, u32[]{:S(2)}, u32[]{:S(2)}) async-start(bf16[8,160,768]{2,1,0:T(8,128)(2,1)} %bitcast.296), calls=%async_computation.1 | async-start | bytes 3932160 | tf_op jit(solution)/shard_map/all_to_all | solution.py:251
  290.7 190.8 %all-gather.25.cloned.1.call-start = ((), (), s32[]{:S(2)}) async-start(), calls=%async_computation.21 | async-start | bytes 3538944 | tf_op jit(solution)/shard_map/all_gather | solution.py:168
  291.6 59.6 %copy-start.89 = (s32[512,1]{0,1:T(1,128)S(1)}, s32[512,1]{0,1:T(1,128)}, u32[]{:S(2)}) copy-start(s32[512,1]{0,1:T(1,128)} %get-tuple-element.389) | copy-start | bytes 6148
  291.6 59.7 %copy-start.16 = (bf16[256,768]{1,0:T(8,128)(2,1)S(1)}, bf16[256,768]{1,0:T(8,128)(2,1)}, u32[]{:S(2)}) copy-start(bf16[256,768]{1,0:T(8,128)(2,1)} %copy-done.15) | copy-start | bytes 1179652
  351.3 15.7 %copy-start.77 = (s32[1024]{0:T(1024)}, s32[1024]{0:T(1024)S(1)}, u32[]{:S(2)}) copy-start(s32[1024]{0:T(1024)S(1)} %pad_clamp_fusion) | copy-start | bytes 12292
  375.0 6.7 copy-start.19
  381.6 78.4 %all-to-all-start.2 = ((bf16[8,160,768]{2,1,0:T(8,128)(2,1)}), bf16[8,160,768]{2,1,0:T(8,128)(2,1)S(1)}, u32[]{:S(2)}, u32[]{:S(2)}) async-start(bf16[8,160,768]{2,1,0:T(8,128)(2,1)} %bitcast.280), calls=%async_computation.2 | async-start | bytes 3932160 | tf_op jit(solution)/shard_map/all_to_all | solution.py:299
  388.5 97.5 %all-gather.23.cloned.1.call-start = ((), (), s32[]{:S(2)}) async-start(), calls=%async_computation.20 | async-start | bytes 3538944 | tf_op jit(solution)/shard_map/all_gather | solution.py:167
  460.1 7.6 copy-start.47
  460.1 7.6 copy-start.96
  473.9 50.8 %all-to-all-start.3 = ((bf16[8,160,768]{2,1,0:T(8,128)(2,1)}), bf16[8,160,768]{2,1,0:T(8,128)(2,1)}, u32[]{:S(2)}, u32[]{:S(2)}) async-start(bf16[8,160,768]{2,1,0:T(8,128)(2,1)} %bitcast.32), calls=%async_computation.3 | async-start | bytes 3932160 | tf_op jit(solution)/shard_map/all_to_all | solution.py:319
  478.4 192.8 %reduce-scatter.13.cloned.1.call-start = ((), (), s32[]{:S(2)}) async-start(), calls=%async_computation.23 | async-start | bytes 7077888 | tf_op jit(solution)/shard_map/reduce_scatter | solution.py:379
  486.1 6.1 copy-start.95
  494.1 32.6 %copy-start.78 = (s32[1024]{0:T(1024)S(1)}, s32[1024]{0:T(1024)}, u32[]{:S(2)}) copy-start(s32[1024]{0:T(1024)} %copy-done.77) | copy-start | bytes 12292
  494.1 43.7 %copy-start.69 = (bf16[256,4]{0,1:T(4,128)(2,1)}, bf16[256,4]{0,1:T(4,128)(2,1)S(1)}, u32[]{:S(2)}) copy-start(bf16[256,4]{0,1:T(4,128)(2,1)S(1)} %multiply_convert_fusion.5) | copy-start | bytes 6148
  533.5 5.5 copy-start.80
  539.3 39.3 %copy-start.10 = (f32[256,768]{1,0:T(8,128)}, f32[256,768]{1,0:T(8,128)S(1)}, u32[]{:S(2)}) copy-start(f32[256,768]{1,0:T(8,128)S(1)} %fusion.81) | copy-start | bytes 2359300
  561.9 179.8 %reduce-scatter.15.cloned.1.call-start = ((), (), s32[]{:S(2)}) async-start(), calls=%async_computation.24 | async-start | bytes 7077888 | tf_op jit(solution)/shard_map/reduce_scatter | solution.py:380
  562.6 249.4 %reduce-scatter.25.cloned.1.call-start = ((), (), s32[]{:S(2)}) async-start(), calls=%async_computation.29 | async-start | bytes 7077888 | tf_op jit(solution)/shard_map/reduce_scatter | solution.py:423
  566.9 315.7 %reduce-scatter.27.cloned.1.call-start = ((), (), s32[]{:S(2)}) async-start(), calls=%async_computation.30 | async-start | bytes 7077888 | tf_op jit(solution)/shard_map/reduce_scatter | solution.py:424
  573.5 379.4 %reduce-scatter.29.cloned.1.call-start = ((), (), s32[]{:S(2)}) async-start(), calls=%async_computation.31 | async-start | bytes 7077888 | tf_op jit(solution)/shard_map/reduce_scatter | solution.py:425
  578.6 411.1 %reduce-scatter.23.cloned.1.call-start = ((), (), s32[]{:S(2)}) async-start(), calls=%async_computation.28 | async-start | bytes 2654208 | tf_op jit(solution)/shard_map/reduce_scatter | solution.py:421
  581.4 90.9 %copy-start.56 = (f32[256,32]{0,1:T(8,128)S(1)}, f32[256,32]{0,1:T(8,128)}, u32[]{:S(2)}) copy-start(f32[256,32]{0,1:T(8,128)} %copy-done.55) | copy-start | bytes 98308
  581.4 90.9 %copy-start.59 = (f32[256,32]{0,1:T(8,128)S(1)}, f32[256,32]{0,1:T(8,128)}, u32[]{:S(2)}) copy-start(f32[256,32]{0,1:T(8,128)} %get-tuple-element.391) | copy-start | bytes 98308
  581.4 445.9 %reduce-scatter.17.cloned.1.call-start = ((), (), s32[]{:S(2)}) async-start(), calls=%async_computation.25 | async-start | bytes 2654208 | tf_op jit(solution)/shard_map/reduce_scatter | solution.py:418
  581.6 91.1 %copy-start.5 = (bf16[1,256,768]{2,1,0:T(8,128)(2,1)S(1)}, bf16[1,256,768]{2,1,0:T(8,128)(2,1)}, u32[]{:S(2)}) copy-start(bf16[1,256,768]{2,1,0:T(8,128)(2,1)} %param.23) | copy-start | bytes 1179652
  581.6 91.1 %copy-start.58 = (f32[768]{0:T(1024)S(1)}, f32[768]{0:T(1024)}, u32[]{:S(2)}) copy-start(f32[768]{0:T(1024)} %copy-done.57) | copy-start | bytes 9220
  581.6 91.1 %copy-start.61 = (f32[256]{0:T(256)S(1)}, f32[256]{0:T(256)}, u32[]{:S(2)}) copy-start(f32[256]{0:T(256)} %copy-done.60) | copy-start | bytes 3076
  674.8 390.3 %reduce-scatter.19.cloned.1.call-start = ((), (), s32[]{:S(2)}) async-start(), calls=%async_computation.26 | async-start | bytes 2654208 | tf_op jit(solution)/shard_map/reduce_scatter | solution.py:419
  676.9 68.2 %copy-start.70 = (bf16[256,4]{0,1:T(4,128)(2,1)S(1)}, bf16[256,4]{0,1:T(4,128)(2,1)}, u32[]{:S(2)}) copy-start(bf16[256,4]{0,1:T(4,128)(2,1)} %copy-done.69) | copy-start | bytes 6148
  676.9 426.0 %reduce-scatter.21.cloned.1.call-start = ((), (), s32[]{:S(2)}) async-start(), calls=%async_computation.27 | async-start | bytes 2654208 | tf_op jit(solution)/shard_map/reduce_scatter | solution.py:420
  744.9 390.3 %reduce-scatter.31.cloned.1.call-start = ((), (), s32[]{:S(2)}) async-start(), calls=%async_computation.32 | async-start | bytes 442368
  746.2 646.9 %all-reduce.10.cloned.1.call-start = ((), (), s32[]{:S(2)}) async-start(), calls=%async_computation.33 | async-start | bytes 25952256 | tf_op jit(solution)/shard_map/psum | solution.py:441
  746.4 6.0 copy-start.43
  1104.3 5.8 copy-start.14
  1110.1 25.9 %copy-start.25 = (bf16[768,768]{1,0:T(8,128)(2,1)S(1)}, bf16[768,768]{1,0:T(8,128)(2,1)}, u32[]{:S(2)}) copy-start(bf16[768,768]{1,0:T(8,128)(2,1)} %all-gather.19.cloned.1.call-done) | copy-start | bytes 3538948
  1110.1 25.9 %copy-start.34 = (bf16[256,12,64]{0,2,1:T(8,128)(2,1)S(1)}, bf16[256,12,64]{0,2,1:T(8,128)(2,1)}, u32[]{:S(2)}) copy-start(bf16[256,12,64]{0,2,1:T(8,128)(2,1)} %copy-done.33) | copy-start | bytes 1179652
  1113.9 22.7 %copy-start.23 = (bf16[768,768]{1,0:T(8,128)(2,1)S(1)}, bf16[768,768]{1,0:T(8,128)(2,1)}, u32[]{:S(2)}) copy-start(bf16[768,768]{1,0:T(8,128)(2,1)} %all-gather.15.cloned.1.call-done) | copy-start | bytes 3538948
  1113.9 22.7 %copy-start.32 = (bf16[256,12,64]{0,2,1:T(8,128)(2,1)S(1)}, bf16[256,12,64]{0,2,1:T(8,128)(2,1)}, u32[]{:S(2)}) copy-start(bf16[256,12,64]{0,2,1:T(8,128)(2,1)} %copy-done.31) | copy-start | bytes 1179652
  1137.6 25.7 %copy-start.82 = (f32[256]{0:T(256)S(1)}, f32[256]{0:T(256)}, u32[]{:S(2)}) copy-start(f32[256]{0:T(256)} %copy-done.81) | copy-start | bytes 3076
  1137.6 25.8 %copy-start.11 = (f32[256,768]{1,0:T(8,128)S(1)}, f32[256,768]{1,0:T(8,128)}, u32[]{:S(2)}) copy-start(f32[256,768]{1,0:T(8,128)} %copy-done.10) | copy-start | bytes 2359300
  1393.2 7.1 copy-start.54
  1393.2 8.0 copy-start.53
  1393.2 8.8 copy-start.52
  (64 other events, 175.1 us)
Sparse Core Ops, SparseCore 0:
  9.7 25.4 all-gather.18
  36.8 22.2 all-gather.14
  60.8 22.4 all-gather.10
  85.3 39.0 all-gather.16
  126.4 36.5 all-gather.12
  164.4 21.5 all-gather.20
  204.3 68.4 all-gather.26
  293.2 68.4 all-gather.24
  391.0 68.4 all-gather.22
  562.0 109.0 reduce-scatter.12
  673.5 68.1 reduce-scatter.14
  743.8 68.1 reduce-scatter.24
  814.3 68.1 reduce-scatter.26
  884.7 68.1 reduce-scatter.28
  955.1 34.6 reduce-scatter.22
  991.9 35.3 reduce-scatter.16
  1029.5 35.5 reduce-scatter.18
  1067.3 35.5 reduce-scatter.20
  1105.1 30.0 reduce-scatter.30
  1142.0 251.0 all-reduce.9
where the time goes:
time: 1430 us; the launch traced here: 1420 us
  waiting for transfers between devices  1060 us (74%)
  matrix products  114 us (8%)
  blocking collectives  99 us (7%)
  local copies, waits for them, and re-layouts  77.9 us (5%)
  other arithmetic  30.1 us (2%)
  starting transfers between devices  20.9 us (1%)
  between operations  18 us (1%)
    psum x1, waiting for transfers between devices, on_device(): lax.psum((shard_gain_attn, shard_gain_ffn, shard_query, shard_key, shard_...  229 us
    reduce_scatter x1, waiting for transfers between devices, on_device(): lax.psum_scatter(key_full.reshape(seq_len, width), 'fsdp', scatter_dimens...  89.5 us
    all_to_all x1, waiting for transfers between devices, on_device(): lax.all_to_all(to_experts(grad_rows_out), 'fsdp', split_axis=0, concat_ax...  70.8 us
    all_to_all x1, waiting for transfers between devices, on_device(): lax.all_to_all(to_experts(normed_ffn[flat_token]), 'fsdp', split_axis=0,...  70.8 us
    reduce_scatter x1, waiting for transfers between devices, on_device(): lax.psum_scatter(grad_shared_up, 'fsdp', scatter_dimension=0, tiled=True)  70.5 us
    reduce_scatter x1, waiting for transfers between devices, on_device(): lax.psum_scatter(grad_shared_down, 'fsdp', scatter_dimension=0, tiled=True)  70.3 us
    reduce_scatter x1, waiting for transfers between devices, on_device(): lax.psum_scatter(value_full.reshape(seq_len, width), 'fsdp', scatter_dime...  64.7 us
    all_gather x1, blocking collectives, on_device(): lax.all_gather(w_router, 'fsdp', axis=0, tiled=True)  56 us
  transfers between devices with their start and end apart: 24, of which 21 were waited for; matrix products, arithmetic and copies ran while one was open for 10% of the time, Pallas kernels for 0%

commit v1 on v0

v1 whole, which is shorter than its diff:
```python
import functools

import jax
import jax.numpy as jnp
from jax import lax
from jax.experimental import pallas as pl
from jax.experimental.pallas import tpu as pltpu
from jax.sharding import PartitionSpec as P

HEADS = 12
HEAD_DIM = 64

EPSILON = 1e-06
ROPE_BASE = 10000.0
NEG_FILL = -1e30
F32 = jnp.float32
BF16 = jnp.bfloat16


def contract(first_op, second_op, first_dim, second_dim):
    return lax.dot_general(
        first_op,
        second_op,
        (((first_dim,), (second_dim,)), ((), ())),
        preferred_element_type=F32,
    )


def matmul(first_op, second_op):
    return contract(first_op, second_op, 1, 0)


def matmul_tn(first_op, second_op):
    return contract(first_op, second_op, 0, 0)


def matmul_nt(first_op, second_op):
    return contract(first_op, second_op, 1, 1)


def inv_rms(values):
    return lax.rsqrt(jnp.mean(values * values, axis=-1, keepdims=True) + EPSILON)


def rms_back(values, scale, grad_scaled):
    return scale * grad_scaled - values * (
        scale * scale * scale * jnp.mean(grad_scaled * values, axis=-1, keepdims=True)
    )


def swiglu(gate_act, up_act):
    return (jax.nn.silu(gate_act) * up_act).astype(BF16)


def swiglu_grad(grad_inner, gate_act, up_act):
    grad_inner = grad_inner.astype(F32)
    sig = jax.nn.sigmoid(gate_act)
    grad_gate = grad_inner * up_act * (sig * (1.0 + gate_act * (1.0 - sig)))
    grad_up = grad_inner * (gate_act * sig)
    return (grad_gate.astype(BF16), grad_up.astype(BF16))


def rope_tables(seq_len):
    half_dim = HEAD_DIM // 2
    frequency = ROPE_BASE ** (-jnp.arange(half_dim, dtype=F32) / half_dim)
    angles = frequency[:, None] * jnp.arange(seq_len, dtype=F32)[None, :]
    return (jnp.cos(angles), jnp.sin(angles))


def rotate_cols(values, cosine, sine):
    rows, seq_len = values.shape
    split = values.reshape(rows // HEAD_DIM, 2, HEAD_DIM // 2, seq_len)
    first, second = (split[:, 0], split[:, 1])
    turned = jnp.stack(
        [first * cosine - second * sine, second * cosine + first * sine], axis=1
    )
    return turned.reshape(rows, seq_len)


def attn_forward_kernel(len_ref, q_ref, k_ref, v_ref, o_ref, l_ref, *, heads, blk):
    row = pl.program_id(0)
    length = len_ref[0]
    queries = q_ref[...]

    def step(masked, col, state):
        cols = pl.ds(pl.multiple_of(col * blk, blk), blk)
        keys, values = (k_ref[:, cols], v_ref[:, cols])
        if masked:
            key_pos = col * blk + lax.broadcasted_iota(jnp.int32, (blk, blk), 0)
            query_pos = row * blk + lax.broadcasted_iota(jnp.int32, (blk, blk), 1)
            allowed = (key_pos <= query_pos) & (key_pos < length)
        result = []
        for head in range(heads):
            top, total, acc = state[head]
            part = slice(head * HEAD_DIM, (head + 1) * HEAD_DIM)
            scores = matmul_tn(keys[part], queries[part])
            if masked:
                scores = jnp.where(allowed, scores, NEG_FILL)
            new_top = jnp.maximum(top, jnp.max(scores, axis=0, keepdims=True))
            probs = jnp.exp(scores - new_top)
            shrink = jnp.exp(top - new_top)
            total = total * shrink + jnp.sum(probs, axis=0, keepdims=True)
            acc = acc * shrink + matmul(values[part], probs.astype(BF16))
            result.append((new_top, total, acc))
        return tuple(result)

    start = tuple(
        (
            jnp.full((1, blk), NEG_FILL, F32),
            jnp.zeros((1, blk), F32),
            jnp.zeros((HEAD_DIM, blk), F32),
        )
        for _ in range(heads)
    )
    whole = jnp.minimum(row, length // blk)
    end = jnp.minimum(row + 1, (length + blk - 1) // blk)
    state = lax.fori_loop(0, whole, functools.partial(step, False), start)
    state = lax.fori_loop(whole, end, functools.partial(step, True), state)
    for head in range(heads):
        top, total, acc = state[head]
        o_ref[head * HEAD_DIM : (head + 1) * HEAD_DIM, :] = acc * (1.0 / total)
        l_ref[head : head + 1, :] = top + jnp.log(total)


def attn_backward_kernel(
    len_ref, q_ref, k_ref, v_ref, o_ref, l_ref, do_ref, dq_ref, dk_ref, dv_ref, *, heads, blk
):
    row = pl.program_id(0)
    length = len_ref[0]

    @pl.when(row == 0)
    def _():
        dk_ref[...] = jnp.zeros_like(dk_ref)
        dv_ref[...] = jnp.zeros_like(dv_ref)

    parts = [slice(head * HEAD_DIM, (head + 1) * HEAD_DIM) for head in range(heads)]
    queries, grad_out = (q_ref[...], do_ref[...])
    deltas = [
        jnp.sum(grad_out[part].astype(F32) * o_ref[part, :], axis=0, keepdims=True)
        for part in parts
    ]
    log_norms = [l_ref[head : head + 1, :] for head in range(heads)]

    def step(masked, col, state):
        cols = pl.ds(pl.multiple_of(col * blk, blk), blk)
        keys, values = (k_ref[:, cols], v_ref[:, cols])
        if masked:
            key_pos = col * blk + lax.broadcasted_iota(jnp.int32, (blk, blk), 0)
            query_pos = row * blk + lax.broadcasted_iota(jnp.int32, (blk, blk), 1)
            allowed = (key_pos <= query_pos) & (key_pos < length)
        result = []
        for head, part in enumerate(parts):
            scores = matmul_tn(keys[part], queries[part])
            grad_probs = matmul_tn(values[part], grad_out[part])
            probs = jnp.exp(scores - log_norms[head])
            if masked:
                probs = jnp.where(allowed, probs, 0.0)
            grad_scores = (probs * (grad_probs - deltas[head])).astype(BF16)
            dv_ref[part, cols] += matmul_nt(grad_out[part], probs.astype(BF16))
            dk_ref[part, cols] += matmul_nt(queries[part], grad_scores)
            result.append(state[head] + matmul(keys[part], grad_scores))
        return tuple(result)

    start = tuple(jnp.zeros((HEAD_DIM, blk), F32) for _ in range(heads))
    whole = jnp.minimum(row, length // blk)
    end = jnp.minimum(row + 1, (length + blk - 1) // blk)
    state = lax.fori_loop(0, whole, functools.partial(step, False), start)
    state = lax.fori_loop(whole, end, functools.partial(step, True), state)
    for head, part in enumerate(parts):
        dq_ref[part, :] = state[head]


def attn_specs(rows, seq_len, heads, blk):
    block = pl.BlockSpec((rows, blk), lambda i, _: (0, i))
    whole = pl.BlockSpec((rows, seq_len), lambda i, _: (0, 0))
    stats = pl.BlockSpec((heads, blk), lambda i, _: (0, i))
    return (block, whole, stats)


def attn_cost(rows, seq_len, heads, products):
    pairs = heads * seq_len * seq_len // 2
    return pl.CostEstimate(
        flops=2 * products * pairs * 256, bytes_accessed=16 * rows * seq_len, transcendentals=pairs
    )


def attn_forward(length, queries, keys, values):
    rows, seq_len = queries.shape
    heads, blk = (rows // HEAD_DIM, min(512, seq_len))
    block, whole, stats = attn_specs(rows, seq_len, heads, blk)
    return pl.pallas_call(
        functools.partial(attn_forward_kernel, heads=heads, blk=blk),
        out_shape=(
            jax.ShapeDtypeStruct((rows, seq_len), F32),
            jax.ShapeDtypeStruct((heads, seq_len), F32),
        ),
        grid_spec=pltpu.PrefetchScalarGridSpec(
            num_scalar_prefetch=1,
            grid=(seq_len // blk,),
            in_specs=[block, whole, whole],
            out_specs=(block, stats),
        ),
        compiler_params=pltpu.CompilerParams(vmem_limit_bytes=40 << 20),
        cost_estimate=attn_cost(rows, seq_len, heads, 2),
        name="attn_forward",
    )(length, queries, keys, values)


def attn_backward(length, queries, keys, values, mixed, log_norm, grad_mixed):
    rows, seq_len = queries.shape
    heads, blk = (rows // HEAD_DIM, min(512, seq_len))
    block, whole, stats = attn_specs(rows, seq_len, heads, blk)
    return pl.pallas_call(
        functools.partial(attn_backward_kernel, heads=heads, blk=blk),
        out_shape=(jax.ShapeDtypeStruct((rows, seq_len), F32),) * 3,
        grid_spec=pltpu.PrefetchScalarGridSpec(
            num_scalar_prefetch=1,
            grid=(seq_len // blk,),
            in_specs=[block, whole, whole, block, stats, block],
            out_specs=(block, whole, whole),
        ),
        compiler_params=pltpu.CompilerParams(vmem_limit_bytes=40 << 20),
        cost_estimate=attn_cost(rows, seq_len, heads, 5),
        name="attn_backward",
    )(length, queries, keys, values, mixed, log_norm, grad_mixed)


def gather_rows(values):
    return lax.all_gather(values, "fsdp", axis=0, tiled=True)


def exchange(chunks):
    return lax.all_to_all(chunks, "fsdp", split_axis=0, concat_axis=0, tiled=True)


def scatter_sum(values):
    return lax.psum_scatter(values, "fsdp", scatter_dimension=0, tiled=True)


def on_device(
    tokens,
    cotangent,
    lengths,
    routes,
    gain_attn,
    gain_ffn,
    w_query,
    w_key,
    w_value,
    w_out,
    w_router,
    shared_gate,
    shared_up,
    shared_down,
    expert_gate,
    expert_up,
    expert_down,
):
    rows_dev, width = tokens.shape[1:]
    groups = lax.axis_size("fsdp")
    me = lax.axis_index("fsdp")
    seq_len = groups * rows_dev
    experts = w_router.shape[1]
    capacity = min(rows_dev, 5 * rows_dev // (2 * experts))
    length = lengths[0]
    my_rows = me * rows_dev
    live_all = jnp.arange(seq_len, dtype=jnp.int32) < length
    live_col = lax.dynamic_slice_in_dim(live_all, my_rows, rows_dev, 0).astype(F32)[:, None]

    cols_dev = width // groups
    first_heads = [d * cols_dev // HEAD_DIM for d in range(groups)]
    span = max(-(-(d + 1) * cols_dev // HEAD_DIM) - first_heads[d] for d in range(groups))
    first_heads = [min(head, HEADS - span) for head in first_heads]
    window = span * HEAD_DIM
    window_starts = [head * HEAD_DIM for head in first_heads]
    offsets = [d * cols_dev - window_starts[d] for d in range(groups)]
    my_offset = jnp.asarray(offsets, jnp.int32)[me]

    tokens_all = gather_rows(tokens[0])
    gain_attn_col = gain_attn.astype(F32)[:, None]
    qkv_rows = [
        (weight.astype(F32) * gain_attn_col).astype(BF16) for weight in (w_query, w_key, w_value)
    ]
    qkv_chunks = jnp.stack(
        [
            jnp.concatenate([weight[:, at : at + window] for weight in qkv_rows], axis=1)
            for at in window_starts
        ]
    )
    qkv_cols = exchange(qkv_chunks).reshape(width, 3 * window)
    shared_cols_dev = shared_gate.shape[1] // groups
    gate_up_chunks = jnp.concatenate(
        [
            weight.reshape(-1, groups, shared_cols_dev).transpose(1, 0, 2)
            for weight in (shared_gate, shared_up)
        ],
        axis=2,
    )
    packed_rows = jnp.concatenate([w_out, w_router, gain_ffn[:, None]], axis=1)
    packed_all = gather_rows(packed_rows)
    out_full = packed_all[:, :width]
    router_full = packed_all[:, width : width + experts]
    gain_two = packed_all[:, width + experts].astype(F32)[None, :]
    cosine, sine = rope_tables(seq_len)

    inputs_all = tokens_all.astype(F32)
    unit = (inputs_all * inv_rms(inputs_all)).astype(BF16)
    qkv = contract(qkv_cols, unit, 0, 1)
    queries = (rotate_cols(qkv[:window], cosine, sine).astype(BF16).astype(F32) * 0.125).astype(
        BF16
    )
    keys = rotate_cols(qkv[window : 2 * window], cosine, sine).astype(BF16)
    values = qkv[2 * window :].astype(BF16)
    mixed_heads, log_norm = attn_forward(lengths, queries, keys, values)
    mixed_own = lax.dynamic_slice_in_dim(mixed_heads, my_offset, cols_dev, 0).astype(BF16)
    mixed_all = gather_rows(mixed_own)

    gate_up_cols = exchange(gate_up_chunks).reshape(width, 2 * shared_cols_dev)
    cotangent_all = gather_rows(cotangent[0])
    routes_all = lax.all_gather(routes[0], "fsdp", axis=0, tiled=True)

    hidden_all = inputs_all + matmul_tn(mixed_all, out_full)
    normed = (hidden_all * inv_rms(hidden_all) * gain_two).astype(BF16)
    router_probs = jax.nn.softmax(matmul(normed, router_full), axis=-1)

    shared_act = matmul(normed, gate_up_cols)
    shared_gate_act = shared_act[:, :shared_cols_dev]
    shared_up_act = shared_act[:, shared_cols_dev:]
    shared_inner = swiglu(shared_gate_act, shared_up_act)
    shared_result = matmul(shared_inner, shared_down)

    my_expert = me // 2
    routed = jnp.any(routes_all == my_expert, axis=1) & live_all
    routed = routed.reshape(groups, rows_dev)
    rank = jnp.cumsum(routed.astype(jnp.int32), axis=1) - 1
    pick = (
        (rank[:, None, :] == jnp.arange(capacity, dtype=jnp.int32)[None, :, None])
        & routed[:, None, :]
    ).astype(BF16)

    def pick_rows(full_rows):
        picked = jnp.einsum(
            "bct,btd->bcd",
            pick,
            full_rows.reshape(groups, rows_dev, -1),
            preferred_element_type=F32,
        )
        return picked.astype(BF16).reshape(groups * capacity, -1)

    def place_rows(picked_rows):
        placed = jnp.einsum(
            "bct,bcd->btd",
            pick,
            picked_rows.reshape(groups, capacity, -1),
            preferred_element_type=F32,
        )
        return placed.reshape(seq_len, -1)

    my_prob = lax.dynamic_slice_in_dim(router_probs, my_expert, 1, 1).reshape(groups, 1, rows_dev)
    row_prob = jnp.sum(jnp.where(pick > 0, my_prob, 0.0), axis=2).reshape(-1, 1)
    rows_in = pick_rows(normed)
    expert_gate_act = matmul(rows_in, expert_gate)
    expert_up_act = matmul(rows_in, expert_up)
    expert_inner = swiglu(expert_gate_act, expert_up_act)
    expert_half = matmul(expert_inner, expert_down).astype(BF16).astype(F32)
    branch_part = shared_result + place_rows((row_prob * expert_half).astype(BF16))

    grad_out_all = jnp.where(live_all[:, None], cotangent_all, jnp.zeros((), BF16))
    shared_gate_grad, shared_up_grad = swiglu_grad(
        matmul_nt(grad_out_all, shared_down).astype(BF16), shared_gate_act, shared_up_act
    )
    shared_act_grad = jnp.concatenate([shared_gate_grad, shared_up_grad], axis=1)
    grad_rows_out = pick_rows(grad_out_all)
    grad_rows_f32 = grad_rows_out.astype(F32)
    route_dots = jnp.sum(grad_rows_f32 * expert_half, axis=1, keepdims=True)
    grad_half = (row_prob * grad_rows_f32).astype(BF16)
    expert_gate_grad, expert_up_grad = swiglu_grad(
        matmul_nt(grad_half, expert_down).astype(BF16), expert_gate_act, expert_up_act
    )
    rows_grad = (
        matmul_nt(expert_gate_grad, expert_gate) + matmul_nt(expert_up_grad, expert_up)
    ).astype(BF16)
    dots_high = route_dots.astype(BF16)
    dots_low = (route_dots - dots_high.astype(F32)).astype(BF16)
    lane = jnp.arange(128, dtype=jnp.int32)[None, :]
    zero = jnp.zeros((), BF16)
    dots_cols = jnp.where(lane == me, dots_high, zero) + jnp.where(
        lane == me + groups, dots_low, zero
    )
    grad_part = place_rows(jnp.concatenate([rows_grad, dots_cols], axis=1))
    grad_part = grad_part + jnp.pad(
        matmul_nt(shared_act_grad, gate_up_cols), ((0, 0), (0, 128))
    )
    grad_own = scatter_sum(grad_part.astype(BF16)).astype(F32)
    branch_own = scatter_sum(branch_part.astype(BF16)).astype(F32)

    grad_expert_gate = matmul_tn(rows_in, expert_gate_grad).astype(BF16)
    grad_expert_up = matmul_tn(rows_in, expert_up_grad).astype(BF16)
    grad_expert_down = matmul_tn(expert_inner, grad_half).astype(BF16)
    sum_expert = lax.psum((grad_expert_gate, grad_expert_up, grad_expert_down), "rep")
    grad_shared_down = matmul_tn(shared_inner, grad_out_all).astype(BF16)
    grad_gate_up_cols = matmul_tn(normed, shared_act_grad).astype(BF16)

    hidden = lax.dynamic_slice_in_dim(hidden_all, my_rows, rows_dev, 0)
    normed_own = lax.dynamic_slice_in_dim(normed, my_rows, rows_dev, 0)
    probs_own = lax.dynamic_slice_in_dim(router_probs, my_rows, rows_dev, 0)
    mixed_rows = lax.dynamic_slice_in_dim(mixed_all, my_rows, rows_dev, 1)
    output = (live_col * (hidden + branch_own)).astype(BF16)
    dots_own = grad_own[:, width : width + groups] + grad_own[:, width + groups : width + 2 * groups]
    grad_rprobs = jnp.sum(dots_own.reshape(rows_dev, experts, 2), axis=2)
    grad_logits = (
        probs_own * (grad_rprobs - jnp.sum(probs_own * grad_rprobs, axis=1, keepdims=True))
    ).astype(BF16)
    grad_normed = grad_own[:, :width] + matmul_nt(grad_logits, router_full)
    scale_two = inv_rms(hidden)
    grad_gain_ffn = jnp.sum(grad_normed * hidden * scale_two, axis=0)
    grad_out = live_col * cotangent[0].astype(F32)
    grad_hidden = grad_out + rms_back(hidden, scale_two, grad_normed * gain_two)
    grad_hidden_b = grad_hidden.astype(BF16)
    grad_mixed = matmul_nt(out_full, grad_hidden_b).astype(BF16)
    mixed_chunks = jnp.stack([grad_mixed[at : at + window] for at in window_starts])
    grad_mixed_cols = exchange(mixed_chunks).transpose(1, 0, 2).reshape(window, seq_len)
    packed_grad = jnp.concatenate(
        [
            matmul(mixed_rows, grad_hidden_b),
            matmul_tn(normed_own, grad_logits),
            grad_gain_ffn[:, None],
        ],
        axis=1,
    )
    packed_own = scatter_sum(packed_grad.astype(BF16))
    gate_up_back = exchange(
        grad_gate_up_cols.reshape(groups, width // groups, 2 * shared_cols_dev)
    )
    gate_up_own = jnp.concatenate(
        [
            gate_up_back[:, :, :shared_cols_dev].transpose(1, 0, 2).reshape(width // groups, -1),
            gate_up_back[:, :, shared_cols_dev:].transpose(1, 0, 2).reshape(width // groups, -1),
        ],
        axis=1,
    )
    sum_dense = lax.psum((grad_shared_down, gate_up_own, packed_own), "rep")

    grad_q, grad_k, grad_v = attn_backward(
        lengths, queries, keys, values, mixed_heads, log_norm, grad_mixed_cols
    )
    channel = jnp.arange(window, dtype=jnp.int32)[:, None]
    owned = (channel >= my_offset) & (channel < my_offset + cols_dev)
    qkv_grad = jnp.concatenate(
        [
            jnp.where(owned, rotate_cols(grad_q * 0.125, cosine, -sine), 0.0),
            jnp.where(owned, rotate_cols(grad_k, cosine, -sine), 0.0),
            jnp.where(owned, grad_v, 0.0),
        ],
        axis=0,
    ).astype(BF16)
    grad_unit = scatter_sum(contract(qkv_grad, qkv_cols, 0, 1).astype(BF16)).astype(F32)
    qkv_weight_grad = contract(unit, qkv_grad, 0, 1).astype(BF16)
    qkv_back = exchange(qkv_weight_grad.reshape(groups, width // groups, 3 * window))
    qkv_own = jnp.concatenate(
        [
            qkv_back[d, :, part * window + offsets[d] : part * window + offsets[d] + cols_dev]
            for part in range(3)
            for d in range(groups)
        ],
        axis=1,
    )
    sum_qkv = lax.psum(qkv_own, "rep").astype(F32)
    inputs = tokens[0].astype(F32)
    input_grad = grad_hidden + rms_back(inputs, inv_rms(inputs), grad_unit)

    sum_gain_attn = sum(
        jnp.sum(sum_qkv[:, part * width : (part + 1) * width] * weight.astype(F32), axis=1)
        for part, weight in enumerate((w_query, w_key, w_value))
    )
    sum_weights = sum_qkv * gain_attn_col
    sum_down, sum_gate_up, sum_packed = [total.astype(F32) for total in sum_dense]
    sum_egate, sum_eup, sum_edown = [total.astype(F32) for total in sum_expert]
    half = sum_gate_up.shape[1] // 2
    return (
        output[None],
        input_grad[None],
        sum_gain_attn,
        sum_packed[:, width + experts],
        sum_weights[:, :width],
        sum_weights[:, width : 2 * width],
        sum_weights[:, 2 * width :],
        sum_packed[:, :width],
        sum_packed[:, width : width + experts],
        sum_gate_up[:, :half],
        sum_gate_up[:, half:],
        sum_down,
        sum_egate,
        sum_eup,
        sum_edown,
    )


def solution(mesh):
    in_specs = (
        P("rep", "fsdp", None),
        P("rep", "fsdp", None),
        P("rep"),
        P("rep", "fsdp", None),
        P("fsdp"),
        P("fsdp"),
        P("fsdp", None),
        P("fsdp", None),
        P("fsdp", None),
        P("fsdp", None),
        P("fsdp", None),
        P("fsdp", None),
        P("fsdp", None),
        P("fsdp", None),
        P(None, "fsdp"),
        P(None, "fsdp"),
        P("fsdp", None),
    )
    out_specs = (
        P("rep", "fsdp", None),
        P("rep", "fsdp", None),
        P("fsdp"),
        P("fsdp"),
        P("fsdp", None),
        P("fsdp", None),
        P("fsdp", None),
        P("fsdp", None),
        P("fsdp", None),
        P("fsdp", None),
        P("fsdp", None),
        P("fsdp", None),
        P(None, "fsdp"),
        P(None, "fsdp"),
        P("fsdp", None),
    )
    return jax.shard_map(
        on_device, mesh=mesh, in_specs=in_specs, out_specs=out_specs, check_vma=False
    )
```

time: 1430 us -> 643 us (0.45)
  waiting for transfers between devices: 1060 us -> 333 us
  blocking collectives: 99 us -> 44.3 us
  local copies, waits for them, and re-layouts: 77.9 us -> 45.6 us
  Pallas kernels: 0 us -> 29.8 us
  matrix products: 114 us -> 90.9 us
  other arithmetic: 30.1 us -> 51 us
    reduce_scatter x9 -> x3, waiting for transfers between devices: 497 us -> 74.9 us  [scatter_sum(): return lax.psum_scatter(values, 'fsdp', scatter_dimension=0, tiled=True)]
    all_to_all x4 -> x5, waiting for transfers between devices: 182 us -> 43.4 us  [exchange(): lax.all_to_all(chunks, 'fsdp', split_axis=0, concat_axis=0, tiled=True)]
    psum x1, waiting for transfers between devices: 229 us -> 146 us  [on_device(): sum_dense = lax.psum((grad_shared_down, gate_up_own, packed_own), 'rep')]
    all_gather x9 -> x4, waiting for transfers between devices: 123 us -> 66.5 us  [gather_rows(): return lax.all_gather(values, 'fsdp', axis=0, tiled=True)]
    unnamed x2 -> x0, blocking collectives: 32.3 us -> none
    pallas_call x0 -> x2, Pallas kernels: none -> 29.8 us  [the longest x1 16.5 us: attn_backward(): pl.pallas_call(functools.partial(attn_backward_kernel, heads=heads, blk=b...]
    unnamed x21 -> x10, waiting for transfers between devices: 26.4 us -> 1.48 us
    dot_general x39 -> x28, matrix products: 113 us -> 90.9 us  [the longest x24 79.4 us: contract(): lax.dot_general(first_op, second_op, (((first_dim,), (second_dim,)), ((),...]
  transfers between devices with their start and end apart: 24 -> 14, of which waited for: 21 -> 9; matrix products, arithmetic and copies ran while one was open for 10% -> 16% of each run, Pallas kernels for 0% -> 5%
where the time goes in v1:
time: 643 us; the launch traced here: 634 us
  waiting for transfers between devices  333 us (52%)
  matrix products  90.9 us (14%)
  other arithmetic  51 us (8%)
  local copies, waits for them, and re-layouts  45.6 us (7%)
  blocking collectives  44.3 us (7%)
  Pallas kernels  29.8 us (5%)
  starting transfers between devices  21.8 us (3%)
  between operations  18.4 us (3%)
    psum x1, waiting for transfers between devices, on_device(): sum_dense = lax.psum((grad_shared_down, gate_up_own, packed_own), 'rep')  146 us
    dot_general x24, matrix products, contract(): lax.dot_general(first_op, second_op, (((first_dim,), (second_dim,)), ((),...  79.4 us
    reduce_scatter x3, waiting for transfers between devices, scatter_sum(): return lax.psum_scatter(values, 'fsdp', scatter_dimension=0, tiled=True)  74.9 us
    all_gather x4, waiting for transfers between devices, gather_rows(): return lax.all_gather(values, 'fsdp', axis=0, tiled=True)  66.5 us
    all_gather x1, blocking collectives, on_device(): routes_all = lax.all_gather(routes[0], 'fsdp', axis=0, tiled=True)  44.3 us
    all_to_all x5, waiting for transfers between devices, exchange(): lax.all_to_all(chunks, 'fsdp', split_axis=0, concat_axis=0, tiled=True)  43.4 us
    unnamed x116, local copies, waits for them, and re-layouts  27.5 us
    all_to_all x5, starting transfers between devices, exchange(): lax.all_to_all(chunks, 'fsdp', split_axis=0, concat_axis=0, tiled=True)  21.4 us
  transfers between devices with their start and end apart: 14, of which 9 were waited for; matrix products, arithmetic and copies ran while one was open for 16% of the time, Pallas kernels for 5%

profile of v1, /device:TPU:0, one launch (start us, length us, event | category | flops | bytes accessed | tf_op | source)
XLA Modules:
  0.0 634.4 jit_solution(6165911519399815903)
XLA Ops:
  9.5 1.7 pad_maximum_fusion.13
  19.2 6.3 all-to-all-start
  28.8 1.8 fusion.61
  30.6 32.7 %all-gather.12.cloned.1.call-done = bf16[1,2048,768]{2,1,0:T(8,128)(2,1)} async-done(((bf16[1,256,768]{2,1,0:T(8,128)(2,1)}), bf16[1,2048,768]{2,1,0:T(8,128)(2,1)}) %all-gather.12.cloned.1.call-update) | async-done | bytes 3145744 | tf_op jit(solution)/shard_map/all_gather | solution.py:229
  63.3 2.6 fusion.1
  65.9 3.9 fusion.25
  70.5 13.2 %attn_forward.1 = (f32[128,2048]{1,0:T(8,128)S(1)}, f32[2,2048]{1,0:T(2,128)S(1)}) custom-call(s32[1]{0:T(128)} %copy.108.len_ref, bf16[128,2048]{1,0:T(8,128)(2,1)S(1)} %bitcast.239, bf16[128,2048]{1,0:T(8,128)(2,1)S(1)} %bitcast.237, bf16[128,2048]{1,0:T(8,128)(2,1)S(1)} %slice.542.v_ref), custom_call_target="tpu_custom_call" | custom-call | flops 4294967296 | bytes 4194304 | tf_op jit(solution)/shard_map/attn_forward/pallas_call | solution.py:191
  89.0 4.2 all-to-all-start.1
  93.3 44.3 %all-gather.1 = s32[1,2048,2]{1,2,0:T(2,128)S(1)} all-gather(s32[1,256,2]{1,2,0:T(2,128)S(1)} %copy-done.38), channel_id=3, replica_groups=mesh['rep'=4,'fsdp'=8] {'fsdp'}, dimensions={1}, use_global_device_ids=true | all-gather | bytes 18432 | tf_op jit(solution)/shard_map/all_gather | solution.py:320
  139.7 1.4 all-gather.14.cloned.1.call-done
  141.2 2.3 bitcast_select_fusion
  143.5 1.7 copy-done.5
  145.2 2.0 convolution_convert_fusion.4
  147.1 32.3 %all-gather.8.cloned.1.call-done = bf16[768,2048]{1,0:T(8,128)(2,1)} async-done(((bf16[96,2048]{1,0:T(8,128)(2,1)}), bf16[768,2048]{1,0:T(8,128)(2,1)}) %all-gather.8.cloned.1.call-update) | async-done | bytes 3145744 | tf_op jit(solution)/shard_map/all_gather | solution.py:229
  179.5 6.4 %multiply_reduce_fusion = (f32[2048]{0:T(1024)S(1)}, f32[2048,768]{1,0:T(8,128)S(1)}) fusion(bf16[768,2048]{1,0:T(8,128)(2,1)} %all-gather.8.cloned.1.call-done, bf16[768,773]{1,0:T(8,128)(2,1)} %all-gather.10.cloned.1.call-done, bf16[1,2048,768]{2,1,0:T(8,128)(2,1)} %all-gather.12.cloned.1.call-done), kind=kOutput, calls=%fused_computation.12 | convolution fusion | flops 2422208512 | bytes 13770752 | tf_op jit(solution)/shard_map/dot_general | solution.py:21
  186.5 2.0 copy-done.7
  188.5 1.7 copy-done.4
  190.1 1.9 fusion.97
  192.6 3.9 convolution_convert_fusion.5
  196.5 6.1 fusion.98
  204.1 2.2 convolution_convert_fusion
  206.8 2.2 fusion.99
  209.0 5.1 fusion.5
  214.1 3.7 fusion.10
  217.9 2.2 fusion.100
  220.1 2.3 add_convert_fusion
  222.5 1.5 pad_maximum_fusion
  224.1 4.5 copy.73
  228.6 3.1 fusion.17
  232.5 1.6 fusion.12
  235.4 5.6 fusion.15
  241.1 6.3 fusion
  247.4 2.6 fusion.20
  250.0 2.7 fusion.3
  254.2 37.3 %reduce-scatter.9.cloned.1.call-done = bf16[256,896]{1,0:T(8,128)(2,1)} async-done(((bf16[2048,896]{1,0:T(8,128)(2,1)}), bf16[256,896]{1,0:T(8,128)(2,1)}) %reduce-scatter.9.cloned.1.call-update) | async-done | bytes 458768 | tf_op jit(solution)/shard_map/reduce_scatter | solution.py:237
  292.8 2.5 multiply_reduce_fusion.1
  295.3 37.6 %reduce-scatter.7.cloned.1.call-done = bf16[256,768]{1,0:T(8,128)(2,1)} async-done(((bf16[2048,768]{1,0:T(8,128)(2,1)}), bf16[256,768]{1,0:T(8,128)(2,1)}) %reduce-scatter.7.cloned.1.call-update) | async-done | bytes 393232 | tf_op jit(solution)/shard_map/reduce_scatter | solution.py:237
  332.9 2.6 fusion.36
  341.2 3.5 all-to-all-start.2
  347.2 1.5 convolution_convert_fusion.9
  349.8 2.6 copy.79
  352.5 7.4 %all-to-all-done.2 = bf16[8,128,256]{2,1,0:T(8,128)(2,1)S(1)} async-done(((bf16[8,128,256]{2,1,0:T(8,128)(2,1)}), bf16[8,128,256]{2,1,0:T(8,128)(2,1)S(1)}, u32[]{:S(2)}, u32[]{:S(2)}) %all-to-all-start.2) | async-done | bytes 524320 | tf_op jit(solution)/shard_map/all_to_all | solution.py:233
  361.9 16.5 %attn_backward.1 = (f32[128,2048]{1,0:T(8,128)S(1)}, f32[128,2048]{1,0:T(8,128)S(1)}, f32[128,2048]{1,0:T(8,128)S(1)}) custom-call(s32[1]{0:T(128)} %copy.108.len_ref, bf16[128,2048]{1,0:T(8,128)(2,1)S(1)} %bitcast.240, bf16[128,2048]{1,0:T(8,128)(2,1)S(1)} %bitcast.238, bf16[128,2048]{1,0:T(8,128)(2,1)S(1)} %slice.542.v_ref, f32[128,2048]{1,0:T(8,128)S(1)} %copy-done.3, ...), custom_call_target="tpu_custom_call" | custom-call | flops 10737418240 | bytes 4194304 | tf_op jit(solution)/shard_map/attn_backward/pallas_call | solution.py:213
  380.3 3.5 convolution_convert_fusion.1
  385.0 5.1 convolution_convert_fusion.10
  390.1 3.8 all-to-all-start.4
  393.9 5.4 convolution_convert_fusion.6
  399.4 3.4 convolution_convert_fusion.8
  402.8 3.4 convolution_convert_fusion.7
  406.3 3.1 convolution_convert_fusion.11
  409.4 18.7 %all-to-all-done.4 = bf16[8,96,512]{2,1,0:T(8,128)(2,1)S(1)} async-done(((bf16[8,96,512]{2,1,0:T(8,128)(2,1)}), bf16[8,96,512]{2,1,0:T(8,128)(2,1)S(1)}, u32[]{:S(2)}, u32[]{:S(2)}) %all-to-all-start.4) | async-done | bytes 786464 | tf_op jit(solution)/shard_map/all_to_all | solution.py:233
  428.1 3.5 all-to-all-start.3
  431.7 3.7 convolution_convert_fusion.12
  436.5 17.3 %all-to-all-done.3 = bf16[8,96,384]{2,1,0:T(8,128)(2,1)S(1)} async-done(((bf16[8,96,384]{2,1,0:T(8,128)(2,1)}), bf16[8,96,384]{2,1,0:T(8,128)(2,1)S(1)}, u32[]{:S(2)}, u32[]{:S(2)}) %all-to-all-start.3) | async-done | bytes 589856 | tf_op jit(solution)/shard_map/all_to_all | solution.py:233
  455.0 1.7 copy.80
  459.0 2.1 fusion.33
  461.1 146.3 %all-reduce.4.cloned.1.call-done = (bf16[96,4096]{1,0:T(8,128)(2,1)}, bf16[96,2304]{1,0:T(8,128)(2,1)}, bf16[96,773]{0,1:T(8,128)(2,1)}, bf16[256,768]{1,0:T(8,1...) async-done(((bf16[96,4096]{1,0:T(8,128)(2,1)}, bf16[96,2304]{1,0:T(8,128)(2,1)}, bf16[96,773]{0,1:T(8,128)(2,1)}, ...) | async-done | bytes 6489040 | tf_op jit(solution)/shard_map/psum | solution.py:442
  608.7 1.7 slice.444
  610.4 1.8 convert_element_type.290
  613.4 1.9 copy.78
  616.5 1.9 convert_element_type.294
  620.8 2.1 convert_element_type.296
  622.9 2.1 convert_element_type.298
  625.0 1.9 convert_element_type.300
  (219 shorter events, 51.8 us)
Async XLA Ops:
  7.2 201.8 %copy-start = (bf16[768,1024]{1,0:T(8,128)(2,1)S(1)}, bf16[768,1024]{1,0:T(8,128)(2,1)}, u32[]{:S(2)}) copy-start(bf16[768,1024]{1,0:T(8,128)(2,1)} %param.33) | copy-start | bytes 4718596
  7.2 56.1 %all-gather.12.cloned.1.call-start = ((), (), s32[]{:S(2)}) async-start(), calls=%async_computation.14 | async-start | bytes 3538944 | tf_op jit(solution)/shard_map/all_gather | solution.py:229
  7.9 130.6 %all-gather.10.cloned.1.call-start = ((), (), s32[]{:S(2)}) async-start(), calls=%async_computation.10 | async-start | bytes 1548288 | tf_op jit(solution)/shard_map/all_gather | solution.py:229
  11.2 15.0 %copy-start.41 = (s32[8]{0:T(128)S(1)}, s32[8]{0:T(128)}, u32[]{:S(2)}) copy-start(s32[8]{0:T(128)} %constant.80.clone) | copy-start | bytes 100
  11.2 129.9 %all-gather.14.cloned.1.call-start = ((), (), s32[]{:S(2)}) async-start(), calls=%async_computation.15 | async-start | bytes 3538944 | tf_op jit(solution)/shard_map/all_gather | solution.py:229
  19.2 46.7 %all-to-all-start = ((bf16[8,96,384]{2,1,0:T(8,128)(2,1)}), bf16[8,96,384]{2,1,0:T(8,128)(2,1)S(1)}, u32[]{:S(2)}, u32[]{:S(2)}) async-start(bf16[8,96,384]{2,1,0:T(8,128)(2,1)} %fusion.69), calls=%async_computation | async-start | bytes 1179648 | tf_op jit(solution)/shard_map/all_to_all | solution.py:233
  25.5 153.9 %all-gather.8.cloned.1.call-start = ((), (), s32[]{:S(2)}) async-start(), calls=%async_computation.9 | async-start | bytes 3538944 | tf_op jit(solution)/shard_map/all_gather | solution.py:229
  65.9 3.9 copy-start.27
  84.6 1.0 copy-start.2
  86.7 6.6 %copy-start.38 = (s32[1,256,2]{1,2,0:T(2,128)S(1)}, s32[1,256,2]{1,2,0:T(2,128)}, u32[]{:S(2)}) copy-start(s32[1,256,2]{1,2,0:T(2,128)} %param.21) | copy-start | bytes 6148
  89.0 107.5 %all-to-all-start.1 = ((bf16[8,96,512]{2,1,0:T(8,128)(2,1)}), bf16[8,96,512]{2,1,0:T(8,128)(2,1)}, u32[]{:S(2)}, u32[]{:S(2)}) async-start(bf16[8,96,512]{2,1,0:T(8,128)(2,1)} %copy.71), calls=%async_computation.1 | async-start | bytes 1572864 | tf_op jit(solution)/shard_map/all_to_all | solution.py:233
  93.2 198.3 %reduce-scatter.9.cloned.1.call-start = ((), (), s32[]{:S(2)}) async-start(), calls=%async_computation.12 | async-start | bytes 4128768 | tf_op jit(solution)/shard_map/reduce_scatter | solution.py:237
  143.5 1.7 copy-start.5
  185.8 2.6 copy-start.7
  188.5 1.7 copy-start.4
  196.5 6.1 copy-start.8
  202.6 1.4 copy-start.39
  204.0 2.3 copy-start.17
  204.0 2.3 copy-start.15
  204.1 2.7 copy-start.40
  214.1 3.8 copy-start.50
  214.1 3.8 copy-start.47
  214.1 6.0 copy-start.45
  228.6 3.1 copy-start.6
  228.6 3.1 copy-start.36
  228.6 3.9 copy-start.49
  234.1 1.0 copy-start.42
  234.1 1.3 copy-start.44
  234.1 15.9 %copy-start.25 = (bf16[2048,256]{0,1:T(8,128)(2,1)}, bf16[2048,256]{0,1:T(8,128)(2,1)S(1)}, u32[]{:S(2)}) copy-start(bf16[2048,256]{0,1:T(8,128)(2,1)S(1)} %get-tuple-element.123) | copy-start | bytes 3145732
  247.4 85.5 %reduce-scatter.7.cloned.1.call-start = ((), (), s32[]{:S(2)}) async-start(), calls=%async_computation.11 | async-start | bytes 3538944 | tf_op jit(solution)/shard_map/reduce_scatter | solution.py:237
  252.9 80.1 %copy-start.20 = (bf16[1,256,768]{2,1,0:T(8,128)(2,1)S(1)}, bf16[1,256,768]{2,1,0:T(8,128)(2,1)}, u32[]{:S(2)}) copy-start(bf16[1,256,768]{2,1,0:T(8,128)(2,1)} %param.19) | copy-start | bytes 1179652
  332.9 2.7 copy-start.37
  335.6 13.2 %copy-start.9 = (f32[256,768]{1,0:T(8,128)}, f32[256,768]{1,0:T(8,128)S(1)}, u32[]{:S(2)}) copy-start(f32[256,768]{1,0:T(8,128)S(1)} %get-tuple-element.119) | copy-start | bytes 2359300
  341.2 18.8 %all-to-all-start.2 = ((bf16[8,128,256]{2,1,0:T(8,128)(2,1)}), bf16[8,128,256]{2,1,0:T(8,128)(2,1)S(1)}, u32[]{:S(2)}, u32[]{:S(2)}) async-start(bf16[8,128,256]{2,1,0:T(8,128)(2,1)} %fusion.70), calls=%async_computation.4 | async-start | bytes 1048576 | tf_op jit(solution)/shard_map/all_to_all | solution.py:233
  344.7 110.3 %reduce-scatter.13.cloned.1.call-start = ((), (), s32[]{:S(2)}) async-start(), calls=%async_computation.16 | async-start | bytes 1548288
  349.8 12.0 %copy-start.3 = (f32[128,2048]{1,0:T(8,128)S(1)}, f32[128,2048]{1,0:T(8,128)}, u32[]{:S(2)}) copy-start(f32[128,2048]{1,0:T(8,128)} %copy-done.2) | copy-start | bytes 3145732
  352.5 104.3 %reduce-scatter.11.cloned.1.call-start = ((), (), s32[]{:S(2)}) async-start(), calls=%async_computation.13 | async-start | bytes 3538944 | tf_op jit(solution)/shard_map/reduce_scatter | solution.py:237
  361.8 16.6 %copy-start.24 = (f32[32,2048]{1,0:T(8,128)S(1)}, f32[32,2048]{1,0:T(8,128)}, u32[]{:S(2)}) copy-start(f32[32,2048]{1,0:T(8,128)} %get-tuple-element.200) | copy-start | bytes 786436
  378.8 1.5 copy-start.28
  379.3 0.8 copy-start.32
  379.3 1.0 copy-start.34
  383.8 1.2 copy-start.43
  385.0 8.9 %copy-start.18 = (bf16[1280,768]{1,0:T(8,128)(2,1)S(1)}, bf16[1280,768]{1,0:T(8,128)(2,1)}, u32[]{:S(2)}) copy-start(bf16[1280,768]{1,0:T(8,128)(2,1)} %copy-done.17) | copy-start | bytes 5898244
  390.1 38.0 %all-to-all-start.4 = ((bf16[8,96,512]{2,1,0:T(8,128)(2,1)}), bf16[8,96,512]{2,1,0:T(8,128)(2,1)S(1)}, u32[]{:S(2)}, u32[]{:S(2)}) async-start(bf16[8,96,512]{2,1,0:T(8,128)(2,1)} %bitcast.76), calls=%async_computation.7 | async-start | bytes 1572864 | tf_op jit(solution)/shard_map/all_to_all | solution.py:233
  393.9 5.4 copy-start.16
  393.9 5.4 copy-start.48
  399.4 3.4 copy-start.46
  402.8 3.5 copy-start.12
  402.8 3.5 copy-start.33
  402.8 3.5 copy-start.35
  406.3 25.4 %copy-start.26 = (bf16[2048,256]{0,1:T(8,128)(2,1)S(1)}, bf16[2048,256]{0,1:T(8,128)(2,1)}, u32[]{:S(2)}) copy-start(bf16[2048,256]{0,1:T(8,128)(2,1)} %copy-done.25) | copy-start | bytes 3145732
  428.1 25.6 %all-to-all-start.3 = ((bf16[8,96,384]{2,1,0:T(8,128)(2,1)}), bf16[8,96,384]{2,1,0:T(8,128)(2,1)S(1)}, u32[]{:S(2)}, u32[]{:S(2)}) async-start(bf16[8,96,384]{2,1,0:T(8,128)(2,1)} %bitcast.50), calls=%async_computation.6 | async-start | bytes 1179648 | tf_op jit(solution)/shard_map/all_to_all | solution.py:233
  431.6 175.7 %all-reduce.4.cloned.1.call-start = ((), (), s32[]{:S(2)}) async-start(), calls=%async_computation.17 | async-start | bytes 13078528 | tf_op jit(solution)/shard_map/psum | solution.py:442
  456.7 1.0 copy-start.11
  456.7 2.2 copy-start.10
  607.4 5.9 copy-start.19
  610.4 8.0 %copy-start.13 = (bf16[96,4096]{1,0:T(8,128)(2,1)S(1)}, bf16[96,4096]{1,0:T(8,128)(2,1)}, u32[]{:S(2)}) copy-start(bf16[96,4096]{1,0:T(8,128)(2,1)} %get-tuple-element.107) | copy-start | bytes 2359300
  618.4 2.3 copy-start.29
  618.4 2.3 copy-start.30
  618.4 2.3 copy-start.31
  618.4 2.4 copy-start.23
  620.8 2.1 copy-start.22
  622.9 2.1 copy-start.21
  622.9 4.5 copy-start.1
  (1 other events, 0.8 us)
Sparse Core Ops, SparseCore 0:
  9.7 53.6 all-gather.11
  65.5 22.7 all-gather.9
  90.0 51.0 all-gather.13
  143.2 36.1 all-gather.7
  247.5 43.9 reduce-scatter.8
  294.2 38.6 reduce-scatter.6
  352.6 34.7 reduce-scatter.12
  390.4 57.6 reduce-scatter.10
  456.9 150.4 all-reduce.3

commit v2 on v1

--- a/solution.py
+++ b/solution.py
@@ -13,6 +13,7 @@
 EPSILON = 1e-06
 ROPE_BASE = 10000.0
 NEG_FILL = -1e30
+MARK = (8, 128)
 F32 = jnp.float32
 BF16 = jnp.bfloat16
 
@@ -123,8 +124,10 @@
 
 
 def attn_backward_kernel(
-    len_ref, q_ref, k_ref, v_ref, o_ref, l_ref, do_ref, dq_ref, dk_ref, dv_ref, *, heads, blk
+    len_ref, q_ref, k_ref, v_ref, o_ref, l_ref, do_ref, *refs, heads, blk
 ):
+    dq_ref, dk_ref, dv_ref, mark_ref = refs[-4:]
+    mark_ref[...] = jnp.zeros_like(mark_ref)
     row = pl.program_id(0)
     length = len_ref[0]
 
@@ -134,7 +137,8 @@
         dv_ref[...] = jnp.zeros_like(dv_ref)
 
     parts = [slice(head * HEAD_DIM, (head + 1) * HEAD_DIM) for head in range(heads)]
-    queries, grad_out = (q_ref[...], do_ref[...])
+    queries = q_ref[...]
+    grad_out = jnp.concatenate([do_ref[src] for src in range(do_ref.shape[0])], axis=1)
     deltas = [
         jnp.sum(grad_out[part].astype(F32) * o_ref[part, :], axis=0, keepdims=True)
         for part in parts
@@ -206,23 +210,329 @@
     )(length, queries, keys, values)
 
 
-def attn_backward(length, queries, keys, values, mixed, log_norm, grad_mixed):
+def attn_backward(length, queries, keys, values, mixed, log_norm, grad_mixed, earlier):
     rows, seq_len = queries.shape
     heads, blk = (rows // HEAD_DIM, min(512, seq_len))
     block, whole, stats = attn_specs(rows, seq_len, heads, blk)
+    rows_dev = grad_mixed.shape[2]
+    sources = pl.BlockSpec((blk // rows_dev, rows, rows_dev), lambda i, _: (i, 0, 0))
     return pl.pallas_call(
         functools.partial(attn_backward_kernel, heads=heads, blk=blk),
-        out_shape=(jax.ShapeDtypeStruct((rows, seq_len), F32),) * 3,
+        out_shape=(
+            *(jax.ShapeDtypeStruct((rows, seq_len), F32),) * 3,
+            jax.ShapeDtypeStruct(MARK, F32),
+        ),
         grid_spec=pltpu.PrefetchScalarGridSpec(
             num_scalar_prefetch=1,
             grid=(seq_len // blk,),
-            in_specs=[block, whole, whole, block, stats, block],
-            out_specs=(block, whole, whole),
+            in_specs=[block, whole, whole, block, stats, sources]
+            + [pl.BlockSpec(memory_space=pl.ANY)] * len(earlier),
+            out_specs=(block, whole, whole, pl.BlockSpec(MARK, lambda i, _: (0, 0))),
         ),
         compiler_params=pltpu.CompilerParams(vmem_limit_bytes=40 << 20),
         cost_estimate=attn_cost(rows, seq_len, heads, 5),
         name="attn_backward",
-    )(length, queries, keys, values, mixed, log_norm, grad_mixed)
+    )(length, queries, keys, values, mixed, log_norm, grad_mixed, *earlier)
+
+
+def branch_kernel(
+    info_ref,
+    mixed_ref,
+    tokens_ref,
+    cotangent_ref,
+    rank_ref,
+    out_w_ref,
+    gate_ref,
+    up_ref,
+    small_ref,
+    down_ref,
+    egate_ref,
+    eup_ref,
+    edown_ref,
+    branch_ref,
+    grad_ref,
+    normed_ref,
+    inner_ref,
+    act_grad_ref,
+    rows_ref,
+    einner_ref,
+    egate_grad_ref,
+    eup_grad_ref,
+    half_grad_ref,
+    *,
+    experts,
+    groups,
+    capacity,
+):
+    rows = tokens_ref.shape[0]
+    blocks, _, rows_dev = rank_ref.shape
+    length, me = (info_ref[0], info_ref[1])
+    first_pos = info_ref[2] + pl.program_id(0) * rows
+
+    hidden = tokens_ref[...].astype(F32) + matmul_tn(mixed_ref[...], out_w_ref[...])
+    small = small_ref[...].astype(F32).T
+    gain = small[experts : experts + 1]
+    normed = (hidden * inv_rms(hidden) * gain).astype(BF16)
+    normed_ref[...] = normed
+    logits = matmul_nt(small[:16].astype(BF16), normed)
+    expert_row = lax.broadcasted_iota(jnp.int32, logits.shape, 0)
+    logits = jnp.where(expert_row < experts, logits, NEG_FILL)
+    weights = jnp.exp(logits - jnp.max(logits, axis=0, keepdims=True))
+    probs = weights / jnp.sum(weights, axis=0, keepdims=True)
+    prob_row = jnp.sum(jnp.where(expert_row == me // 2, probs, 0.0), axis=0, keepdims=True)
+
+    position = first_pos + lax.broadcasted_iota(jnp.int32, (rows, 1), 0)
+    live = (position < length).astype(F32)
+    grad_out = (cotangent_ref[...].astype(F32) * live).astype(BF16)
+
+    gate_act, up_act = (matmul(normed, gate_ref[...]), matmul(normed, up_ref[...]))
+    inner = swiglu(gate_act, up_act)
+    inner_ref[...] = (inner.astype(F32) * live).astype(BF16)
+    branch = matmul(inner, down_ref[...])
+    gate_grad, up_grad = swiglu_grad(
+        matmul_nt(grad_out, down_ref[...]).astype(BF16), gate_act, up_act
+    )
+    act_grad = jnp.concatenate([gate_grad, up_grad], axis=1)
+    act_grad_ref[...] = act_grad
+    grad = matmul_nt(gate_grad, gate_ref[...]) + matmul_nt(up_grad, up_ref[...])
+
+    picks, picked, picked_grad, picked_prob = ([], [], [], [])
+    slot = lax.broadcasted_iota(jnp.int32, (capacity, rows_dev), 0)
+    for blk in range(blocks):
+        part = slice(blk * rows_dev, (blk + 1) * rows_dev)
+        hot = (slot == rank_ref[blk]).astype(F32)
+        picked_prob.append(jnp.sum(hot * prob_row[:, part], axis=1, keepdims=True))
+        pick = hot.astype(BF16)
+        picks.append(pick)
+        picked.append(matmul(pick, normed[part]).astype(BF16))
+        picked_grad.append(matmul(pick, grad_out[part]).astype(BF16))
+    rows_in = jnp.concatenate(picked, axis=0)
+    grad_rows = jnp.concatenate(picked_grad, axis=0).astype(F32)
+    row_prob = jnp.concatenate(picked_prob, axis=0)
+    rows_ref[...] = rows_in
+    egate_act = matmul(rows_in, egate_ref[...])
+    eup_act = matmul(rows_in, eup_ref[...])
+    einner = swiglu(egate_act, eup_act)
+    einner_ref[...] = einner
+    half = matmul(einner, edown_ref[...]).astype(BF16).astype(F32)
+    dots = jnp.sum(grad_rows * half, axis=1, keepdims=True)
+    half_grad = (row_prob * grad_rows).astype(BF16)
+    half_grad_ref[...] = half_grad
+    egate_grad, eup_grad = swiglu_grad(
+        matmul_nt(half_grad, edown_ref[...]).astype(BF16), egate_act, eup_act
+    )
+    egate_grad_ref[...] = egate_grad
+    eup_grad_ref[...] = eup_grad
+    rows_grad = (
+        matmul_nt(egate_grad, egate_ref[...]) + matmul_nt(eup_grad, eup_ref[...])
+    ).astype(BF16)
+    gated = (row_prob * half).astype(BF16)
+
+    dots_high = dots.astype(BF16).astype(F32)
+    lane = lax.broadcasted_iota(jnp.int32, (1, 128), 1)
+    dots_cols = jnp.where(lane == me, dots_high, 0.0) + jnp.where(
+        lane == me + groups, dots - dots_high, 0.0
+    )
+    dots_cols = dots_cols.astype(BF16)
+    width = normed.shape[1]
+    for blk in range(blocks):
+        part = slice(blk * rows_dev, (blk + 1) * rows_dev)
+        from_part = slice(blk * capacity, (blk + 1) * capacity)
+        pick = picks[blk]
+        branch_ref[part, :] = (branch[part] + matmul_tn(pick, gated[from_part])).astype(BF16)
+        grad_ref[part, :width] = (grad[part] + matmul_tn(pick, rows_grad[from_part])).astype(BF16)
+        grad_ref[part, width:] = matmul_tn(pick, dots_cols[from_part]).astype(BF16)
+
+
+def run_branches(
+    info, mixed, tokens, cotangent, rank, packed, down, egate, eup, edown, experts, capacity
+):
+    seq_len, width = tokens.shape
+    groups, _, rows_dev = rank.shape
+    blocks = 2 if groups % 2 == 0 else 1
+    rows, picked = (blocks * rows_dev, blocks * capacity)
+    hidden, ehidden = (down.shape[0], egate.shape[1])
+    act_cols = 2 * hidden
+
+    def step_rows(count, cols):
+        return pl.BlockSpec((count, cols), lambda i, _: (i, 0))
+
+    def whole(shape):
+        return pl.BlockSpec(shape, lambda i, _: (0, 0), pipeline_mode=pl.Buffered(1))
+
+    def packed_part(cols, at):
+        return pl.BlockSpec(
+            (width, cols), lambda i, _: (0, at // cols), pipeline_mode=pl.Buffered(1)
+        )
+
+    def result(count, cols):
+        return jax.ShapeDtypeStruct((count, cols), BF16)
+
+    all_picked = groups * capacity
+    flops = 2 * seq_len * width * (width + 6 * act_cols // 2) + 2 * all_picked * width * (
+        6 * ehidden + 4 * rows_dev
+    )
+    return pl.pallas_call(
+        functools.partial(branch_kernel, experts=experts, groups=groups, capacity=capacity),
+        out_shape=(
+            result(seq_len, width),
+            result(seq_len, width + 128),
+            result(seq_len, width),
+            result(seq_len, hidden),
+            result(seq_len, act_cols),
+            result(all_picked, width),
+            result(all_picked, ehidden),
+            result(all_picked, ehidden),
+            result(all_picked, ehidden),
+            result(all_picked, width),
+        ),
+        grid_spec=pltpu.PrefetchScalarGridSpec(
+            num_scalar_prefetch=1,
+            grid=(groups // blocks,),
+            in_specs=[
+                pl.BlockSpec((width, rows), lambda i, _: (0, i)),
+                step_rows(rows, width),
+                step_rows(rows, width),
+                pl.BlockSpec((blocks, 1, rows_dev), lambda i, _: (i, 0, 0)),
+                packed_part(width, 0),
+                packed_part(hidden, width),
+                packed_part(hidden, width + hidden),
+                packed_part(128, width + act_cols),
+                whole(down.shape),
+                whole(egate.shape),
+                whole(eup.shape),
+                whole(edown.shape),
+            ],
+            out_specs=(
+                step_rows(rows, width),
+                step_rows(rows, width + 128),
+                step_rows(rows, width),
+                step_rows(rows, hidden),
+                step_rows(rows, act_cols),
+                step_rows(picked, width),
+                step_rows(picked, ehidden),
+                step_rows(picked, ehidden),
+                step_rows(picked, ehidden),
+                step_rows(picked, width),
+            ),
+        ),
+        compiler_params=pltpu.CompilerParams(vmem_limit_bytes=56 << 20),
+        cost_estimate=pl.CostEstimate(
+            flops=flops, bytes_accessed=40 << 20, transcendentals=2 * all_picked * ehidden
+        ),
+        name="branches",
+    )(info, mixed, tokens, cotangent, rank, packed, packed, packed, packed, down, egate, eup, edown)
+
+
+def own_rows_kernel(
+    info_ref,
+    grad_ref,
+    mixed_ref,
+    tokens_ref,
+    cotangent_ref,
+    out_w_ref,
+    small_ref,
+    *refs,
+    experts,
+    groups,
+    window_starts,
+):
+    hidden_ref, grad_hidden_ref, grad_mixed_ref, normed_ref, logits_ref, back_ref, mark_ref = refs[
+        -8:-1
+    ]
+    mark_ref[...] = jnp.zeros_like(mark_ref)
+    rows, width = tokens_ref.shape
+    length, me = (info_ref[0], info_ref[1])
+    small = small_ref[...].astype(F32)
+    gain = small.T[experts : experts + 1]
+    hidden = tokens_ref[...].astype(F32) + matmul_tn(mixed_ref[...], out_w_ref[...])
+    scale = inv_rms(hidden)
+    unit = hidden * scale
+    normed = (unit * gain).astype(BF16)
+    lane = lax.broadcasted_iota(jnp.int32, (rows, 128), 1)
+    is_expert = lane < experts
+    logits = jnp.where(is_expert, matmul(normed, small.astype(BF16)), NEG_FILL)
+    weights = jnp.exp(logits - jnp.max(logits, axis=1, keepdims=True))
+    probs = weights / jnp.sum(weights, axis=1, keepdims=True)
+    dots = grad_ref[:, width:].astype(F32)
+    grad_probs = jnp.zeros((rows, 128), F32)
+    for expert in range(experts):
+        source = lane % groups // 2
+        part = jnp.where((lane < 2 * groups) & (source == expert), dots, 0.0)
+        grad_probs = jnp.where(
+            lane == expert, jnp.sum(part, axis=1, keepdims=True), grad_probs
+        )
+    mean = jnp.sum(probs * grad_probs, axis=1, keepdims=True)
+    grad_logits = jnp.where(is_expert, probs * (grad_probs - mean), 0.0).astype(BF16)
+    router = jnp.where(
+        lax.broadcasted_iota(jnp.int32, small.shape, 1) < experts, small, 0.0
+    ).astype(BF16)
+    grad_normed = grad_ref[:, :width].astype(F32) + matmul_nt(grad_logits, router)
+    position = me * rows + lax.broadcasted_iota(jnp.int32, (rows, 1), 0)
+    live = (position < length).astype(F32)
+    grad_hidden = cotangent_ref[...].astype(F32) * live + rms_back(
+        hidden, scale, grad_normed * gain
+    )
+    hidden_ref[...] = hidden * live
+    grad_hidden_ref[...] = grad_hidden
+    grad_mixed = matmul_nt(out_w_ref[...], grad_hidden.astype(BF16)).astype(BF16)
+    for dest, at in enumerate(window_starts):
+        grad_mixed_ref[dest] = grad_mixed[at : at + grad_mixed_ref.shape[1]]
+    normed_ref[...] = normed
+    logits_ref[...] = jnp.where(lane == experts, jnp.ones((), BF16), grad_logits)
+    back_ref[...] = (grad_normed * unit).astype(BF16)
+
+
+def own_rows(
+    info, grad_own, mixed, tokens, cotangent, packed, branch, earlier, experts, groups,
+    window, window_starts,
+):
+    rows, width = tokens.shape
+    small_at = packed.shape[1] // 128 - 1
+
+    def whole(shape):
+        return pl.BlockSpec(shape, lambda i, _: (0,) * len(shape))
+
+    anywhere = pl.BlockSpec(memory_space=pl.ANY)
+    shapes = (
+        ((rows, width), F32),
+        ((rows, width), F32),
+        ((groups, window, rows), BF16),
+        ((rows, width), BF16),
+        ((rows, 128), BF16),
+        ((rows, width), BF16),
+        (MARK, F32),
+    )
+    return pl.pallas_call(
+        functools.partial(
+            own_rows_kernel, experts=experts, groups=groups, window_starts=tuple(window_starts)
+        ),
+        out_shape=(
+            *(jax.ShapeDtypeStruct(shape, dtype) for shape, dtype in shapes),
+            jax.ShapeDtypeStruct(branch.shape, branch.dtype),
+        ),
+        grid_spec=pltpu.PrefetchScalarGridSpec(
+            num_scalar_prefetch=1,
+            grid=(1,),
+            in_specs=[
+                whole(grad_own.shape),
+                pl.BlockSpec((width, rows), lambda i, info: (0, info[1])),
+                whole(tokens.shape),
+                whole(cotangent.shape),
+                whole((width, width)),
+                pl.BlockSpec((width, 128), lambda i, _: (0, small_at)),
+                anywhere,
+            ]
+            + [anywhere] * len(earlier),
+            out_specs=(*(whole(shape) for shape, _ in shapes), anywhere),
+        ),
+        input_output_aliases={7: len(shapes)},
+        compiler_params=pltpu.CompilerParams(vmem_limit_bytes=40 << 20),
+        cost_estimate=pl.CostEstimate(
+            flops=6 * rows * width * width, bytes_accessed=6 << 20, transcendentals=rows * 128
+        ),
+        name="own_rows",
+    )(info, grad_own, mixed, tokens, cotangent, packed, packed, branch, *earlier)
 
 
 def gather_rows(values):
@@ -235,6 +545,49 @@
 
 def scatter_sum(values):
     return lax.psum_scatter(values, "fsdp", scatter_dimension=0, tiled=True)
+
+
+def after(values, mark):
+    mark = mark[(slice(0, 1),) * mark.ndim].reshape(()).astype(F32)
+    return jnp.where(mark < jnp.inf, values, jnp.zeros((), values.dtype))
+
+
+def swap_rep(values, bit):
+    count = lax.axis_size("rep")
+    return lax.ppermute(values, "rep", [(i, i ^ (1 << bit)) for i in range(count)])
+
+
+def rep_bits():
+    count = lax.axis_size("rep")
+    bits = count.bit_length() - 1
+    assert count == 1 << bits
+    return range(bits)
+
+
+def rep_scatter_sum(values, axis, bits=None, marks=()):
+    index = lax.axis_index("rep")
+    for step, bit in enumerate(rep_bits() if bits is None else bits):
+        half = values.shape[axis] // 2
+        mine = (index >> bit) & 1
+        keep = lax.dynamic_slice_in_dim(values, mine * half, half, axis)
+        send = lax.dynamic_slice_in_dim(values, (1 - mine) * half, half, axis)
+        if step < len(marks):
+            keep = after(keep, marks[step])
+        values = (keep.astype(F32) + swap_rep(send, bit).astype(F32)).astype(values.dtype)
+    return values
+
+
+def rep_join(values, axis, bits=None):
+    index = lax.axis_index("rep")
+    for bit in reversed(rep_bits() if bits is None else bits):
+        other = swap_rep(values, bit)
+        mine = (index >> bit) & 1
+        values = jnp.where(
+            mine == 0,
+            jnp.concatenate([values, other], axis=axis),
+            jnp.concatenate([other, values], axis=axis),
+        )
+    return values
 
 
 def on_device(
@@ -258,6 +611,7 @@
 ):
     rows_dev, width = tokens.shape[1:]
     groups = lax.axis_size("fsdp")
+    reps = lax.axis_size("rep")
     me = lax.axis_index("fsdp")
     seq_len = groups * rows_dev
     experts = w_router.shape[1]
@@ -277,9 +631,16 @@
     my_offset = jnp.asarray(offsets, jnp.int32)[me]
 
     tokens_all = gather_rows(tokens[0])
-    gain_attn_col = gain_attn.astype(F32)[:, None]
+    rep_rows = cols_dev // reps
+    rep_at = lax.axis_index("rep") * rep_rows
+
+    def rep_part(weight):
+        return lax.dynamic_slice_in_dim(weight, rep_at, rep_rows, 0)
+
+    gain_part = rep_part(gain_attn).astype(F32)[:, None]
     qkv_rows = [
-        (weight.astype(F32) * gain_attn_col).astype(BF16) for weight in (w_query, w_key, w_value)
+        (rep_part(weight).astype(F32) * gain_part).astype(BF16)
+        for weight in (w_query, w_key, w_value)
     ]
     qkv_chunks = jnp.stack(
         [
@@ -287,21 +648,64 @@
             for at in window_starts
         ]
     )
-    qkv_cols = exchange(qkv_chunks).reshape(width, 3 * window)
+    qkv_part = exchange(qkv_chunks)
+    qkv_cols = lax.all_gather(qkv_part, "rep", axis=0)
+    qkv_cols = qkv_cols.transpose(1, 0, 2, 3).reshape(width, 3 * window)
+    cosine, sine = rope_tables(seq_len)
+
+    cotangent_all = gather_rows(after(cotangent[0], qkv_cols))
     shared_cols_dev = shared_gate.shape[1] // groups
-    gate_up_chunks = jnp.concatenate(
+    gate_chunks, up_chunks = [
+        rep_part(weight).reshape(rep_rows, groups, shared_cols_dev).transpose(1, 0, 2)
+        for weight in (shared_gate, shared_up)
+    ]
+    route_cols = -(-2 * rows_dev // rep_rows)
+    route_chunk = jnp.pad(
+        routes[0].astype(BF16).reshape(-1), (0, route_cols * rep_rows - 2 * rows_dev)
+    ).reshape(rep_rows, route_cols)
+    small_cols = experts + 1 + route_cols
+    small = jnp.concatenate(
         [
-            weight.reshape(-1, groups, shared_cols_dev).transpose(1, 0, 2)
-            for weight in (shared_gate, shared_up)
+            rep_part(w_router),
+            rep_part(gain_ffn)[:, None],
+            route_chunk,
+            jnp.zeros((rep_rows, -small_cols % 128), BF16),
         ],
-        axis=2,
-    )
-    packed_rows = jnp.concatenate([w_out, w_router, gain_ffn[:, None]], axis=1)
-    packed_all = gather_rows(packed_rows)
-    out_full = packed_all[:, :width]
-    router_full = packed_all[:, width : width + experts]
-    gain_two = packed_all[:, width + experts].astype(F32)[None, :]
-    cosine, sine = rope_tables(seq_len)
+        axis=1,
+    )
+    packed_part = exchange(
+        after(
+            jnp.concatenate(
+                [
+                    jnp.broadcast_to(rep_part(w_out), (groups, rep_rows, width)),
+                    gate_chunks,
+                    up_chunks,
+                    jnp.broadcast_to(small, (groups, *small.shape)),
+                ],
+                axis=2,
+            ),
+            qkv_cols,
+        )
+    )
+    small_at = width + 2 * shared_cols_dev
+    routes_all = (
+        packed_part[:, :, small_at + experts + 1 : small_at + small_cols]
+        .reshape(groups, rep_rows * route_cols)[:, : 2 * rows_dev]
+        .reshape(groups, rows_dev, 2)
+        .astype(jnp.int32)
+    )
+    packed_all = lax.psum(
+        lax.dynamic_update_slice_in_dim(
+            jnp.zeros((groups, cols_dev, small_at + 128), BF16),
+            packed_part[:, :, : small_at + 128],
+            rep_at,
+            1,
+        ),
+        "rep",
+    ).reshape(width, -1)
+    routed = jnp.any(routes_all == me // 2, axis=2) & live_all.reshape(groups, rows_dev)
+    rank = jnp.cumsum(routed.astype(jnp.int32), axis=1) - 1
+    rank = jnp.where(routed, rank, -1)[:, None, :]
 
     inputs_all = tokens_all.astype(F32)
     unit = (inputs_all * inv_rms(inputs_all)).astype(BF16)
@@ -313,137 +717,112 @@
     values = qkv[2 * window :].astype(BF16)
     mixed_heads, log_norm = attn_forward(lengths, queries, keys, values)
     mixed_own = lax.dynamic_slice_in_dim(mixed_heads, my_offset, cols_dev, 0).astype(BF16)
+    mixed_own = after(mixed_own, cotangent_all)
     mixed_all = gather_rows(mixed_own)
 
-    gate_up_cols = exchange(gate_up_chunks).reshape(width, 2 * shared_cols_dev)
-    cotangent_all = gather_rows(cotangent[0])
-    routes_all = lax.all_gather(routes[0], "fsdp", axis=0, tiled=True)
-
-    hidden_all = inputs_all + matmul_tn(mixed_all, out_full)
-    normed = (hidden_all * inv_rms(hidden_all) * gain_two).astype(BF16)
-    router_probs = jax.nn.softmax(matmul(normed, router_full), axis=-1)
-
-    shared_act = matmul(normed, gate_up_cols)
-    shared_gate_act = shared_act[:, :shared_cols_dev]
-    shared_up_act = shared_act[:, shared_cols_dev:]
-    shared_inner = swiglu(shared_gate_act, shared_up_act)
-    shared_result = matmul(shared_inner, shared_down)
-
-    my_expert = me // 2
-    routed = jnp.any(routes_all == my_expert, axis=1) & live_all
-    routed = routed.reshape(groups, rows_dev)
-    rank = jnp.cumsum(routed.astype(jnp.int32), axis=1) - 1
-    pick = (
-        (rank[:, None, :] == jnp.arange(capacity, dtype=jnp.int32)[None, :, None])
-        & routed[:, None, :]
-    ).astype(BF16)
-
-    def pick_rows(full_rows):
-        picked = jnp.einsum(
-            "bct,btd->bcd",
-            pick,
-            full_rows.reshape(groups, rows_dev, -1),
-            preferred_element_type=F32,
+    info = jnp.stack([length, me, jnp.zeros((), jnp.int32)])
+    (
+        branch_part,
+        grad_part,
+        normed,
+        shared_inner,
+        shared_act_grad,
+        rows_in,
+        expert_inner,
+        expert_gate_grad,
+        expert_up_grad,
+        grad_half,
+    ) = run_branches(
+        info,
+        mixed_all,
+        tokens_all,
+        cotangent_all,
+        rank,
+        packed_all,
+        shared_down,
+        expert_gate,
+        expert_up,
+        expert_down,
+        experts,
+        capacity,
+    )
+    grad_own = scatter_sum(grad_part)
+
+    expert_grads = jnp.concatenate(
+        [
+            matmul_tn(rows_in, expert_gate_grad).astype(BF16),
+            matmul_tn(rows_in, expert_up_grad).astype(BF16),
+            matmul_tn(grad_half, expert_inner).astype(BF16),
+        ],
+        axis=0,
+    )
+    grad_down = matmul_tn(shared_inner, cotangent_all).astype(BF16)
+    grad_gate_up = matmul_tn(normed, shared_act_grad).astype(BF16)
+
+    hidden, grad_hidden, grad_mixed, normed_own, logits_own, back_own, mark_own, branch_part = (
+        own_rows(
+            info,
+            grad_own,
+            mixed_all,
+            tokens[0],
+            cotangent[0],
+            packed_all,
+            branch_part,
+            (expert_grads, grad_down, grad_gate_up),
+            experts,
+            groups,
+            window,
+            window_starts,
         )
-        return picked.astype(BF16).reshape(groups * capacity, -1)
-
-    def place_rows(picked_rows):
-        placed = jnp.einsum(
-            "bct,bcd->btd",
-            pick,
-            picked_rows.reshape(groups, capacity, -1),
-            preferred_element_type=F32,
-        )
-        return placed.reshape(seq_len, -1)
-
-    my_prob = lax.dynamic_slice_in_dim(router_probs, my_expert, 1, 1).reshape(groups, 1, rows_dev)
-    row_prob = jnp.sum(jnp.where(pick > 0, my_prob, 0.0), axis=2).reshape(-1, 1)
-    rows_in = pick_rows(normed)
-    expert_gate_act = matmul(rows_in, expert_gate)
-    expert_up_act = matmul(rows_in, expert_up)
-    expert_inner = swiglu(expert_gate_act, expert_up_act)
-    expert_half = matmul(expert_inner, expert_down).astype(BF16).astype(F32)
-    branch_part = shared_result + place_rows((row_prob * expert_half).astype(BF16))
-
-    grad_out_all = jnp.where(live_all[:, None], cotangent_all, jnp.zeros((), BF16))
-    shared_gate_grad, shared_up_grad = swiglu_grad(
-        matmul_nt(grad_out_all, shared_down).astype(BF16), shared_gate_act, shared_up_act
-    )
-    shared_act_grad = jnp.concatenate([shared_gate_grad, shared_up_grad], axis=1)
-    grad_rows_out = pick_rows(grad_out_all)
-    grad_rows_f32 = grad_rows_out.astype(F32)
-    route_dots = jnp.sum(grad_rows_f32 * expert_half, axis=1, keepdims=True)
-    grad_half = (row_prob * grad_rows_f32).astype(BF16)
-    expert_gate_grad, expert_up_grad = swiglu_grad(
-        matmul_nt(grad_half, expert_down).astype(BF16), expert_gate_act, expert_up_act
-    )
-    rows_grad = (
-        matmul_nt(expert_gate_grad, expert_gate) + matmul_nt(expert_up_grad, expert_up)
-    ).astype(BF16)
-    dots_high = route_dots.astype(BF16)
-    dots_low = (route_dots - dots_high.astype(F32)).astype(BF16)
-    lane = jnp.arange(128, dtype=jnp.int32)[None, :]
-    zero = jnp.zeros((), BF16)
-    dots_cols = jnp.where(lane == me, dots_high, zero) + jnp.where(
-        lane == me + groups, dots_low, zero
-    )
-    grad_part = place_rows(jnp.concatenate([rows_grad, dots_cols], axis=1))
-    grad_part = grad_part + jnp.pad(
-        matmul_nt(shared_act_grad, gate_up_cols), ((0, 0), (0, 128))
-    )
-    grad_own = scatter_sum(grad_part.astype(BF16)).astype(F32)
-    branch_own = scatter_sum(branch_part.astype(BF16)).astype(F32)
-
-    grad_expert_gate = matmul_tn(rows_in, expert_gate_grad).astype(BF16)
-    grad_expert_up = matmul_tn(rows_in, expert_up_grad).astype(BF16)
-    grad_expert_down = matmul_tn(expert_inner, grad_half).astype(BF16)
-    sum_expert = lax.psum((grad_expert_gate, grad_expert_up, grad_expert_down), "rep")
-    grad_shared_down = matmul_tn(shared_inner, grad_out_all).astype(BF16)
-    grad_gate_up_cols = matmul_tn(normed, shared_act_grad).astype(BF16)
-
-    hidden = lax.dynamic_slice_in_dim(hidden_all, my_rows, rows_dev, 0)
-    normed_own = lax.dynamic_slice_in_dim(normed, my_rows, rows_dev, 0)
-    probs_own = lax.dynamic_slice_in_dim(router_probs, my_rows, rows_dev, 0)
-    mixed_rows = lax.dynamic_slice_in_dim(mixed_all, my_rows, rows_dev, 1)
-    output = (live_col * (hidden + branch_own)).astype(BF16)
-    dots_own = grad_own[:, width : width + groups] + grad_own[:, width + groups : width + 2 * groups]
-    grad_rprobs = jnp.sum(dots_own.reshape(rows_dev, experts, 2), axis=2)
-    grad_logits = (
-        probs_own * (grad_rprobs - jnp.sum(probs_own * grad_rprobs, axis=1, keepdims=True))
-    ).astype(BF16)
-    grad_normed = grad_own[:, :width] + matmul_nt(grad_logits, router_full)
-    scale_two = inv_rms(hidden)
-    grad_gain_ffn = jnp.sum(grad_normed * hidden * scale_two, axis=0)
-    grad_out = live_col * cotangent[0].astype(F32)
-    grad_hidden = grad_out + rms_back(hidden, scale_two, grad_normed * gain_two)
-    grad_hidden_b = grad_hidden.astype(BF16)
-    grad_mixed = matmul_nt(out_full, grad_hidden_b).astype(BF16)
-    mixed_chunks = jnp.stack([grad_mixed[at : at + window] for at in window_starts])
-    grad_mixed_cols = exchange(mixed_chunks).transpose(1, 0, 2).reshape(window, seq_len)
+    )
+    grad_mixed_cols = exchange(grad_mixed)
+    branch_own = scatter_sum(branch_part).astype(F32)
+    orders = (list(rep_bits()), list(rep_bits())[::-1])
+    half_rows = expert_grads.shape[0] // 2
+    expert_parts = [
+        rep_scatter_sum(expert_grads[at : at + half_rows], 0, order, (mark_own,))
+        for at, order in zip((0, half_rows), orders)
+    ]
     packed_grad = jnp.concatenate(
         [
-            matmul(mixed_rows, grad_hidden_b),
-            matmul_tn(normed_own, grad_logits),
-            grad_gain_ffn[:, None],
+            matmul(
+                lax.dynamic_slice_in_dim(mixed_all, my_rows, rows_dev, 1),
+                grad_hidden.astype(BF16),
+            ),
+            matmul_tn(normed_own, logits_own[:, :experts]),
+            matmul_tn(back_own, logits_own[:, experts : experts + 1]),
         ],
         axis=1,
-    )
-    packed_own = scatter_sum(packed_grad.astype(BF16))
-    gate_up_back = exchange(
-        grad_gate_up_cols.reshape(groups, width // groups, 2 * shared_cols_dev)
-    )
-    gate_up_own = jnp.concatenate(
+    ).astype(BF16)
+
+    grad_q, grad_k, grad_v, mark_attn = attn_backward(
+        lengths,
+        queries,
+        keys,
+        values,
+        mixed_heads,
+        log_norm,
+        grad_mixed_cols,
+        tuple(expert_parts),
+    )
+    grad_down = rep_scatter_sum(grad_down, 0, orders[1], (mark_attn,))
+    grad_gate_up = rep_scatter_sum(
+        grad_gate_up.reshape(groups, cols_dev, -1), 1, orders[1], (mark_attn,)
+    )
+    gate_up_back = exchange(grad_gate_up)
+    gate_up_part = jnp.concatenate(
         [
-            gate_up_back[:, :, :shared_cols_dev].transpose(1, 0, 2).reshape(width // groups, -1),
-            gate_up_back[:, :, shared_cols_dev:].transpose(1, 0, 2).reshape(width // groups, -1),
+            gate_up_back[:, :, at : at + shared_cols_dev]
+            .transpose(1, 0, 2)
+            .reshape(rep_rows, -1)
+            for at in (0, shared_cols_dev)
         ],
         axis=1,
     )
-    sum_dense = lax.psum((grad_shared_down, gate_up_own, packed_own), "rep")
-
-    grad_q, grad_k, grad_v = attn_backward(
-        lengths, queries, keys, values, mixed_heads, log_norm, grad_mixed_cols
-    )
+    packed_part = rep_scatter_sum(
+        packed_grad.reshape(groups, cols_dev, -1), 1, orders[0], (mark_attn,)
+    )
+    packed_part = jnp.sum(exchange(packed_part).astype(F32), axis=0).astype(BF16)
     channel = jnp.arange(window, dtype=jnp.int32)[:, None]
     owned = (channel >= my_offset) & (channel < my_offset + cols_dev)
     qkv_grad = jnp.concatenate(
@@ -455,9 +834,24 @@
         axis=0,
     ).astype(BF16)
     grad_unit = scatter_sum(contract(qkv_grad, qkv_cols, 0, 1).astype(BF16)).astype(F32)
+    expert_sum = jnp.concatenate(
+        [rep_join(part, 0, order) for part, order in zip(expert_parts, orders)], axis=0
+    )
+    expert_sum = expert_sum.astype(F32)
+    sum_egate, sum_eup, sum_edown = (
+        expert_sum[:width],
+        expert_sum[width : 2 * width],
+        expert_sum[2 * width :].T,
+    )
+    sum_down = rep_join(grad_down, 0, orders[1]).astype(F32)
+    inputs = tokens[0].astype(F32)
+    output = (hidden + live_col * branch_own).astype(BF16)
+    input_grad = grad_hidden + rms_back(inputs, inv_rms(inputs), grad_unit)
+
     qkv_weight_grad = contract(unit, qkv_grad, 0, 1).astype(BF16)
-    qkv_back = exchange(qkv_weight_grad.reshape(groups, width // groups, 3 * window))
-    qkv_own = jnp.concatenate(
+    qkv_part = rep_scatter_sum(qkv_weight_grad.reshape(groups, cols_dev, 3 * window), 1)
+    qkv_back = exchange(qkv_part)
+    qkv_part = jnp.concatenate(
         [
             qkv_back[d, :, part * window + offsets[d] : part * window + offsets[d] + cols_dev]
             for part in range(3)
@@ -465,17 +859,15 @@
         ],
         axis=1,
     )
-    sum_qkv = lax.psum(qkv_own, "rep").astype(F32)
-    inputs = tokens[0].astype(F32)
-    input_grad = grad_hidden + rms_back(inputs, inv_rms(inputs), grad_unit)
+    sum_qkv = rep_join(qkv_part, 0).astype(F32)
+    sum_gate_up = rep_join(gate_up_part, 0, orders[1]).astype(F32)
+    sum_packed = rep_join(packed_part, 0).astype(F32)
 
     sum_gain_attn = sum(
         jnp.sum(sum_qkv[:, part * width : (part + 1) * width] * weight.astype(F32), axis=1)
         for part, weight in enumerate((w_query, w_key, w_value))
     )
-    sum_weights = sum_qkv * gain_attn_col
-    sum_down, sum_gate_up, sum_packed = [total.astype(F32) for total in sum_dense]
-    sum_egate, sum_eup, sum_edown = [total.astype(F32) for total in sum_expert]
+    sum_weights = sum_qkv * gain_attn.astype(F32)[:, None]
     half = sum_gate_up.shape[1] // 2
     return (
         output[None],

time: 643 us -> 429 us (0.67)
  waiting for transfers between devices: 333 us -> 123 us
  matrix products: 90.9 us -> 22.6 us
  Pallas kernels: 29.8 us -> 70.8 us
  starting transfers between devices: 21.8 us -> 47.6 us
  blocking collectives: 44.3 us -> 23.5 us
  other arithmetic: 51 us -> 62.1 us
    psum x1, waiting for transfers between devices: 146 us -> 29.3 us  [on_device(): lax.psum(lax.dynamic_update_slice_in_dim(jnp.zeros((groups, cols_dev, sma...]
    reduce_scatter x3, waiting for transfers between devices: 74.9 us -> 15.9 us  [scatter_sum(): return lax.psum_scatter(values, 'fsdp', scatter_dimension=0, tiled=True)]
    dot_general x24 -> x11, matrix products: 79.4 us -> 22.6 us  [contract(): lax.dot_general(first_op, second_op, (((first_dim,), (second_dim,)), ((),...]
    all_gather x4 -> x3, waiting for transfers between devices: 66.5 us -> 14.9 us  [gather_rows(): return lax.all_gather(values, 'fsdp', axis=0, tiled=True)]
    pallas_call x0 -> x2, Pallas kernels: none -> 40.3 us  [the longest x1 36.7 us: run_branches(): pl.pallas_call(functools.partial(branch_kernel, experts=experts, groups=g...]
    all_gather x1, blocking collectives: 44.3 us -> 10.3 us  [on_device(): qkv_cols = lax.all_gather(qkv_part, 'rep', axis=0)]
    ppermute x0 -> x24, waiting for transfers between devices: none -> 33 us  [swap_rep(): lax.ppermute(values, 'rep', [(i, i ^ 1 << bit) for i in range(count)])]
    ppermute x0 -> x24, starting transfers between devices: none -> 25.8 us  [swap_rep(): lax.ppermute(values, 'rep', [(i, i ^ 1 << bit) for i in range(count)])]
  transfers between devices with their start and end apart: 14 -> 36, of which waited for: 9 -> 12; matrix products, arithmetic and copies ran while one was open for 16% -> 26% of each run, Pallas kernels for 5% -> 8%
where the time goes in v2:
time: 429 us; the launch traced here: 421 us
  waiting for transfers between devices  123 us (29%)
  Pallas kernels  70.8 us (17%)
  other arithmetic  62.1 us (14%)
  local copies, waits for them, and re-layouts  48.1 us (11%)
  starting transfers between devices  47.6 us (11%)
  blocking collectives  23.5 us (5%)
  between operations  23 us (5%)
  matrix products  22.6 us (5%)
    pallas_call x1, Pallas kernels, run_branches(): pl.pallas_call(functools.partial(branch_kernel, experts=experts, groups=g...  36.7 us
    ppermute x24, waiting for transfers between devices, swap_rep(): lax.ppermute(values, 'rep', [(i, i ^ 1 << bit) for i in range(count)])  33 us
    psum x1, waiting for transfers between devices, on_device(): lax.psum(lax.dynamic_update_slice_in_dim(jnp.zeros((groups, cols_dev, sma...  29.3 us
    all_to_all x5, waiting for transfers between devices, exchange(): lax.all_to_all(chunks, 'fsdp', split_axis=0, concat_axis=0, tiled=True)  29.2 us
    ppermute x24, starting transfers between devices, swap_rep(): lax.ppermute(values, 'rep', [(i, i ^ 1 << bit) for i in range(count)])  25.8 us
    unnamed x140, local copies, waits for them, and re-layouts  24.5 us
    dot_general x11, matrix products, contract(): lax.dot_general(first_op, second_op, (((first_dim,), (second_dim,)), ((),...  22.6 us
    all_to_all x5, starting transfers between devices, exchange(): lax.all_to_all(chunks, 'fsdp', split_axis=0, concat_axis=0, tiled=True)  21 us
  transfers between devices with their start and end apart: 36, of which 12 were waited for; matrix products, arithmetic and copies ran while one was open for 26% of the time, Pallas kernels for 8%

profile of v2, /device:TPU:0, one launch (start us, length us, event | category | flops | bytes accessed | tf_op | source)
XLA Modules:
  0.0 420.7 jit_solution(15149242821018424722)
XLA Ops:
  10.8 13.2 %all_to_all.30 = bf16[8,24,384]{2,1,0:T(8,128)(2,1)S(1)} all-to-all(bf16[8,24,384]{2,1,0:T(8,128)(2,1)S(1)} %constant_dynamic-update-slice_fusion), channel_id=1, replica_groups=mesh['rep'=4,'fsdp'=8] {'fsdp'}, dimensions={0} | all-to-all | bytes 294912 | tf_op jit(solution)/shard_map/all_to_all | solution.py:543
  24.0 10.3 %all-gather = bf16[32,24,384]{2,1,0:T(8,128)(2,1)S(1)} all-gather(bf16[8,24,384]{2,1,0:T(8,128)(2,1)S(1)} %all_to_all.30), channel_id=2, replica_groups=mesh['rep'=4,'fsdp'=8] {'rep'}, dimensions={0}, use_global_device_ids=true | all-gather | bytes 737280 | tf_op jit(solution)/shard_map/all_gather | solution.py:652
  40.2 3.5 all-to-all-start.1
  47.0 1.8 fusion.31
  48.8 12.8 %all-to-all-done.1 = bf16[8,24,1408]{2,1,0:T(8,128)(2,1)S(1)} async-done(((bf16[8,24,1408]{2,1,0:T(8,128)(2,1)}), bf16[8,24,1408]{2,1,0:T(8,128)(2,1)S(1)}, u32[]{:S(2)}, u32[]{:S(2)}) %all-to-all-start.1) | async-done | bytes 540704 | tf_op jit(solution)/shard_map/all_to_all | solution.py:543
  61.8 1.3 copy-done.31
  63.3 2.9 fusion
  66.4 3.0 fusion.3
  70.8 13.2 %attn_forward.1 = (f32[128,2048]{1,0:T(8,128)S(1)}, f32[2,2048]{1,0:T(2,128)S(1)}) custom-call(s32[1]{0:T(128)} %copy.114.len_ref, bf16[128,2048]{1,0:T(8,128)(2,1)S(1)} %bitcast.186, bf16[128,2048]{1,0:T(8,128)(2,1)S(1)} %bitcast.184, bf16[128,2048]{1,0:T(8,128)(2,1)S(1)} %slice.494.v_ref), custom_call_target="tpu_custom_call" | custom-call | flops 4294967296 | bytes 4194304 | tf_op jit(solution)/shard_map/attn_forward/pallas_call | solution.py:195
  84.8 11.3 %all-gather.6.cloned.1.call-done.cotangent_ref = bf16[2048,768]{1,0:T(8,128)(2,1)} async-done(((bf16[256,768]{1,0:T(8,128)(2,1)}), bf16[2048,768]{1,0:T(8,128)(2,1)}) %all-gather.6.cloned.1.call-update) | async-done | bytes 3145744 | tf_op jit(solution)/shard_map/all_gather | solution.py:539
  103.2 29.3 %all-reduce.3.cloned.1.call-done.out_w_ref.gate_ref.up_ref.small_ref = bf16[768,1408]{1,0:T(8,128)(2,1)} async-done(((bf16[768,1408]{1,0:T(8,128)(2,1)}), bf16[768,1408]{1,0:T(8,128)(2,1)}) %all-reduce.3.cloned.1.call-update) | async-done | bytes 2162704 | tf_op jit(solution)/shard_map/psum | solution.py:697
  132.5 3.6 all-gather.8.cloned.1.call-done.mixed_ref
  136.1 36.7 %branches.1 = (bf16[2048,768]{1,0:T(8,128)(2,1)}, bf16[2048,896]{1,0:T(8,128)(2,1)}, bf16[2048,768]{1,0:T(8,128)(2,1)}, bf16[2048,256]{1,0:T(8,128)(2,1)}, bf16[...) custom-call(s32[3]{0:T(128)} %pad_add_fusion.info_ref, ...), custom_call_target="tpu_custom_call" | custom-call | flops 21340618752 | bytes 41943040 | tf_op jit(solution)/shard_map/branches/pallas_call | solution.py:375
  175.2 2.4 convolution_convert_fusion.7.refs_2_
  179.0 1.5 collective-permute-start.16
  180.5 2.3 convolution_convert_fusion.3
  182.8 2.3 convolution_convert_fusion.2
  185.7 2.3 convolution_convert_fusion.1
  188.1 3.9 fusion.8
  192.5 1.5 collective-permute-start
  194.0 1.8 convolution_convert_fusion.5.refs_3_
  196.5 1.5 collective-permute-start.12
  198.0 3.0 pad_maximum_fusion.refs_1_
  201.0 15.9 %reduce-scatter.4.cloned.1.call-done.grad_ref = bf16[256,896]{1,0:T(8,128)(2,1)} async-done(((bf16[2048,896]{1,0:T(8,128)(2,1)}), bf16[256,896]{1,0:T(8,128)(2,1)}) %reduce-scatter.4.cloned.1.call-update) | async-done | bytes 458768 | tf_op jit(solution)/shard_map/reduce_scatter | solution.py:547
  216.9 1.9 copy-done.4
  221.8 3.6 own_rows.1
  230.1 4.2 all-to-all-start.2
  235.5 4.5 %add_convert_fusion = (bf16[576,1024]{1,0:T(8,128)(2,1)S(1)}, bf16[576,1024]{1,0:T(8,128)(2,1)S(1)}) fusion(bf16[576,1024]{1,0:T(8,128)(2,1)} %collective-permute-done.2, s32[]{:T(128)S(6)} %select_n.282, bf16[768,1024]{1,0:T(8,128)(2,1)} %copy-done.29, bf16[768,1024]{1,0:T(8,128)(2,1)} %copy-done.30, pred[]{:T(512)} %bitcast.32, ...), kind=kLoop, calls=%fused_computation.18 | loop fusion | flops 10616832 | bytes 9437193 | tf_op jit(solution)/shard_map/convert_element_type | solution.py:576
  240.8 1.5 collective-permute-start.1
  243.2 1.4 collective-permute-start.3
  244.6 2.5 convolution_convert_fusion.4
  247.7 1.6 pad_maximum_fusion.2
  250.9 5.8 %collective-permute-done.1 = bf16[288,1024]{1,0:T(8,128)(2,1)} collective-permute-done((bf16[288,1024]{1,0:T(8,128)(2,1)}, bf16[288,1024]{1,0:T(8,128)(2,1)}, u32[]{:S(2)}, u32[]{:S(2)}) %collective-permute-start.1) | collective-permute-done | bytes 589856 | tf_op jit(solution)/shard_map/ppermute | solution.py:557
  256.7 1.5 add_convert_fusion.4.refs_0_
  258.2 1.5 collective-permute-start.20
  261.1 1.5 collective-permute-start.22
  266.9 17.3 %attn_backward.1 = (f32[128,2048]{1,0:T(8,128)S(1)}, f32[128,2048]{1,0:T(8,128)S(1)}, f32[128,2048]{1,0:T(8,128)S(1)}, f32[8,128]{1,0:T(8,128)S(1)}) custom-call(s32[1]{0:T(128)} %copy.114.len_ref, bf16[128,2048]{1,0:T(8,128)(2,1)S(1)} %bitcast.187, bf16[128,2048]{1,0:T(8,128)(2,1)S(1)} %bitcast.185, bf16[128,2048]{1,0:T(8,128)(2,1)S(1)} %copy-done.15, ...), custom_call_target="tpu_custom_call" | custom-call | flops 10737418240 | bytes 4194304 | tf_op jit(solution)/shard_map/attn_backward/pallas_call | solution.py:219
  288.4 2.0 collective-permute-start.13
  292.8 2.2 convolution_convert_fusion.6
  297.3 3.5 convolution_convert_fusion
  303.1 2.1 collective-permute-start.18
  305.1 1.7 add_convert_fusion.12
  306.9 4.9 %all-to-all-start.5 = ((bf16[8,24,512]{2,1,0:T(8,128)(2,1)}), bf16[8,24,512]{2,1,0:T(8,128)(2,1)S(1)}, u32[]{:S(2)}, u32[]{:S(2)}) async-start(bf16[8,24,512]{2,1,0:T(8,128)(2,1)} %add_convert_fusion.12), calls=%async_computation.8 | async-start | bytes 393216 | tf_op jit(solution)/shard_map/all_to_all | solution.py:543
  311.9 1.6 collective-permute-start.19
  313.5 2.7 maximum_select_fusion.3
  316.7 2.8 maximum_select_fusion.2
  320.6 1.6 collective-permute-start.5
  322.2 1.8 add_convert_fusion.7
  324.9 22.8 %collective-permute-done.5 = bf16[8,24,384]{2,1,0:T(8,128)(2,1)S(1)} collective-permute-done((bf16[8,24,384]{2,1,0:T(8,128)(2,1)S(1)}, bf16[8,24,384]{2,1,0:T(8,128)(2,1)S(1)}, u32[]{:S(2)}, u32[]{:S(2)}) %collective-permute-start.5) | collective-permute-done | bytes 147488 | tf_op jit(solution)/shard_map/ppermute | solution.py:557
  348.4 4.7 %all-to-all-start.3 = ((bf16[8,24,384]{2,1,0:T(8,128)(2,1)}), bf16[8,24,384]{2,1,0:T(8,128)(2,1)S(1)}, u32[]{:S(2)}, u32[]{:S(2)}) async-start(bf16[8,24,384]{2,1,0:T(8,128)(2,1)} %add_convert_fusion.13), calls=%async_computation.6 | async-start | bytes 294912 | tf_op jit(solution)/shard_map/all_to_all | solution.py:543
  353.2 6.9 %all-to-all-done.3 = bf16[8,24,384]{2,1,0:T(8,128)(2,1)S(1)} async-done(((bf16[8,24,384]{2,1,0:T(8,128)(2,1)}), bf16[8,24,384]{2,1,0:T(8,128)(2,1)S(1)}, u32[]{:S(2)}, u32[]{:S(2)}) %all-to-all-start.3) | async-done | bytes 147488 | tf_op jit(solution)/shard_map/all_to_all | solution.py:543
  360.1 3.7 all-to-all-start.4
  364.2 1.6 collective-permute-start.6
  365.8 9.4 %all-to-all-done.4 = bf16[8,24,773]{2,1,0:T(8,128)(2,1)S(1)} async-done(((bf16[8,24,773]{2,1,0:T(8,128)(2,1)}), bf16[8,24,773]{2,1,0:T(8,128)(2,1)S(1)}, u32[]{:S(2)}, u32[]{:S(2)}) %all-to-all-start.4) | async-done | bytes 296864 | tf_op jit(solution)/shard_map/all_to_all | solution.py:543
  375.3 1.6 collective-permute-start.10
  379.5 2.1 collective-permute-start.7
  381.6 2.9 collective-permute-done.11
  390.4 1.6 fusion.18
  393.3 2.9 maximum_select_fusion.1
  396.2 2.7 maximum_select_fusion
  400.1 4.0 slice_bitcast_fusion
  404.1 3.6 copy.94
  407.7 1.9 fusion.21
  410.9 2.1 fusion.15
  (310 shorter events, 66.7 us)
Async XLA Ops:
  8.0 31.1 %copy-start = (bf16[96,768]{1,0:T(8,128)(2,1)S(1)}, bf16[96,768]{1,0:T(8,128)(2,1)}, u32[]{:S(2)}) copy-start(bf16[96,768]{1,0:T(8,128)(2,1)} %param.27) | copy-start | bytes 442372
  8.0 28.3 %copy-start.7 = (bf16[1,256,768]{2,1,0:T(8,128)(2,1)S(1)}, bf16[1,256,768]{2,1,0:T(8,128)(2,1)}, u32[]{:S(2)}) copy-start(bf16[1,256,768]{2,1,0:T(8,128)(2,1)} %param.19) | copy-start | bytes 1179652
  8.0 29.1 %copy-start.55 = (s32[1,256,2]{1,2,0:T(2,128)S(1)}, s32[1,256,2]{1,2,0:T(2,128)}, u32[]{:S(2)}) copy-start(s32[1,256,2]{1,2,0:T(2,128)} %param.21) | copy-start | bytes 6148
  8.1 29.1 %copy-start.56 = (bf16[96,4]{0,1:T(4,128)(2,1)S(1)}, bf16[96,4]{0,1:T(4,128)(2,1)}, u32[]{:S(2)}) copy-start(bf16[96,4]{0,1:T(4,128)(2,1)} %param.28) | copy-start | bytes 2308
  8.1 29.3 %copy-start.59 = (bf16[96]{0:T(256)(128)(2,1)S(1)}, bf16[96]{0:T(256)(128)(2,1)}, u32[]{:S(2)}) copy-start(bf16[96]{0:T(256)(128)(2,1)} %param.23) | copy-start | bytes 580
  8.1 55.2 %all-gather.10.cloned.1.call-start = ((), (), s32[]{:S(2)}) async-start(), calls=%async_computation.15 | async-start | bytes 3538944 | tf_op jit(solution)/shard_map/all_gather | solution.py:539
  8.8 87.3 %all-gather.6.cloned.1.call-start = ((), (), s32[]{:S(2)}) async-start(), calls=%async_computation.9 | async-start | bytes 3538944 | tf_op jit(solution)/shard_map/all_gather | solution.py:539
  37.2 7.3 %copy-start.61 = (s32[8]{0:T(128)S(1)}, s32[8]{0:T(128)}, u32[]{:S(2)}) copy-start(s32[8]{0:T(128)} %constant.93.clone) | copy-start | bytes 100
  40.2 21.4 %all-to-all-start.1 = ((bf16[8,24,1408]{2,1,0:T(8,128)(2,1)}), bf16[8,24,1408]{2,1,0:T(8,128)(2,1)S(1)}, u32[]{:S(2)}, u32[]{:S(2)}) async-start(bf16[8,24,1408]{2,1,0:T(8,128)(2,1)} %maximum_select_fusion.5), calls=%async_computation.1 | async-start | bytes 1081344 | tf_op jit(solution)/shard_map/all_to_all | solution.py:543
  43.7 88.8 %all-reduce.3.cloned.1.call-start = ((), (), s32[]{:S(2)}) async-start(), calls=%async_computation.11 | async-start | bytes 4325376 | tf_op jit(solution)/shard_map/psum | solution.py:697
  48.8 20.8 %copy-start.41 = (f32[32,2048]{1,0:T(8,128)}, f32[32,2048]{1,0:T(8,128)S(1)}, u32[]{:S(2)}) copy-start(f32[32,2048]{1,0:T(8,128)S(1)} %get-tuple-element.211) | copy-start | bytes 786436
  63.2 72.9 %all-gather.8.cloned.1.call-start = ((), (), s32[]{:S(2)}) async-start(), calls=%async_computation.10 | async-start | bytes 3538944 | tf_op jit(solution)/shard_map/all_gather | solution.py:539
  84.8 88.0 %copy-start.25 = (f32[128,2048]{1,0:T(8,128)}, f32[128,2048]{1,0:T(8,128)S(1)}, u32[]{:S(2)}) copy-start(f32[128,2048]{1,0:T(8,128)S(1)} %get-tuple-element.39.o_ref) | copy-start | bytes 3145732
  98.8 118.1 %reduce-scatter.4.cloned.1.call-start = ((), (), s32[]{:S(2)}) async-start(), calls=%async_computation.12 | async-start | bytes 4128768 | tf_op jit(solution)/shard_map/reduce_scatter | solution.py:547
  172.8 234.9 %reduce-scatter.6.cloned.1.call-start = ((), (), s32[]{:S(2)}) async-start(), calls=%async_computation.13 | async-start | bytes 3538944 | tf_op jit(solution)/shard_map/reduce_scatter | solution.py:547
  175.2 5.3 %copy-start.64 = (bf16[1280,1024]{1,0:T(8,128)(2,1)S(1)}, bf16[1280,1024]{1,0:T(8,128)(2,1)}, u32[]{:S(2)}) copy-start(bf16[1280,1024]{1,0:T(8,128)(2,1)} %get-tuple-element.43) | copy-start | bytes 7864324
  179.0 106.4 %collective-permute-start.16 = (bf16[128,768]{1,0:T(8,128)(2,1)}, bf16[128,768]{1,0:T(8,128)(2,1)}, u32[]{:S(2)}, u32[]{:S(2)}) collective-permute-start(bf16[128,768]{1,0:T(8,128)(2,1)} %constant_dynamic-slice_fusion.1), channel_id=1, source_target_pairs={{0,16},{8,24},{16,0},{24,8},{1,17},{9,25},{17,1},{25,9},{2,18},{10... | collective-permute-start | bytes 589832 | tf_op jit(solution)/shard_map/ppermute | solution.py:557
  182.8 15.3 %copy-start.28 = (bf16[768,1024]{1,0:T(8,128)(2,1)}, bf16[768,1024]{1,0:T(8,128)(2,1)S(1)}, u32[]{:S(2)}) copy-start(bf16[768,1024]{1,0:T(8,128)(2,1)S(1)} %convolution_convert_fusion.3) | copy-start | bytes 4718596
  185.1 13.0 %copy-start.29 = (bf16[768,1024]{1,0:T(8,128)(2,1)}, bf16[768,1024]{1,0:T(8,128)(2,1)S(1)}, u32[]{:S(2)}) copy-start(bf16[768,1024]{1,0:T(8,128)(2,1)S(1)} %convolution_convert_fusion.2) | copy-start | bytes 4718596
  188.0 10.0 %copy-start.30 = (bf16[768,1024]{1,0:T(8,128)(2,1)}, bf16[768,1024]{1,0:T(8,128)(2,1)S(1)}, u32[]{:S(2)}) copy-start(bf16[768,1024]{1,0:T(8,128)(2,1)S(1)} %convolution_convert_fusion.1) | copy-start | bytes 4718596
  188.0 5.9 %copy-start.39 = (bf16[2048,768]{1,0:T(8,128)(2,1)S(1)}, bf16[2048,768]{1,0:T(8,128)(2,1)}, u32[]{:S(2)}) copy-start(bf16[2048,768]{1,0:T(8,128)(2,1)} %get-tuple-element.48) | copy-start | bytes 9437188
  188.0 5.9 %copy-start.43 = (bf16[2048,512]{1,0:T(8,128)(2,1)S(1)}, bf16[2048,512]{1,0:T(8,128)(2,1)}, u32[]{:S(2)}) copy-start(bf16[2048,512]{1,0:T(8,128)(2,1)} %get-tuple-element.49) | copy-start | bytes 6291460
  191.9 43.5 %collective-permute-start.2 = (bf16[576,1024]{1,0:T(8,128)(2,1)}, bf16[576,1024]{1,0:T(8,128)(2,1)}, u32[]{:S(2)}, u32[]{:S(2)}) collective-permute-start(bf16[576,1024]{1,0:T(8,128)(2,1)} %get-tuple-element.141), channel_id=1, source_target_pairs={{0,16},{8,24},{16,0},{24,8},{1,17},{9,25},{17,1},{25,9},{2,18},{10... | collective-permute-start | bytes 3538952 | tf_op jit(solution)/shard_map/ppermute | solution.py:557
  192.5 43.0 %collective-permute-start = (bf16[576,1024]{1,0:T(8,128)(2,1)}, bf16[576,1024]{1,0:T(8,128)(2,1)}, u32[]{:S(2)}, u32[]{:S(2)}) collective-permute-start(bf16[576,1024]{1,0:T(8,128)(2,1)} %get-tuple-element.142), channel_id=1, source_target_pairs={{0,8},{8,0},{16,24},{24,16},{1,9},{9,1},{17,25},{25,17},{2,10},{10... | collective-permute-start | bytes 3538952 | tf_op jit(solution)/shard_map/ppermute | solution.py:557
  196.5 20.4 %copy-start.2 = (bf16[768,1408]{1,0:T(8,128)(2,1)S(1)}, bf16[768,1408]{1,0:T(8,128)(2,1)}, u32[]{:S(2)}) copy-start(bf16[768,1408]{1,0:T(8,128)(2,1)} %all-reduce.3.cloned.1.call-done.out_w_ref.gate_ref.up_ref.small_ref) | copy-start | bytes 6488068
  196.5 20.4 %copy-start.3 = (bf16[1,256,768]{2,1,0:T(8,128)(2,1)S(1)}, bf16[1,256,768]{2,1,0:T(8,128)(2,1)}, u32[]{:S(2)}) copy-start(bf16[1,256,768]{2,1,0:T(8,128)(2,1)} %param.18) | copy-start | bytes 1179652
  196.5 20.4 %copy-start.27 = (s32[3]{0:T(128)S(1)}, s32[3]{0:T(128)}, u32[]{:S(2)}) copy-start(s32[3]{0:T(128)} %pad_add_fusion.info_ref) | copy-start | bytes 40
  196.5 90.0 %collective-permute-start.12 = (bf16[8,48,512]{2,1,0:T(8,128)(2,1)}, bf16[8,48,512]{2,1,0:T(8,128)(2,1)}, u32[]{:S(2)}, u32[]{:S(2)}) collective-permute-start(bf16[8,48,512]{2,1,0:T(8,128)(2,1)} %constant_dynamic-slice_fusion.3), channel_id=1, source_target_pairs={{0,16},{8,24},{16,0},{24,8},{1,17},{9,25},{17,1},{25,9},{2,18},{10... | collective-permute-start | bytes 1179656 | tf_op jit(solution)/shard_map/ppermute | solution.py:557
  228.7 5.6 %copy-start.24 = (bf16[256,768]{1,0:T(8,128)(2,1)S(1)}, bf16[256,768]{1,0:T(8,128)(2,1)}, u32[]{:S(2)}) copy-start(bf16[256,768]{1,0:T(8,128)(2,1)} %copy-done.23) | copy-start | bytes 1179652
  229.9 5.4 %copy-start.22 = (bf16[256,768]{1,0:T(8,128)(2,1)S(1)}, bf16[256,768]{1,0:T(8,128)(2,1)}, u32[]{:S(2)}) copy-start(bf16[256,768]{1,0:T(8,128)(2,1)} %copy-done.21) | copy-start | bytes 1179652
  230.1 32.4 %all-to-all-start.2 = ((bf16[8,128,256]{2,1,0:T(8,128)(2,1)}), bf16[8,128,256]{2,1,0:T(8,128)(2,1)}, u32[]{:S(2)}, u32[]{:S(2)}) async-start(bf16[8,128,256]{2,1,0:T(8,128)(2,1)} %get-tuple-element.54), calls=%async_computation.4 | async-start | bytes 1048576 | tf_op jit(solution)/shard_map/all_to_all | solution.py:543
  234.3 175.4 %reduce-scatter.8.cloned.1.call-start = ((), (), s32[]{:S(2)}) async-start(), calls=%async_computation.14 | async-start | bytes 3538944 | tf_op jit(solution)/shard_map/reduce_scatter | solution.py:547
  239.9 7.1 %copy-start.34 = (bf16[576,1024]{1,0:T(8,128)(2,1)}, bf16[576,1024]{1,0:T(8,128)(2,1)S(1)}, u32[]{:S(2)}) copy-start(bf16[576,1024]{1,0:T(8,128)(2,1)S(1)} %get-tuple-element.139) | copy-start | bytes 3538948
  239.9 7.1 %copy-start.36 = (bf16[576,1024]{1,0:T(8,128)(2,1)}, bf16[576,1024]{1,0:T(8,128)(2,1)S(1)}, u32[]{:S(2)}) copy-start(bf16[576,1024]{1,0:T(8,128)(2,1)S(1)} %get-tuple-element.140) | copy-start | bytes 3538948
  240.0 7.1 %copy-start.44 = (bf16[768,256]{1,0:T(8,128)(2,1)S(1)}, bf16[768,256]{1,0:T(8,128)(2,1)}, u32[]{:S(2)}) copy-start(bf16[768,256]{1,0:T(8,128)(2,1)} %copy.88) | copy-start | bytes 1179652
  240.8 15.9 %collective-permute-start.1 = (bf16[288,1024]{1,0:T(8,128)(2,1)}, bf16[288,1024]{1,0:T(8,128)(2,1)}, u32[]{:S(2)}, u32[]{:S(2)}) collective-permute-start(bf16[288,1024]{1,0:T(8,128)(2,1)} %constant_dynamic-slice_fusion.9), channel_id=1, source_target_pairs={{0,16},{8,24},{16,0},{24,8},{1,17},{9,25},{17,1},{25,9},{2,18},{10... | collective-permute-start | bytes 1769480 | tf_op jit(solution)/shard_map/ppermute | solution.py:557
  243.2 16.6 %collective-permute-start.3 = (bf16[288,1024]{1,0:T(8,128)(2,1)}, bf16[288,1024]{1,0:T(8,128)(2,1)}, u32[]{:S(2)}, u32[]{:S(2)}) collective-permute-start(bf16[288,1024]{1,0:T(8,128)(2,1)} %constant_dynamic-slice_fusion.8), channel_id=1, source_target_pairs={{0,8},{8,0},{16,24},{24,16},{1,9},{9,1},{17,25},{25,17},{2,10},{10... | collective-permute-start | bytes 1769480 | tf_op jit(solution)/shard_map/ppermute | solution.py:557
  247.7 12.1 %copy-start.35 = (bf16[576,1024]{1,0:T(8,128)(2,1)S(1)}, bf16[576,1024]{1,0:T(8,128)(2,1)}, u32[]{:S(2)}) copy-start(bf16[576,1024]{1,0:T(8,128)(2,1)} %copy-done.34) | copy-start | bytes 3538948
  249.3 11.8 %copy-start.32 = (bf16[8,96,773]{2,1,0:T(8,128)(2,1)}, bf16[8,96,773]{2,1,0:T(8,128)(2,1)S(1)}, u32[]{:S(2)}) copy-start(bf16[8,96,773]{2,1,0:T(8,128)(2,1)S(1)} %pad_maximum_fusion.2) | copy-start | bytes 3561988
  250.3 45.5 %collective-permute-start.8 = (bf16[8,48,773]{2,1,0:T(8,128)(2,1)}, bf16[8,48,773]{2,1,0:T(8,128)(2,1)}, u32[]{:S(2)}, u32[]{:S(2)}) collective-permute-start(bf16[8,48,773]{2,1,0:T(8,128)(2,1)} %constant_dynamic-slice_fusion.5), channel_id=1, source_target_pairs={{0,8},{8,0},{16,24},{24,16},{1,9},{9,1},{17,25},{25,17},{2,10},{10... | collective-permute-start | bytes 1781000 | tf_op jit(solution)/shard_map/ppermute | solution.py:557
  258.2 58.5 %collective-permute-start.20 = (bf16[288,1024]{1,0:T(8,128)(2,1)S(1)}, bf16[288,1024]{1,0:T(8,128)(2,1)}, u32[]{:S(2)}, u32[]{:S(2)}) collective-permute-start(bf16[288,1024]{1,0:T(8,128)(2,1)S(1)} %add_convert_fusion.4.refs_0_), channel_id=1, source_target_pairs={{0,16},{8,24},{16,0},{24,8},{1,17},{9,25},{17,1},{25,9},{2,18},{10... | collective-permute-start | bytes 1769480 | tf_op jit(solution)/shard_map/ppermute | solution.py:557
  261.1 52.4 %collective-permute-start.22 = (bf16[288,1024]{1,0:T(8,128)(2,1)S(1)}, bf16[288,1024]{1,0:T(8,128)(2,1)}, u32[]{:S(2)}, u32[]{:S(2)}) collective-permute-start(bf16[288,1024]{1,0:T(8,128)(2,1)S(1)} %add_convert_fusion.3.refs_1_), channel_id=1, source_target_pairs={{0,8},{8,0},{16,24},{24,16},{1,9},{9,1},{17,25},{25,17},{2,10},{10... | collective-permute-start | bytes 1769480 | tf_op jit(solution)/shard_map/ppermute | solution.py:557
  266.9 18.5 %copy-start.11 = (bf16[256,768]{1,0:T(8,128)(2,1)S(1)}, bf16[256,768]{1,0:T(8,128)(2,1)}, u32[]{:S(2)}) copy-start(bf16[256,768]{1,0:T(8,128)(2,1)} %copy-done.9) | copy-start | bytes 1179652
  284.2 6.3 %copy-start.42 = (f32[32,2048]{1,0:T(8,128)S(1)}, f32[32,2048]{1,0:T(8,128)}, u32[]{:S(2)}) copy-start(f32[32,2048]{1,0:T(8,128)} %copy-done.41) | copy-start | bytes 786436
  284.2 6.3 %copy-start.46 = (f32[32,2048]{1,0:T(8,128)S(1)}, f32[32,2048]{1,0:T(8,128)}, u32[]{:S(2)}) copy-start(f32[32,2048]{1,0:T(8,128)} %get-tuple-element.209) | copy-start | bytes 786436
  286.4 15.1 %collective-permute-start.17 = (bf16[64,768]{1,0:T(8,128)(2,1)S(1)}, bf16[64,768]{1,0:T(8,128)(2,1)}, u32[]{:S(2)}, u32[]{:S(2)}) collective-permute-start(bf16[64,768]{1,0:T(8,128)(2,1)S(1)} %constant_dynamic-slice_fusion), channel_id=1, source_target_pairs={{0,8},{8,0},{16,24},{24,16},{1,9},{9,1},{17,25},{25,17},{2,10},{10... | collective-permute-start | bytes 294920 | tf_op jit(solution)/shard_map/ppermute | solution.py:557
  288.4 14.6 %collective-permute-start.13 = (bf16[8,24,512]{2,1,0:T(8,128)(2,1)}, bf16[8,24,512]{2,1,0:T(8,128)(2,1)}, u32[]{:S(2)}, u32[]{:S(2)}) collective-permute-start(bf16[8,24,512]{2,1,0:T(8,128)(2,1)} %constant_dynamic-slice_fusion.2), channel_id=1, source_target_pairs={{0,8},{8,0},{16,24},{24,16},{1,9},{9,1},{17,25},{25,17},{2,10},{10... | collective-permute-start | bytes 589832 | tf_op jit(solution)/shard_map/ppermute | solution.py:557
  295.9 23.6 %collective-permute-start.4 = (bf16[8,48,384]{2,1,0:T(8,128)(2,1)}, bf16[8,48,384]{2,1,0:T(8,128)(2,1)}, u32[]{:S(2)}, u32[]{:S(2)}) collective-permute-start(bf16[8,48,384]{2,1,0:T(8,128)(2,1)} %constant_dynamic-slice_fusion.7), channel_id=1, source_target_pairs={{0,8},{8,0},{16,24},{24,16},{1,9},{9,1},{17,25},{25,17},{2,10},{10... | collective-permute-start | bytes 884744 | tf_op jit(solution)/shard_map/ppermute | solution.py:557
  301.5 20.6 %collective-permute-start.9 = (bf16[8,24,773]{2,1,0:T(8,128)(2,1)}, bf16[8,24,773]{2,1,0:T(8,128)(2,1)}, u32[]{:S(2)}, u32[]{:S(2)}) collective-permute-start(bf16[8,24,773]{2,1,0:T(8,128)(2,1)} %constant_dynamic-slice_fusion.4), channel_id=1, source_target_pairs={{0,16},{8,24},{16,0},{24,8},{1,17},{9,25},{17,1},{25,9},{2,18},{10... | collective-permute-start | bytes 890504 | tf_op jit(solution)/shard_map/ppermute | solution.py:557
  303.1 8.7 %collective-permute-start.18 = (bf16[64,768]{1,0:T(8,128)(2,1)S(1)}, bf16[64,768]{1,0:T(8,128)(2,1)S(1)}, u32[]{:S(2)}, u32[]{:S(2)}) collective-permute-start(bf16[64,768]{1,0:T(8,128)(2,1)S(1)} %add_convert_fusion.14), channel_id=1, source_target_pairs={{0,8},{8,0},{16,24},{24,16},{1,9},{9,1},{17,25},{25,17},{2,10},{10... | collective-permute-start | bytes 294920 | tf_op jit(solution)/shard_map/ppermute | solution.py:557
  306.9 41.5 %all-to-all-start.5 = ((bf16[8,24,512]{2,1,0:T(8,128)(2,1)}), bf16[8,24,512]{2,1,0:T(8,128)(2,1)S(1)}, u32[]{:S(2)}, u32[]{:S(2)}) async-start(bf16[8,24,512]{2,1,0:T(8,128)(2,1)} %add_convert_fusion.12), calls=%async_computation.8 | async-start | bytes 393216 | tf_op jit(solution)/shard_map/all_to_all | solution.py:543
  311.9 7.7 %copy-start.49 = (bf16[768,384]{1,0:T(8,128)(2,1)S(1)}, bf16[768,384]{1,0:T(8,128)(2,1)}, u32[]{:S(2)}) copy-start(bf16[768,384]{1,0:T(8,128)(2,1)} %copy-done.48) | copy-start | bytes 1769476
  311.9 12.1 %collective-permute-start.19 = (bf16[128,768]{1,0:T(8,128)(2,1)S(1)}, bf16[128,768]{1,0:T(8,128)(2,1)S(1)}, u32[]{:S(2)}, u32[]{:S(2)}) collective-permute-start(bf16[128,768]{1,0:T(8,128)(2,1)S(1)} %maximum_select_fusion.10), channel_id=1, source_target_pairs={{0,16},{8,24},{16,0},{24,8},{1,17},{9,25},{17,1},{25,9},{2,18},{10... | collective-permute-start | bytes 589832 | tf_op jit(solution)/shard_map/ppermute | solution.py:557
  316.2 77.1 %collective-permute-start.23 = (bf16[576,1024]{1,0:T(8,128)(2,1)}, bf16[576,1024]{1,0:T(8,128)(2,1)}, u32[]{:S(2)}, u32[]{:S(2)}) collective-permute-start(bf16[576,1024]{1,0:T(8,128)(2,1)} %maximum_select_fusion.3), channel_id=1, source_target_pairs={{0,16},{8,24},{16,0},{24,8},{1,17},{9,25},{17,1},{25,9},{2,18},{10... | collective-permute-start | bytes 3538952 | tf_op jit(solution)/shard_map/ppermute | solution.py:557
  319.5 76.7 %collective-permute-start.21 = (bf16[576,1024]{1,0:T(8,128)(2,1)}, bf16[576,1024]{1,0:T(8,128)(2,1)}, u32[]{:S(2)}, u32[]{:S(2)}) collective-permute-start(bf16[576,1024]{1,0:T(8,128)(2,1)} %maximum_select_fusion.2), channel_id=1, source_target_pairs={{0,8},{8,0},{16,24},{24,16},{1,9},{9,1},{17,25},{25,17},{2,10},{10... | collective-permute-start | bytes 3538952 | tf_op jit(solution)/shard_map/ppermute | solution.py:557
  320.6 27.1 %collective-permute-start.5 = (bf16[8,24,384]{2,1,0:T(8,128)(2,1)S(1)}, bf16[8,24,384]{2,1,0:T(8,128)(2,1)S(1)}, u32[]{:S(2)}, u32[]{:S(2)}) collective-permute-start(bf16[8,24,384]{2,1,0:T(8,128)(2,1)S(1)} %constant_dynamic-slice_fusion.6), channel_id=1, source_target_pairs={{0,16},{8,24},{16,0},{24,8},{1,17},{9,25},{17,1},{25,9},{2,18},{10... | collective-permute-start | bytes 442376 | tf_op jit(solution)/shard_map/ppermute | solution.py:557
  348.4 11.7 %all-to-all-start.3 = ((bf16[8,24,384]{2,1,0:T(8,128)(2,1)}), bf16[8,24,384]{2,1,0:T(8,128)(2,1)S(1)}, u32[]{:S(2)}, u32[]{:S(2)}) async-start(bf16[8,24,384]{2,1,0:T(8,128)(2,1)} %add_convert_fusion.13), calls=%async_computation.6 | async-start | bytes 294912 | tf_op jit(solution)/shard_map/all_to_all | solution.py:543
  360.1 15.1 %all-to-all-start.4 = ((bf16[8,24,773]{2,1,0:T(8,128)(2,1)}), bf16[8,24,773]{2,1,0:T(8,128)(2,1)S(1)}, u32[]{:S(2)}, u32[]{:S(2)}) async-start(bf16[8,24,773]{2,1,0:T(8,128)(2,1)} %add_convert_fusion.7), calls=%async_computation.7 | async-start | bytes 688128 | tf_op jit(solution)/shard_map/all_to_all | solution.py:543
  363.8 13.0 %collective-permute-start.14 = (bf16[24,4096]{1,0:T(8,128)(2,1)S(1)}, bf16[24,4096]{1,0:T(8,128)(2,1)S(1)}, u32[]{:S(2)}, u32[]{:S(2)}) collective-permute-start(bf16[24,4096]{1,0:T(8,128)(2,1)S(1)} %constant_dynamic-update-slice_fusion.8), channel_id=1, source_target_pairs={{0,8},{8,0},{16,24},{24,16},{1,9},{9,1},{17,25},{25,17},{2,10},{10... | collective-permute-start | bytes 589832 | tf_op jit(solution)/shard_map/ppermute | solution.py:557
  364.2 15.3 %collective-permute-start.6 = (bf16[24,2304]{1,0:T(8,128)(2,1)S(1)}, bf16[24,2304]{1,0:T(8,128)(2,1)S(1)}, u32[]{:S(2)}, u32[]{:S(2)}) collective-permute-start(bf16[24,2304]{1,0:T(8,128)(2,1)S(1)} %concatenate.147), channel_id=1, source_target_pairs={{0,16},{8,24},{16,0},{24,8},{1,17},{9,25},{17,1},{25,9},{2,18},{10... | collective-permute-start | bytes 331784 | tf_op jit(solution)/shard_map/ppermute | solution.py:557
  375.3 4.1 collective-permute-start.10
  377.7 12.8 %collective-permute-start.15 = (bf16[48,4096]{1,0:T(8,128)(2,1)}, bf16[48,4096]{1,0:T(8,128)(2,1)}, u32[]{:S(2)}, u32[]{:S(2)}) collective-permute-start(bf16[48,4096]{1,0:T(8,128)(2,1)} %maximum_select_fusion.7), channel_id=1, source_target_pairs={{0,16},{8,24},{16,0},{24,8},{1,17},{9,25},{17,1},{25,9},{2,18},{10... | collective-permute-start | bytes 1179656 | tf_op jit(solution)/shard_map/ppermute | solution.py:557
  379.4 5.1 %collective-permute-start.11 = (bf16[48,773]{1,0:T(8,128)(2,1)S(1)}, bf16[48,773]{1,0:T(8,128)(2,1)S(1)}, u32[]{:S(2)}, u32[]{:S(2)}) collective-permute-start(bf16[48,773]{1,0:T(8,128)(2,1)S(1)} %maximum_select_fusion.12), channel_id=1, source_target_pairs={{0,8},{8,0},{16,24},{24,16},{1,9},{9,1},{17,25},{25,17},{2,10},{10... | collective-permute-start | bytes 222632 | tf_op jit(solution)/shard_map/ppermute | solution.py:557
  379.5 7.3 %collective-permute-start.7 = (bf16[48,2304]{1,0:T(8,128)(2,1)S(1)}, bf16[48,2304]{1,0:T(8,128)(2,1)S(1)}, u32[]{:S(2)}, u32[]{:S(2)}) collective-permute-start(bf16[48,2304]{1,0:T(8,128)(2,1)S(1)} %maximum_select_fusion.9), channel_id=1, source_target_pairs={{0,8},{8,0},{16,24},{24,16},{1,9},{9,1},{17,25},{25,17},{2,10},{10... | collective-permute-start | bytes 663560 | tf_op jit(solution)/shard_map/ppermute | solution.py:557
  (39 other events, 78.0 us)
Sparse Core Ops, SparseCore 0:
  10.5 42.9 all-gather.9
  55.8 40.3 all-gather.5
  98.9 37.1 all-gather.7
  173.0 43.9 reduce-scatter.3
  230.0 46.6 reduce-scatter.5
  301.7 44.3 reduce-scatter.7
Sparse Core Ops, SparseCore 1:
  63.3 69.2 all-reduce.2

commit v3 on v2

--- a/solution.py
+++ b/solution.py
@@ -14,6 +14,8 @@
 ROPE_BASE = 10000.0
 NEG_FILL = -1e30
 MARK = (8, 128)
+ALL_VMEM = 60 << 20
+IN_HBM = pl.BlockSpec(memory_space=pltpu.HBM)
 F32 = jnp.float32
 BF16 = jnp.bfloat16
 
@@ -76,6 +78,16 @@
         [first * cosine - second * sine, second * cosine + first * sine], axis=1
     )
     return turned.reshape(rows, seq_len)
+
+
+def put_halves(values, mine, keep_ref, send_ref, at=0):
+    groups, rows, _ = keep_ref.shape
+    cols = slice(at, at + values.shape[1])
+    for dest in range(groups):
+        first = values[2 * dest * rows : (2 * dest + 1) * rows]
+        last = values[(2 * dest + 1) * rows : (2 * dest + 2) * rows]
+        keep_ref[dest, :, cols] = jnp.where(mine == 0, first, last).astype(BF16)
+        send_ref[dest, :, cols] = jnp.where(mine == 0, last, first).astype(BF16)
 
 
 def attn_forward_kernel(len_ref, q_ref, k_ref, v_ref, o_ref, l_ref, *, heads, blk):
@@ -226,13 +238,89 @@
             num_scalar_prefetch=1,
             grid=(seq_len // blk,),
             in_specs=[block, whole, whole, block, stats, sources]
-            + [pl.BlockSpec(memory_space=pl.ANY)] * len(earlier),
+            + [IN_HBM] * len(earlier),
             out_specs=(block, whole, whole, pl.BlockSpec(MARK, lambda i, _: (0, 0))),
         ),
-        compiler_params=pltpu.CompilerParams(vmem_limit_bytes=40 << 20),
-        cost_estimate=attn_cost(rows, seq_len, heads, 5),
+        compiler_params=pltpu.CompilerParams(vmem_limit_bytes=ALL_VMEM),
+        cost_estimate=pl.CostEstimate(flops=0, bytes_accessed=0, transcendentals=0),
         name="attn_backward",
     )(length, queries, keys, values, mixed, log_norm, grad_mixed, *earlier)
+
+
+def projections_kernel(
+    info_ref, dq_ref, dk_ref, dv_ref, cos_ref, sin_ref, unit_ref, w_ref, *refs, cols_dev
+):
+    grad_ref, keep_ref, send_ref, total_ref = refs[-4:]
+    rows = dq_ref.shape[0]
+    cosine, sine = (cos_ref[...], sin_ref[...])
+    channel = lax.broadcasted_iota(jnp.int32, (rows, 1), 0)
+    owned = ((channel >= info_ref[3]) & (channel < info_ref[3] + cols_dev)).astype(F32)
+
+    def turn_back(values):
+        parts = []
+        for at in range(0, rows, HEAD_DIM):
+            first = values[at : at + HEAD_DIM // 2]
+            second = values[at + HEAD_DIM // 2 : at + HEAD_DIM]
+            parts += [first * cosine + second * sine, second * cosine - first * sine]
+        return jnp.concatenate(parts, axis=0)
+
+    grads = jnp.concatenate(
+        [
+            (owned * turn_back(dq_ref[...] * 0.125)).astype(BF16),
+            (owned * turn_back(dk_ref[...])).astype(BF16),
+            (owned * dv_ref[...]).astype(BF16),
+        ],
+        axis=0,
+    )
+    grad_ref[...] = contract(grads, w_ref[...], 0, 1).astype(BF16)
+    part = matmul(grads, unit_ref[...])
+
+    @pl.when(pl.program_id(0) == 0)
+    def _():
+        total_ref[...] = part
+
+    @pl.when(pl.program_id(0) > 0)
+    def _():
+        total_ref[...] += part
+
+    @pl.when(pl.program_id(0) == pl.num_programs(0) - 1)
+    def _():
+        put_halves(total_ref[...].T, info_ref[4], keep_ref, send_ref)
+
+
+def projections_backward(
+    info, grad_q, grad_k, grad_v, cosine, sine, unit, weight, cols_dev, earlier
+):
+    rows, seq_len = grad_q.shape
+    width = unit.shape[1]
+    blk = min(512, seq_len)
+
+    def part(count):
+        return pl.BlockSpec((count, blk), lambda i, _: (0, i))
+
+    by_row = pl.BlockSpec((blk, width), lambda i, _: (i, 0))
+    whole = pl.BlockSpec(weight.shape, lambda i, _: (0, 0))
+    half_shape = (width // cols_dev, cols_dev // 2, 3 * rows)
+    return pl.pallas_call(
+        functools.partial(projections_kernel, cols_dev=cols_dev),
+        out_shape=(
+            pltpu.HBM((seq_len, width), BF16),
+            *(jax.ShapeDtypeStruct(half_shape, BF16),) * 2,
+        ),
+        grid_spec=pltpu.PrefetchScalarGridSpec(
+            num_scalar_prefetch=1,
+            grid=(seq_len // blk,),
+            in_specs=[part(rows)] * 3
+            + [part(HEAD_DIM // 2)] * 2
+            + [by_row, whole]
+            + [IN_HBM] * len(earlier),
+            out_specs=(by_row, *(pl.BlockSpec(half_shape, lambda i, _: (0, 0, 0)),) * 2),
+            scratch_shapes=[pltpu.VMEM((3 * rows, width), F32)],
+        ),
+        compiler_params=pltpu.CompilerParams(vmem_limit_bytes=40 << 20),
+        cost_estimate=pl.CostEstimate(flops=0, bytes_accessed=0, transcendentals=0),
+        name="projections_backward",
+    )(info, grad_q, grad_k, grad_v, cosine, sine, unit, weight, *earlier)
 
 
 def branch_kernel(
@@ -416,7 +504,7 @@
                 step_rows(picked, width),
             ),
         ),
-        compiler_params=pltpu.CompilerParams(vmem_limit_bytes=56 << 20),
+        compiler_params=pltpu.CompilerParams(vmem_limit_bytes=ALL_VMEM),
         cost_estimate=pl.CostEstimate(
             flops=flops, bytes_accessed=40 << 20, transcendentals=2 * all_picked * ehidden
         ),
@@ -432,15 +520,15 @@
     cotangent_ref,
     out_w_ref,
     small_ref,
+    shared_ref,
     *refs,
     experts,
     groups,
     window_starts,
 ):
-    hidden_ref, grad_hidden_ref, grad_mixed_ref, normed_ref, logits_ref, back_ref, mark_ref = refs[
-        -8:-1
+    hidden_ref, grad_hidden_ref, grad_mixed_ref, *first_refs, last_keep_ref, last_send_ref = refs[
+        -7:
     ]
-    mark_ref[...] = jnp.zeros_like(mark_ref)
     rows, width = tokens_ref.shape
     length, me = (info_ref[0], info_ref[1])
     small = small_ref[...].astype(F32)
@@ -475,17 +563,22 @@
     )
     hidden_ref[...] = hidden * live
     grad_hidden_ref[...] = grad_hidden
-    grad_mixed = matmul_nt(out_w_ref[...], grad_hidden.astype(BF16)).astype(BF16)
+    grad_hidden_b = grad_hidden.astype(BF16)
+    grad_mixed = matmul_nt(out_w_ref[...], grad_hidden_b).astype(BF16)
     for dest, at in enumerate(window_starts):
         grad_mixed_ref[dest] = grad_mixed[at : at + grad_mixed_ref.shape[1]]
-    normed_ref[...] = normed
-    logits_ref[...] = jnp.where(lane == experts, jnp.ones((), BF16), grad_logits)
-    back_ref[...] = (grad_normed * unit).astype(BF16)
+    cut = first_refs[0].shape[2]
+    grad_out_w = matmul(mixed_ref[...], grad_hidden_b)
+    put_halves(grad_out_w[:, :cut], info_ref[4], *first_refs)
+    ones = jnp.where(lane == experts, 1.0, 0.0).astype(BF16)
+    small_grad = matmul_tn(normed, grad_logits) + matmul_tn((grad_normed * unit).astype(BF16), ones)
+    last = jnp.concatenate([grad_out_w[:, cut:], small_grad, shared_ref[...].astype(F32)], axis=1)
+    put_halves(last, info_ref[5], last_keep_ref, last_send_ref)
 
 
 def own_rows(
-    info, grad_own, mixed, tokens, cotangent, packed, branch, earlier, experts, groups,
-    window, window_starts,
+    info, grad_own, mixed, tokens, cotangent, packed, grad_shared, earlier, experts, groups, window,
+    window_starts,
 ):
     rows, width = tokens.shape
     small_at = packed.shape[1] // 128 - 1
@@ -493,46 +586,207 @@
     def whole(shape):
         return pl.BlockSpec(shape, lambda i, _: (0,) * len(shape))
 
-    anywhere = pl.BlockSpec(memory_space=pl.ANY)
     shapes = (
         ((rows, width), F32),
         ((rows, width), F32),
         ((groups, window, rows), BF16),
-        ((rows, width), BF16),
-        ((rows, 128), BF16),
-        ((rows, width), BF16),
-        (MARK, F32),
+        *(((groups, width // groups // 2, width - 128), BF16),) * 2,
+        *(((groups, width // groups // 2, 256 + grad_shared.shape[1]), BF16),) * 2,
     )
     return pl.pallas_call(
         functools.partial(
             own_rows_kernel, experts=experts, groups=groups, window_starts=tuple(window_starts)
         ),
-        out_shape=(
-            *(jax.ShapeDtypeStruct(shape, dtype) for shape, dtype in shapes),
-            jax.ShapeDtypeStruct(branch.shape, branch.dtype),
-        ),
+        out_shape=tuple(jax.ShapeDtypeStruct(shape, dtype) for shape, dtype in shapes),
         grid_spec=pltpu.PrefetchScalarGridSpec(
             num_scalar_prefetch=1,
             grid=(1,),
             in_specs=[
                 whole(grad_own.shape),
-                pl.BlockSpec((width, rows), lambda i, info: (0, info[1])),
+                whole(mixed.shape),
                 whole(tokens.shape),
                 whole(cotangent.shape),
                 whole((width, width)),
                 pl.BlockSpec((width, 128), lambda i, _: (0, small_at)),
-                anywhere,
+                whole(grad_shared.shape),
             ]
-            + [anywhere] * len(earlier),
-            out_specs=(*(whole(shape) for shape, _ in shapes), anywhere),
-        ),
-        input_output_aliases={7: len(shapes)},
-        compiler_params=pltpu.CompilerParams(vmem_limit_bytes=40 << 20),
+            + [IN_HBM] * len(earlier),
+            out_specs=tuple(whole(shape) for shape, _ in shapes),
+        ),
+        compiler_params=pltpu.CompilerParams(vmem_limit_bytes=ALL_VMEM),
         cost_estimate=pl.CostEstimate(
             flops=6 * rows * width * width, bytes_accessed=6 << 20, transcendentals=rows * 128
         ),
         name="own_rows",
-    )(info, grad_own, mixed, tokens, cotangent, packed, packed, branch, *earlier)
+    )(info, grad_own, mixed, tokens, cotangent, packed, packed, grad_shared, *earlier)
+
+
+def passed_after(values, mark):
+    return pl.pallas_call(
+        lambda *_: None,
+        out_shape=jax.ShapeDtypeStruct(values.shape, values.dtype),
+        in_specs=[IN_HBM, IN_HBM],
+        out_specs=IN_HBM,
+        input_output_aliases={0: 0},
+        name="passed_after",
+    )(values, mark)
+
+
+def finish_expert_kernel(mine_ref, *refs):
+    half = pl.program_id(0)
+    refs[4][...] = jnp.concatenate(
+        [
+            jnp.where(
+                mine_ref[part] == half, refs[part][...].astype(F32), refs[2 + part][...].astype(F32)
+            )
+            for part in range(2)
+        ],
+        axis=1,
+    )
+
+
+def finish_expert(mine, own, other):
+    rows, cols = own[0].shape
+    taken = pl.BlockSpec((rows, cols), lambda i, _: (0, 0))
+    return pl.pallas_call(
+        finish_expert_kernel,
+        out_shape=jax.ShapeDtypeStruct((2 * rows, 2 * cols), F32),
+        grid_spec=pltpu.PrefetchScalarGridSpec(
+            num_scalar_prefetch=1,
+            grid=(2,),
+            in_specs=[taken] * 4,
+            out_specs=pl.BlockSpec((rows, 2 * cols), lambda i, _: (i, 0)),
+        ),
+        compiler_params=pltpu.CompilerParams(vmem_limit_bytes=32 << 20),
+        cost_estimate=pl.CostEstimate(flops=0, bytes_accessed=5 << 20, transcendentals=0),
+        name="finish_expert",
+    )(mine, *own, *other)
+
+
+def finish_dense_kernel(
+    mine_ref, first_ref, first_other_ref, last_ref, last_other_ref, gain_ref, wq_ref, wk_ref, wv_ref,
+    *refs
+):
+    *weight_refs, out_ref, gate_ref, up_ref, gain_one_ref, gain_two_ref, router_ref = refs[-9:]
+
+    def pieces(own_ref, other_ref, mine, widths):
+        own, other = (own_ref[...].astype(F32), other_ref[...].astype(F32))
+        whole = jnp.concatenate(
+            [jnp.where(mine == 0, own, other), jnp.where(mine == 0, other, own)], axis=0
+        )
+        at = 0
+        for cols in widths:
+            yield whole[:, at : at + cols]
+            at += cols
+
+    width = out_ref.shape[1]
+    *weights, out = pieces(first_ref, first_other_ref, mine_ref[0], [width] * 3 + [width - 128])
+    out_end, small, gate, up = pieces(
+        last_ref, last_other_ref, mine_ref[1], [128] * 2 + [gate_ref.shape[1]] * 2
+    )
+    gain_grad = jnp.zeros(gain_ref.shape, F32)
+    for total, w_ref, weight_ref in zip(weights, (wq_ref, wk_ref, wv_ref), weight_refs):
+        weight_ref[...] = total * gain_ref[...]
+        gain_grad += jnp.sum(total * w_ref[...].astype(F32), axis=1, keepdims=True)
+    out_ref[...] = jnp.concatenate([out, out_end], axis=1)
+    gate_ref[...], up_ref[...] = (gate, up)
+    lane = lax.broadcasted_iota(jnp.int32, small.shape, 1)
+    experts = router_ref.shape[0]
+    rows = jnp.where(lane == experts + 1, gain_grad, small).T
+    router_ref[...] = rows[:experts]
+    gain_two_ref[...] = rows[experts : experts + 1]
+    gain_one_ref[...] = rows[experts + 1 : experts + 2]
+
+
+def finish_dense(mine, first, first_other, last, last_other, gain, weights, earlier, experts):
+    rows, width = weights[0].shape
+    half = (last.shape[1] - 256) // 2
+    shapes = [(rows, width)] * 4 + [(rows, half)] * 2 + [(1, rows)] * 2 + [(experts, rows)]
+    vmem = pl.BlockSpec(memory_space=pltpu.VMEM)
+    return pl.pallas_call(
+        finish_dense_kernel,
+        out_shape=tuple(jax.ShapeDtypeStruct(shape, F32) for shape in shapes),
+        in_specs=[pl.BlockSpec(memory_space=pltpu.SMEM)] + [vmem] * 8 + [IN_HBM] * len(earlier),
+        out_specs=(vmem,) * len(shapes),
+        compiler_params=pltpu.CompilerParams(vmem_limit_bytes=ALL_VMEM),
+        name="finish_dense",
+    )(mine, first, first_other, last, last_other, gain, *weights, *earlier)
+
+
+def assemble_kernel(back_ref, *refs, offsets, width, window):
+    first_ref, last_ref = refs[-2:]
+    groups = back_ref.shape[0]
+    back = [back_ref[d].astype(F32) for d in range(groups)]
+    cols_dev, first_at = (width // groups, 3 * window)
+    last_at = first_at + width - 128
+    act_at = last_at + 256
+    hidden = (back_ref.shape[2] - act_at) // 2
+    columns = [
+        back[d][:, part * window + offsets[d] : part * window + offsets[d] + cols_dev]
+        for part in range(3)
+        for d in range(groups)
+    ]
+    summed = back[0][:, first_at:act_at]
+    for d in range(1, groups):
+        summed += back[d][:, first_at:act_at]
+    first_ref[...] = jnp.concatenate(columns + [summed[:, : last_at - first_at]], axis=1).astype(
+        BF16
+    )
+    last_ref[...] = jnp.concatenate(
+        [summed[:, last_at - first_at :]]
+        + [
+            back[d][:, act_at + part * hidden : act_at + (part + 1) * hidden]
+            for part in range(2)
+            for d in range(groups)
+        ],
+        axis=1,
+    ).astype(BF16)
+
+
+def assemble(back, offsets, width, hidden, window, earlier):
+    groups, rows, cols = back.shape
+    vmem = pl.BlockSpec(memory_space=pltpu.VMEM)
+    return pl.pallas_call(
+        functools.partial(
+            assemble_kernel, offsets=tuple(offsets), width=width, window=window
+        ),
+        out_shape=(
+            jax.ShapeDtypeStruct((rows, 4 * width - 128), BF16),
+            jax.ShapeDtypeStruct((rows, 256 + 2 * groups * hidden), BF16),
+        ),
+        in_specs=[vmem] + [IN_HBM] * len(earlier),
+        out_specs=(vmem, vmem),
+        compiler_params=pltpu.CompilerParams(vmem_limit_bytes=ALL_VMEM),
+        name="assemble",
+    )(back, *earlier)
+
+
+def finish_rows_kernel(
+    info_ref, hidden_ref, branch_ref, grad_hidden_ref, grad_unit_ref, tokens_ref, out_ref, grad_ref
+):
+    rows = hidden_ref.shape[0]
+    position = info_ref[1] * rows + lax.broadcasted_iota(jnp.int32, (rows, 1), 0)
+    live = (position < info_ref[0]).astype(F32)
+    out_ref[...] = (hidden_ref[...] + live * branch_ref[...].astype(F32)).astype(BF16)
+    inputs = tokens_ref[...].astype(F32)
+    grad_ref[...] = grad_hidden_ref[...] + rms_back(
+        inputs, inv_rms(inputs), grad_unit_ref[...].astype(F32)
+    )
+
+
+def finish_rows(info, hidden, branch, grad_hidden, grad_unit, tokens):
+    vmem = pl.BlockSpec(memory_space=pltpu.VMEM)
+    return pl.pallas_call(
+        finish_rows_kernel,
+        out_shape=(
+            jax.ShapeDtypeStruct(hidden.shape, BF16),
+            jax.ShapeDtypeStruct(hidden.shape, F32),
+        ),
+        in_specs=[pl.BlockSpec(memory_space=pltpu.SMEM)] + [vmem] * 5,
+        out_specs=(vmem, vmem),
+        compiler_params=pltpu.CompilerParams(vmem_limit_bytes=ALL_VMEM),
+        name="finish_rows",
+    )(info, hidden, branch, grad_hidden, grad_unit, tokens)
 
 
 def gather_rows(values):
@@ -548,7 +802,7 @@
 
 
 def after(values, mark):
-    mark = mark[(slice(0, 1),) * mark.ndim].reshape(()).astype(F32)
+    mark = mark[(slice(-1, None),) * mark.ndim].reshape(()).astype(F32)
     return jnp.where(mark < jnp.inf, values, jnp.zeros((), values.dtype))
 
 
@@ -564,30 +818,41 @@
     return range(bits)
 
 
-def rep_scatter_sum(values, axis, bits=None, marks=()):
-    index = lax.axis_index("rep")
-    for step, bit in enumerate(rep_bits() if bits is None else bits):
-        half = values.shape[axis] // 2
-        mine = (index >> bit) & 1
-        keep = lax.dynamic_slice_in_dim(values, mine * half, half, axis)
-        send = lax.dynamic_slice_in_dim(values, (1 - mine) * half, half, axis)
-        if step < len(marks):
-            keep = after(keep, marks[step])
-        values = (keep.astype(F32) + swap_rep(send, bit).astype(F32)).astype(values.dtype)
+def rep_add(keep, send, bit, mark=None):
+    if mark is not None:
+        keep = after(keep, mark)
+    return (keep.astype(F32) + swap_rep(send, bit).astype(F32)).astype(keep.dtype)
+
+
+def rep_step(values, axis, bit, ready=None):
+    half = values.shape[axis] // 2
+    mine = (lax.axis_index("rep") >> bit) & 1
+    keep = lax.dynamic_slice_in_dim(values, mine * half, half, axis)
+    send = lax.dynamic_slice_in_dim(values, (1 - mine) * half, half, axis)
+    if ready is not None:
+        send = after(send, ready)
+    return rep_add(keep, send, bit)
+
+
+def rep_scatter_sum(values, axis, bits):
+    for bit in bits:
+        values = rep_step(values, axis, bit)
     return values
 
 
 def rep_join(values, axis, bits=None):
     index = lax.axis_index("rep")
     for bit in reversed(rep_bits() if bits is None else bits):
-        other = swap_rep(values, bit)
-        mine = (index >> bit) & 1
-        values = jnp.where(
-            mine == 0,
-            jnp.concatenate([values, other], axis=axis),
-            jnp.concatenate([other, values], axis=axis),
-        )
+        values = joined(values, swap_rep(values, bit), (index >> bit) & 1, axis)
     return values
+
+
+def joined(own, other, mine, axis):
+    return jnp.where(
+        mine == 0,
+        jnp.concatenate([own, other], axis=axis),
+        jnp.concatenate([other, own], axis=axis),
+    )
 
 
 def on_device(
@@ -720,7 +985,9 @@
     mixed_own = after(mixed_own, cotangent_all)
     mixed_all = gather_rows(mixed_own)
 
-    info = jnp.stack([length, me, jnp.zeros((), jnp.int32)])
+    orders = (list(rep_bits()), list(rep_bits())[::-1])
+    mine = [(lax.axis_index("rep") >> order[0]) & 1 for order in orders]
+    info = jnp.stack([length, me, jnp.zeros((), jnp.int32), my_offset, *mine])
     (
         branch_part,
         grad_part,
@@ -748,27 +1015,41 @@
     )
     grad_own = scatter_sum(grad_part)
 
-    expert_grads = jnp.concatenate(
-        [
+    half_rows, half_cols = (expert_inner.shape[1] // 2, width // 2)
+
+    def half_grad(part, half):
+        rows_half = lax.dynamic_slice_in_dim(expert_inner, half * half_rows, half_rows, 1)
+        cols_half = grad_half[:, part * half_cols : (part + 1) * half_cols]
+        return matmul_tn(rows_half, cols_half).astype(BF16)
+
+    received = [
+        swap_rep(half_grad(part, 1 - mine[part]), order[0]) for part, order in enumerate(orders)
+    ]
+    expert_parts = [
+        (half_grad(part, mine[part]).astype(F32) + received[part].astype(F32)).astype(BF16)
+        for part in range(2)
+    ]
+    whole_sums = lax.psum(
+        (
             matmul_tn(rows_in, expert_gate_grad).astype(BF16),
             matmul_tn(rows_in, expert_up_grad).astype(BF16),
-            matmul_tn(grad_half, expert_inner).astype(BF16),
-        ],
-        axis=0,
-    )
-    grad_down = matmul_tn(shared_inner, cotangent_all).astype(BF16)
-    grad_gate_up = matmul_tn(normed, shared_act_grad).astype(BF16)
-
-    hidden, grad_hidden, grad_mixed, normed_own, logits_own, back_own, mark_own, branch_part = (
+            matmul_tn(shared_inner, cotangent_all).astype(BF16),
+        ),
+        "rep",
+    )
+    grad_shared = matmul_tn(normed, shared_act_grad).astype(BF16)
+    mixed_rows = lax.dynamic_slice_in_dim(mixed_all, my_rows, rows_dev, 1)
+
+    hidden, grad_hidden, grad_mixed, first_keep, first_send, last_keep, last_send = (
         own_rows(
             info,
             grad_own,
-            mixed_all,
+            mixed_rows,
             tokens[0],
             cotangent[0],
             packed_all,
-            branch_part,
-            (expert_grads, grad_down, grad_gate_up),
+            grad_shared,
+            tuple(expert_parts),
             experts,
             groups,
             window,
@@ -776,25 +1057,13 @@
         )
     )
     grad_mixed_cols = exchange(grad_mixed)
-    branch_own = scatter_sum(branch_part).astype(F32)
-    orders = (list(rep_bits()), list(rep_bits())[::-1])
-    half_rows = expert_grads.shape[0] // 2
+    branch_own = scatter_sum(passed_after(branch_part, grad_mixed_cols))
     expert_parts = [
-        rep_scatter_sum(expert_grads[at : at + half_rows], 0, order, (mark_own,))
-        for at, order in zip((0, half_rows), orders)
+        rep_scatter_sum(
+            rep_step(part, 0, order[1], ready=grad_mixed_cols), 0, order[2:]
+        )
+        for part, order in zip(expert_parts, orders)
     ]
-    packed_grad = jnp.concatenate(
-        [
-            matmul(
-                lax.dynamic_slice_in_dim(mixed_all, my_rows, rows_dev, 1),
-                grad_hidden.astype(BF16),
-            ),
-            matmul_tn(normed_own, logits_own[:, :experts]),
-            matmul_tn(back_own, logits_own[:, experts : experts + 1]),
-        ],
-        axis=1,
-    ).astype(BF16)
-
     grad_q, grad_k, grad_v, mark_attn = attn_backward(
         lengths,
         queries,
@@ -803,84 +1072,62 @@
         mixed_heads,
         log_norm,
         grad_mixed_cols,
-        tuple(expert_parts),
-    )
-    grad_down = rep_scatter_sum(grad_down, 0, orders[1], (mark_attn,))
-    grad_gate_up = rep_scatter_sum(
-        grad_gate_up.reshape(groups, cols_dev, -1), 1, orders[1], (mark_attn,)
-    )
-    gate_up_back = exchange(grad_gate_up)
-    gate_up_part = jnp.concatenate(
-        [
-            gate_up_back[:, :, at : at + shared_cols_dev]
-            .transpose(1, 0, 2)
-            .reshape(rep_rows, -1)
-            for at in (0, shared_cols_dev)
-        ],
-        axis=1,
-    )
-    packed_part = rep_scatter_sum(
-        packed_grad.reshape(groups, cols_dev, -1), 1, orders[0], (mark_attn,)
-    )
-    packed_part = jnp.sum(exchange(packed_part).astype(F32), axis=0).astype(BF16)
-    channel = jnp.arange(window, dtype=jnp.int32)[:, None]
-    owned = (channel >= my_offset) & (channel < my_offset + cols_dev)
-    qkv_grad = jnp.concatenate(
-        [
-            jnp.where(owned, rotate_cols(grad_q * 0.125, cosine, -sine), 0.0),
-            jnp.where(owned, rotate_cols(grad_k, cosine, -sine), 0.0),
-            jnp.where(owned, grad_v, 0.0),
-        ],
-        axis=0,
-    ).astype(BF16)
-    grad_unit = scatter_sum(contract(qkv_grad, qkv_cols, 0, 1).astype(BF16)).astype(F32)
-    expert_sum = jnp.concatenate(
-        [rep_join(part, 0, order) for part, order in zip(expert_parts, orders)], axis=0
-    )
-    expert_sum = expert_sum.astype(F32)
-    sum_egate, sum_eup, sum_edown = (
-        expert_sum[:width],
-        expert_sum[width : 2 * width],
-        expert_sum[2 * width :].T,
-    )
-    sum_down = rep_join(grad_down, 0, orders[1]).astype(F32)
-    inputs = tokens[0].astype(F32)
-    output = (hidden + live_col * branch_own).astype(BF16)
-    input_grad = grad_hidden + rms_back(inputs, inv_rms(inputs), grad_unit)
-
-    qkv_weight_grad = contract(unit, qkv_grad, 0, 1).astype(BF16)
-    qkv_part = rep_scatter_sum(qkv_weight_grad.reshape(groups, cols_dev, 3 * window), 1)
-    qkv_back = exchange(qkv_part)
-    qkv_part = jnp.concatenate(
-        [
-            qkv_back[d, :, part * window + offsets[d] : part * window + offsets[d] + cols_dev]
-            for part in range(3)
-            for d in range(groups)
-        ],
-        axis=1,
-    )
-    sum_qkv = rep_join(qkv_part, 0).astype(F32)
-    sum_gate_up = rep_join(gate_up_part, 0, orders[1]).astype(F32)
-    sum_packed = rep_join(packed_part, 0).astype(F32)
-
-    sum_gain_attn = sum(
-        jnp.sum(sum_qkv[:, part * width : (part + 1) * width] * weight.astype(F32), axis=1)
-        for part, weight in enumerate((w_query, w_key, w_value))
-    )
-    sum_weights = sum_qkv * gain_attn.astype(F32)[:, None]
-    half = sum_gate_up.shape[1] // 2
+        (),
+    )
+    dense_first = rep_add(first_keep, first_send, orders[0][0], mark_attn)
+    dense_last = rep_add(last_keep, last_send, orders[1][0], mark_attn)
+    grad_unit_part, qkv_keep, qkv_send = projections_backward(
+        info,
+        grad_q,
+        grad_k,
+        grad_v,
+        cosine,
+        sine,
+        unit,
+        qkv_cols,
+        cols_dev,
+        (dense_first, dense_last),
+    )
+    qkv_part = rep_add(qkv_keep, qkv_send, orders[0][0], expert_parts[1])
+    dense_first = rep_scatter_sum(dense_first, 1, orders[0][1:])
+    dense_last = rep_scatter_sum(dense_last, 1, orders[1][1:])
+    grad_unit = scatter_sum(grad_unit_part)
+    output, input_grad = finish_rows(info, hidden, branch_own, grad_hidden, grad_unit, tokens[0])
+
+    expert_own = [
+        rep_join(after(part, qkv_part), 0, order[1:]) for part, order in zip(expert_parts, orders)
+    ]
+    expert_other = [swap_rep(part, order[0]) for part, order in zip(expert_own, orders)]
+    sum_edown = finish_expert(jnp.stack(mine), expert_own, expert_other)
+    qkv_part = rep_scatter_sum(qkv_part, 1, orders[0][1:])
+    back = exchange(jnp.concatenate([qkv_part, dense_first, dense_last], axis=2))
+    sum_egate, sum_eup, sum_down = [after(total, back).astype(F32) for total in whole_sums]
+    first_part, last_part = assemble(back, offsets, width, shared_cols_dev, window, (sum_edown,))
+    first_part = rep_join(first_part, 0, orders[0][1:])
+    last_part = rep_join(last_part, 0, orders[1][1:])
+    first_other = swap_rep(first_part, orders[0][0])
+    last_other = swap_rep(last_part, orders[1][0])
+    *sums_qkv, sum_out, sum_gate, sum_up, sum_gain_attn, sum_gain_ffn, sum_router = finish_dense(
+        jnp.stack(mine),
+        first_part,
+        first_other,
+        last_part,
+        last_other,
+        gain_attn.astype(F32)[:, None],
+        (w_query, w_key, w_value),
+        (sum_egate, sum_edown),
+        experts,
+    )
     return (
         output[None],
         input_grad[None],
-        sum_gain_attn,
-        sum_packed[:, width + experts],
-        sum_weights[:, :width],
-        sum_weights[:, width : 2 * width],
-        sum_weights[:, 2 * width :],
-        sum_packed[:, :width],
-        sum_packed[:, width : width + experts],
-        sum_gate_up[:, :half],
-        sum_gate_up[:, half:],
+        sum_gain_attn[0],
+        sum_gain_ffn[0],
+        *sums_qkv,
+        sum_out,
+        sum_router.T,
+        sum_gate,
+        sum_up,
         sum_down,
         sum_egate,
         sum_eup,

time: 429 us -> 380 us (0.89)
  other arithmetic: 62.1 us -> 24.4 us
  local copies, waits for them, and re-layouts: 48.1 us -> 28.6 us
  Pallas kernels: 70.8 us -> 90.1 us
  starting transfers between devices: 47.6 us -> 37.3 us
    ppermute x24 -> x18, waiting for transfers between devices: 33 us -> 51.4 us  [swap_rep(): lax.ppermute(values, 'rep', [(i, i ^ 1 << bit) for i in range(count)])]
    pallas_call x0 -> x6, Pallas kernels: none -> 16.8 us  [the longest x1 6.19 us: projections_backward(): pl.pallas_call(functools.partial(projections_kernel, cols_dev=cols_dev),...]
    unnamed x140 -> x108, local copies, waits for them, and re-layouts: 24.5 us -> 10.5 us
    select_n x8 -> x4, other arithmetic: 12 us -> 0.39 us  [joined(): jnp.where(mine == 0, jnp.concatenate([own, other], axis=axis), jnp.concat...]
    convert_element_type x18 -> x11, other arithmetic: 20.7 us -> 10 us  [the longest x3 6.25 us: on_device(): after(total, back).astype(F32)]
    reduce_scatter x3, waiting for transfers between devices: 15.9 us -> 5.97 us  [scatter_sum(): return lax.psum_scatter(values, 'fsdp', scatter_dimension=0, tiled=True)]
    all_to_all x5 -> x3, starting transfers between devices: 21 us -> 12.4 us  [exchange(): lax.all_to_all(chunks, 'fsdp', split_axis=0, concat_axis=0, tiled=True)]
    concatenate x3 -> x1, other arithmetic: 8.43 us -> 0.9 us  [on_device(): jnp.concatenate([qkv_part, dense_first, dense_last], axis=2)]
  transfers between devices with their start and end apart: 36 -> 29, of which waited for: 12 -> 20; matrix products, arithmetic and copies ran while one was open for 26% -> 17% of each run, Pallas kernels for 8% -> 14%
where the time goes in v3:
time: 380 us; the launch traced here: 373 us
  waiting for transfers between devices  123 us (32%)
  Pallas kernels  90.1 us (24%)
  starting transfers between devices  37.3 us (10%)
  local copies, waits for them, and re-layouts  28.6 us (8%)
  other arithmetic  24.4 us (6%)
  between operations  24.1 us (6%)
  blocking collectives  23.5 us (6%)
  matrix products  22 us (6%)
    ppermute x18, waiting for transfers between devices, swap_rep(): lax.ppermute(values, 'rep', [(i, i ^ 1 << bit) for i in range(count)])  51.4 us
    pallas_call x1, Pallas kernels, run_branches(): pl.pallas_call(functools.partial(branch_kernel, experts=experts, groups=g...  36.7 us
    all_to_all x3, waiting for transfers between devices, exchange(): lax.all_to_all(chunks, 'fsdp', split_axis=0, concat_axis=0, tiled=True)  24.6 us
    psum x1, waiting for transfers between devices, on_device(): lax.psum(lax.dynamic_update_slice_in_dim(jnp.zeros((groups, cols_dev, sma...  24 us
    ppermute x18, starting transfers between devices, swap_rep(): lax.ppermute(values, 'rep', [(i, i ^ 1 << bit) for i in range(count)])  23.9 us
    dot_general x9, matrix products, contract(): lax.dot_general(first_op, second_op, (((first_dim,), (second_dim,)), ((),...  22 us
    pallas_call x1, Pallas kernels, attn_backward(): pl.pallas_call(functools.partial(attn_backward_kernel, heads=heads, blk=b...  17.6 us
    all_gather x3, waiting for transfers between devices, gather_rows(): return lax.all_gather(values, 'fsdp', axis=0, tiled=True)  15.5 us
  transfers between devices with their start and end apart: 29, of which 20 were waited for; matrix products, arithmetic and copies ran while one was open for 17% of the time, Pallas kernels for 14%

profile of v3, /device:TPU:0, one launch (start us, length us, event | category | flops | bytes accessed | tf_op | source)
XLA Modules:
  0.0 372.8 jit_solution(12291730481416733614)
XLA Ops:
  10.8 13.2 %all_to_all.20 = bf16[8,24,384]{2,1,0:T(8,128)(2,1)S(1)} all-to-all(bf16[8,24,384]{2,1,0:T(8,128)(2,1)S(1)} %fusion.43), channel_id=1, replica_groups=mesh['rep'=4,'fsdp'=8] {'fsdp'}, dimensions={0} | all-to-all | bytes 294912 | tf_op jit(solution)/shard_map/all_to_all | solution.py:797
  24.0 10.3 %all-gather = bf16[32,24,384]{2,1,0:T(8,128)(2,1)S(1)} all-gather(bf16[8,24,384]{2,1,0:T(8,128)(2,1)S(1)} %all_to_all.20), channel_id=2, replica_groups=mesh['rep'=4,'fsdp'=8] {'rep'}, dimensions={0}, use_global_device_ids=true | all-gather | bytes 737280 | tf_op jit(solution)/shard_map/all_gather | solution.py:917
  40.2 3.5 all-to-all-start.1
  47.1 1.8 fusion.34
  48.8 12.7 %all-to-all-done.1 = bf16[8,24,1408]{2,1,0:T(8,128)(2,1)S(1)} async-done(((bf16[8,24,1408]{2,1,0:T(8,128)(2,1)}), bf16[8,24,1408]{2,1,0:T(8,128)(2,1)S(1)}, u32[]{:S(2)}, u32[]{:S(2)}) %all-to-all-start.1) | async-done | bytes 540704 | tf_op jit(solution)/shard_map/all_to_all | solution.py:797
  61.8 1.3 copy-done.26
  63.3 2.9 fusion
  67.6 1.4 fusion.62
  71.4 12.0 %attn_forward.1 = (f32[128,2048]{1,0:T(8,128)S(1)}, f32[2,2048]{1,0:T(2,128)S(1)}) custom-call(s32[1]{0:T(128)} %copy.78.len_ref, bf16[128,2048]{1,0:T(8,128)(2,1)S(1)} %bitcast.99, bf16[128,2048]{1,0:T(8,128)(2,1)S(1)} %bitcast.97, bf16[128,2048]{1,0:T(8,128)(2,1)S(1)} %slice.248.v_ref), custom_call_target="tpu_custom_call" | custom-call | flops 4294967296 | bytes 4194304 | tf_op jit(solution)/shard_map/attn_forward/pallas_call | solution.py:207
  85.2 10.8 %all-gather.6.cloned.1.call-done.cotangent_ref = bf16[2048,768]{1,0:T(8,128)(2,1)} async-done(((bf16[256,768]{1,0:T(8,128)(2,1)}), bf16[2048,768]{1,0:T(8,128)(2,1)}) %all-gather.6.cloned.1.call-update) | async-done | bytes 3145744 | tf_op jit(solution)/shard_map/all_gather | solution.py:793
  96.0 1.3 slice.210
  97.9 1.9 fusion.32
  100.1 1.3 stack.62.info_ref
  108.5 24.0 %all-reduce.5.cloned.1.call-done.out_w_ref.gate_ref.up_ref.small_ref = bf16[768,1408]{1,0:T(8,128)(2,1)} async-done(((bf16[768,1408]{1,0:T(8,128)(2,1)}), bf16[768,1408]{1,0:T(8,128)(2,1)}) %all-reduce.5.cloned.1.call-update) | async-done | bytes 2162704 | tf_op jit(solution)/shard_map/psum | solution.py:962
  132.4 4.7 %all-gather.8.cloned.1.call-done.mixed_ref = bf16[768,2048]{1,0:T(8,128)(2,1)} async-done(((bf16[96,2048]{1,0:T(8,128)(2,1)}), bf16[768,2048]{1,0:T(8,128)(2,1)}) %all-gather.8.cloned.1.call-update) | async-done | bytes 3145744 | tf_op jit(solution)/shard_map/all_gather | solution.py:793
  137.2 36.7 %branches.1 = (bf16[2048,768]{1,0:T(8,128)(2,1)}, bf16[2048,896]{1,0:T(8,128)(2,1)}, bf16[2048,768]{1,0:T(8,128)(2,1)}, bf16[2048,256]{1,0:T(8,128)(2,1)}, bf16[...) custom-call(s32[6]{0:T(128)} %stack.62.info_ref, ...), custom_call_target="tpu_custom_call" | custom-call | flops 21340618752 | bytes 41943040 | tf_op jit(solution)/shard_map/branches/pallas_call | solution.py:463
  174.2 4.1 %convolution_convert_fusion.3 = bf16[256,768]{1,0:T(8,128)(2,1)} fusion(bf16[2048,256]{1,0:T(8,128)(2,1)} %get-tuple-element.91, bf16[2048,768]{1,0:T(8,128)(2,1)} %all-gather.6.cloned.1.call-done.cotangent_ref), kind=kOutput, calls=%fused_computation.21 | convolution fusion | flops 805502976 | bytes 4587520 | tf_op jit(solution)/shard_map/dot_general | solution.py:24
  178.3 3.4 convolution_convert_fusion
  181.7 3.4 convolution_convert_fusion.1
  185.2 2.7 fusion.19
  187.9 1.5 collective-permute-start.1
  190.3 1.5 collective-permute-start
  191.9 2.7 convolution_convert_fusion.2.shared_ref
  194.6 1.8 constant_dynamic-slice_fusion.3.mixed_ref
  196.3 11.3 %collective-permute-done.1 = bf16[512,384]{1,0:T(8,128)(2,1)S(1)} collective-permute-done((bf16[512,384]{1,0:T(8,128)(2,1)S(1)}, bf16[512,384]{1,0:T(8,128)(2,1)S(1)}, u32[]{:S(2)}, u32[]{:S(2)}) %collective-permute-start.1) | collective-permute-done | bytes 393248 | tf_op jit(solution)/shard_map/ppermute | solution.py:811
  207.6 1.6 add_convert_fusion.2.refs_1_
  210.4 1.6 add_convert_fusion.3.refs_0_
  212.0 5.9 %reduce-scatter.4.cloned.1.call-done.grad_ref = bf16[256,896]{1,0:T(8,128)(2,1)} async-done(((bf16[2048,896]{1,0:T(8,128)(2,1)}), bf16[256,896]{1,0:T(8,128)(2,1)}) %reduce-scatter.4.cloned.1.call-update) | async-done | bytes 458768 | tf_op jit(solution)/shard_map/reduce_scatter | solution.py:801
  218.0 7.1 %own_rows.1 = (f32[256,768]{1,0:T(8,128)}, f32[256,768]{1,0:T(8,128)}, bf16[8,128,256]{2,1,0:T(8,128)(2,1)}, bf16[8,48,640]{2,1,0:T(8,128)(2,1)}, bf16[8,48,640]...) custom-call(s32[6]{0:T(128)} %stack.62.info_ref, ...), custom_call_target="tpu_custom_call" | custom-call | flops 905969664 | bytes 6291456 | tf_op jit(solution)/shard_map/own_rows/pallas_call | solution.py:596
  225.0 4.1 %all-to-all-start.2 = ((bf16[8,128,256]{2,1,0:T(8,128)(2,1)}), bf16[8,128,256]{2,1,0:T(8,128)(2,1)}, u32[]{:S(2)}, u32[]{:S(2)}) async-start(bf16[8,128,256]{2,1,0:T(8,128)(2,1)} %get-tuple-element.62), calls=%async_computation.3 | async-start | bytes 1048576 | tf_op jit(solution)/shard_map/all_to_all | solution.py:797
  229.5 1.7 collective-permute-start.2
  231.1 1.5 collective-permute-start.3
  232.6 11.9 %all-to-all-done.2.__1_.do_ref = bf16[8,128,256]{2,1,0:T(8,128)(2,1)} async-done(((bf16[8,128,256]{2,1,0:T(8,128)(2,1)}), bf16[8,128,256]{2,1,0:T(8,128)(2,1)}, u32[]{:S(2)}, u32[]{:S(2)}) %all-to-all-start.2) | async-done | bytes 524320 | tf_op jit(solution)/shard_map/all_to_all | solution.py:797
  244.5 17.6 %attn_backward.1 = (f32[128,2048]{1,0:T(8,128)}, f32[128,2048]{1,0:T(8,128)}, f32[128,2048]{1,0:T(8,128)}, f32[8,128]{1,0:T(8,128)}) custom-call(s32[1]{0:T(128)} %copy.78.len_ref, bf16[128,2048]{1,0:T(8,128)(2,1)} %bitcast.100, bf16[128,2048]{1,0:T(8,128)(2,1)} %bitcast.98, bf16[128,2048]{1,0:T(8,128)(2,1)} %copy-done.11, f32[128,2048]{1,0:T(8,128)} %copy-done.14, ...), custom_call_target="tpu_custom_call" | custom-call | tf_op jit(solution)/shard_map/attn_backward/pallas_call | solution.py:231
  262.2 1.4 slice.180
  264.3 1.2 add_convert_fusion.1.refs_0_
  265.5 1.7 add_convert_fusion.refs_1_
  267.2 1.6 copy-done.17
  268.8 6.2 %projections_backward.1 = (bf16[2048,768]{1,0:T(8,128)(2,1)}, bf16[8,48,384]{2,1,0:T(8,128)(2,1)S(1)}, bf16[8,48,384]{2,1,0:T(8,128)(2,1)S(1)}) custom-call(s32[6]{0:T(128)S(1)} %copy-done.21, f32[128,2048]{1,0:T(8,128)S(1)} %copy-done.15, f32[128,2048]{1,0:T(8,128)S(1)} %copy-done.16, f32[128,2048]{1,0:T(8,128)S(1)} %copy-done.17, ...), custom_call_target="tpu_custom_call" | custom-call | tf_op jit(solution)/shard_map/projections_backward/pallas_call | solution.py:304
  277.1 1.3 slice.221
  279.1 3.3 collective-permute-start.4
  282.5 1.9 collective-permute-start.7
  284.7 7.7 %collective-permute-done.4 = bf16[256,384]{1,0:T(8,128)(2,1)S(1)} collective-permute-done((bf16[256,384]{1,0:T(8,128)(2,1)S(1)}, bf16[256,384]{1,0:T(8,128)(2,1)S(1)}, u32[]{:S(2)}, u32[]{:S(2)}) %collective-permute-start.4) | collective-permute-done | bytes 196640 | tf_op jit(solution)/shard_map/ppermute | solution.py:811
  293.6 1.1 collective-permute-done.7
  294.9 5.3 %collective-permute-done.5 = bf16[8,48,384]{2,1,0:T(8,128)(2,1)S(1)} collective-permute-done((bf16[8,48,384]{2,1,0:T(8,128)(2,1)S(1)}, bf16[8,48,384]{2,1,0:T(8,128)(2,1)S(1)}, u32[]{:S(2)}, u32[]{:S(2)}) %collective-permute-start.5) | collective-permute-done | bytes 294944 | tf_op jit(solution)/shard_map/ppermute | solution.py:811
  300.3 1.6 collective-permute-start.6
  302.0 4.1 %collective-permute-done.8 = bf16[8,24,768]{2,1,0:T(8,128)(2,1)S(1)} collective-permute-done((bf16[8,24,768]{2,1,0:T(8,128)(2,1)S(1)}, bf16[8,24,768]{2,1,0:T(8,128)(2,1)S(1)}, u32[]{:S(2)}, u32[]{:S(2)}) %collective-permute-start.8) | collective-permute-done | bytes 294944 | tf_op jit(solution)/shard_map/ppermute | solution.py:811
  307.2 4.7 %all-to-all-start.3 = ((bf16[8,24,1792]{2,1,0:T(8,128)(2,1)}), bf16[8,24,1792]{2,1,0:T(8,128)(2,1)S(1)}, u32[]{:S(2)}, u32[]{:S(2)}) async-start(bf16[8,24,1792]{2,1,0:T(8,128)(2,1)} %pad_maximum_fusion), calls=%async_computation.6 | async-start | bytes 1376256 | tf_op jit(solution)/shard_map/all_to_all | solution.py:797
  312.0 1.5 collective-permute-start.9
  315.4 3.9 %collective-permute-done.9 = bf16[256,384]{1,0:T(8,128)(2,1)S(1)} collective-permute-done((bf16[256,384]{1,0:T(8,128)(2,1)S(1)}, bf16[256,384]{1,0:T(8,128)(2,1)S(1)}, u32[]{:S(2)}, u32[]{:S(2)}) %collective-permute-start.9) | collective-permute-done | bytes 196640 | tf_op jit(solution)/shard_map/ppermute | solution.py:811
  319.4 1.5 collective-permute-start.10
  322.6 4.7 %collective-permute-done.10 = bf16[256,384]{1,0:T(8,128)(2,1)S(1)} collective-permute-done((bf16[256,384]{1,0:T(8,128)(2,1)S(1)}, bf16[256,384]{1,0:T(8,128)(2,1)S(1)}, u32[]{:S(2)}, u32[]{:S(2)}) %collective-permute-start.10) | collective-permute-done | bytes 196640 | tf_op jit(solution)/shard_map/ppermute | solution.py:811
  328.9 5.6 %collective-permute-done.13.refs_3_ = bf16[512,384]{1,0:T(8,128)(2,1)S(1)} collective-permute-done((bf16[512,384]{1,0:T(8,128)(2,1)S(1)}, bf16[512,384]{1,0:T(8,128)(2,1)S(1)}, u32[]{:S(2)}, u32[]{:S(2)}) %collective-permute-start.13) | collective-permute-done | bytes 393248 | tf_op jit(solution)/shard_map/ppermute | solution.py:811
  334.4 1.6 collective-permute-done.12.refs_2_
  336.1 2.4 finish_expert.1.refs_0_.refs_1_
  339.8 1.9 assemble.1
  342.2 1.5 collective-permute-start.14
  343.7 3.4 select_convert_fusion
  347.6 1.9 collective-permute-start.15
  349.6 1.7 collective-permute-start.17
  351.3 1.9 select_convert_fusion.1.refs_0_
  354.3 3.5 collective-permute-done.17.last_other_ref
  358.5 3.3 finish_dense.1
  361.9 3.0 finish_rows.1
  (228 shorter events, 36.8 us)
Async XLA Ops:
  8.0 31.2 %copy-start = (bf16[96,768]{1,0:T(8,128)(2,1)S(1)}, bf16[96,768]{1,0:T(8,128)(2,1)}, u32[]{:S(2)}) copy-start(bf16[96,768]{1,0:T(8,128)(2,1)} %param.27) | copy-start | bytes 442372
  8.0 28.4 %copy-start.33 = (bf16[1,256,768]{2,1,0:T(8,128)(2,1)S(1)}, bf16[1,256,768]{2,1,0:T(8,128)(2,1)}, u32[]{:S(2)}) copy-start(bf16[1,256,768]{2,1,0:T(8,128)(2,1)} %param.19) | copy-start | bytes 1179652
  8.0 55.2 %all-gather.10.cloned.1.call-start = ((), (), s32[]{:S(2)}) async-start(), calls=%async_computation.13 | async-start | bytes 3538944 | tf_op jit(solution)/shard_map/all_gather | solution.py:793
  8.8 28.5 %copy-start.44 = (bf16[96,4]{0,1:T(4,128)(2,1)S(1)}, bf16[96,4]{0,1:T(4,128)(2,1)}, u32[]{:S(2)}) copy-start(bf16[96,4]{0,1:T(4,128)(2,1)} %param.28) | copy-start | bytes 2308
  8.8 28.7 %copy-start.45 = (bf16[96]{0:T(256)(128)(2,1)S(1)}, bf16[96]{0:T(256)(128)(2,1)}, u32[]{:S(2)}) copy-start(bf16[96]{0:T(256)(128)(2,1)} %param.23) | copy-start | bytes 580
  8.8 28.8 %copy-start.43 = (s32[1,256,2]{1,2,0:T(2,128)S(1)}, s32[1,256,2]{1,2,0:T(2,128)}, u32[]{:S(2)}) copy-start(s32[1,256,2]{1,2,0:T(2,128)} %param.21) | copy-start | bytes 6148
  8.8 87.2 %all-gather.6.cloned.1.call-start = ((), (), s32[]{:S(2)}) async-start(), calls=%async_computation.7 | async-start | bytes 3538944 | tf_op jit(solution)/shard_map/all_gather | solution.py:793
  37.2 7.3 %copy-start.47 = (s32[8]{0:T(128)S(1)}, s32[8]{0:T(128)}, u32[]{:S(2)}) copy-start(s32[8]{0:T(128)} %constant.88.clone) | copy-start | bytes 100
  40.2 21.3 %all-to-all-start.1 = ((bf16[8,24,1408]{2,1,0:T(8,128)(2,1)}), bf16[8,24,1408]{2,1,0:T(8,128)(2,1)S(1)}, u32[]{:S(2)}, u32[]{:S(2)}) async-start(bf16[8,24,1408]{2,1,0:T(8,128)(2,1)} %maximum_select_fusion), calls=%async_computation.1 | async-start | bytes 1081344 | tf_op jit(solution)/shard_map/all_to_all | solution.py:797
  43.8 88.6 %all-reduce.5.cloned.1.call-start = ((), (), s32[]{:S(2)}) async-start(), calls=%async_computation.9 | async-start | bytes 4325376 | tf_op jit(solution)/shard_map/psum | solution.py:962
  63.2 74.0 %all-gather.8.cloned.1.call-start = ((), (), s32[]{:S(2)}) async-start(), calls=%async_computation.8 | async-start | bytes 3538944 | tf_op jit(solution)/shard_map/all_gather | solution.py:793
  85.2 88.7 %copy-start.20 = (f32[2,2048]{1,0:T(2,128)}, f32[2,2048]{1,0:T(2,128)S(1)}, u32[]{:S(2)}) copy-start(f32[2,2048]{1,0:T(2,128)S(1)} %get-tuple-element.64.l_ref) | copy-start | bytes 49156
  99.9 118.1 %reduce-scatter.4.cloned.1.call-start = ((), (), s32[]{:S(2)}) async-start(), calls=%async_computation.10 | async-start | bytes 4128768 | tf_op jit(solution)/shard_map/reduce_scatter | solution.py:801
  173.9 169.8 %all-reduce.7.cloned.1.call-start = ((), (), s32[]{:S(2)}) async-start(), calls=%async_computation.14 | async-start | bytes 7077888 | tf_op jit(solution)/shard_map/psum | solution.py:1032
  174.2 4.1 %copy-start.49 = (bf16[1280,1024]{1,0:T(8,128)(2,1)S(1)}, bf16[1280,1024]{1,0:T(8,128)(2,1)}, u32[]{:S(2)}) copy-start(bf16[1280,1024]{1,0:T(8,128)(2,1)} %get-tuple-element.92) | copy-start | bytes 7864324
  174.2 4.1 %copy-start.50 = (bf16[1280,768]{1,0:T(8,128)(2,1)S(1)}, bf16[1280,768]{1,0:T(8,128)(2,1)}, u32[]{:S(2)}) copy-start(bf16[1280,768]{1,0:T(8,128)(2,1)} %get-tuple-element.80) | copy-start | bytes 5898244
  185.2 4.2 %copy-start.51 = (bf16[1280,1024]{1,0:T(8,128)(2,1)S(1)}, bf16[1280,1024]{1,0:T(8,128)(2,1)}, u32[]{:S(2)}) copy-start(bf16[1280,1024]{1,0:T(8,128)(2,1)} %get-tuple-element.58) | copy-start | bytes 7864324
  185.2 4.2 %copy-start.52 = (bf16[1280,768]{1,0:T(8,128)(2,1)S(1)}, bf16[1280,768]{1,0:T(8,128)(2,1)}, u32[]{:S(2)}) copy-start(bf16[1280,768]{1,0:T(8,128)(2,1)} %get-tuple-element.59) | copy-start | bytes 5898244
  187.9 4.0 %copy-start.27 = (bf16[2048,768]{1,0:T(8,128)(2,1)S(1)}, bf16[2048,768]{1,0:T(8,128)(2,1)}, u32[]{:S(2)}) copy-start(bf16[2048,768]{1,0:T(8,128)(2,1)} %get-tuple-element.56) | copy-start | bytes 9437188
  187.9 4.0 %copy-start.30 = (bf16[2048,512]{1,0:T(8,128)(2,1)S(1)}, bf16[2048,512]{1,0:T(8,128)(2,1)}, u32[]{:S(2)}) copy-start(bf16[2048,512]{1,0:T(8,128)(2,1)} %get-tuple-element.57) | copy-start | bytes 6291460
  187.9 19.7 %collective-permute-start.1 = (bf16[512,384]{1,0:T(8,128)(2,1)S(1)}, bf16[512,384]{1,0:T(8,128)(2,1)S(1)}, u32[]{:S(2)}, u32[]{:S(2)}) collective-permute-start(bf16[512,384]{1,0:T(8,128)(2,1)S(1)} %fusion.19), channel_id=1, source_target_pairs={{0,16},{8,24},{16,0},{24,8},{1,17},{9,25},{17,1},{25,9},{2,18},{10... | collective-permute-start | bytes 1179656 | tf_op jit(solution)/shard_map/ppermute | solution.py:811
  190.3 20.0 %collective-permute-start = (bf16[512,384]{1,0:T(8,128)(2,1)S(1)}, bf16[512,384]{1,0:T(8,128)(2,1)S(1)}, u32[]{:S(2)}, u32[]{:S(2)}) collective-permute-start(bf16[512,384]{1,0:T(8,128)(2,1)S(1)} %fusion.13), channel_id=1, source_target_pairs={{0,8},{8,0},{16,24},{24,16},{1,9},{9,1},{17,25},{25,17},{2,10},{10... | collective-permute-start | bytes 1179656 | tf_op jit(solution)/shard_map/ppermute | solution.py:811
  225.0 19.5 %all-to-all-start.2 = ((bf16[8,128,256]{2,1,0:T(8,128)(2,1)}), bf16[8,128,256]{2,1,0:T(8,128)(2,1)}, u32[]{:S(2)}, u32[]{:S(2)}) async-start(bf16[8,128,256]{2,1,0:T(8,128)(2,1)} %get-tuple-element.62), calls=%async_computation.3 | async-start | bytes 1048576 | tf_op jit(solution)/shard_map/all_to_all | solution.py:797
  229.2 132.6 %reduce-scatter.8.cloned.1.call-start = ((), (), s32[]{:S(2)}) async-start(), calls=%async_computation.12 | async-start | bytes 3538944 | tf_op jit(solution)/shard_map/reduce_scatter | solution.py:801
  229.5 34.8 %collective-permute-start.2 = (bf16[8,48,640]{2,1,0:T(8,128)(2,1)}, bf16[8,48,640]{2,1,0:T(8,128)(2,1)}, u32[]{:S(2)}, u32[]{:S(2)}) collective-permute-start(bf16[8,48,640]{2,1,0:T(8,128)(2,1)} %get-tuple-element.70), channel_id=1, source_target_pairs={{0,8},{8,0},{16,24},{24,16},{1,9},{9,1},{17,25},{25,17},{2,10},{10... | collective-permute-start | bytes 1474568 | tf_op jit(solution)/shard_map/ppermute | solution.py:811
  231.1 34.4 %collective-permute-start.3 = (bf16[8,48,768]{2,1,0:T(8,128)(2,1)}, bf16[8,48,768]{2,1,0:T(8,128)(2,1)}, u32[]{:S(2)}, u32[]{:S(2)}) collective-permute-start(bf16[8,48,768]{2,1,0:T(8,128)(2,1)} %get-tuple-element.72), channel_id=1, source_target_pairs={{0,16},{8,24},{16,0},{24,8},{1,17},{9,25},{17,1},{25,9},{2,18},{10... | collective-permute-start | bytes 1769480 | tf_op jit(solution)/shard_map/ppermute | solution.py:811
  244.5 19.8 %copy-start.37 = (bf16[8,48,640]{2,1,0:T(8,128)(2,1)S(1)}, bf16[8,48,640]{2,1,0:T(8,128)(2,1)}, u32[]{:S(2)}) copy-start(bf16[8,48,640]{2,1,0:T(8,128)(2,1)} %get-tuple-element.69) | copy-start | bytes 1474564
  262.2 5.0 %copy-start.7 = (f32[32,2048]{1,0:T(8,128)S(1)}, f32[32,2048]{1,0:T(8,128)}, u32[]{:S(2)}) copy-start(f32[32,2048]{1,0:T(8,128)} %get-tuple-element.129.sin_ref) | copy-start | bytes 786436
  262.2 5.0 %copy-start.10 = (bf16[4,8,24,384]{3,2,0,1:T(8,128)(2,1)S(1)}, bf16[4,8,24,384]{3,2,0,1:T(8,128)(2,1)}, u32[]{:S(2)}) copy-start(bf16[4,8,24,384]{3,2,0,1:T(8,128)(2,1)} %copy-done.8) | copy-start | bytes 1769476
  262.2 5.0 %copy-start.15 = (f32[128,2048]{1,0:T(8,128)S(1)}, f32[128,2048]{1,0:T(8,128)}, u32[]{:S(2)}) copy-start(f32[128,2048]{1,0:T(8,128)} %get-tuple-element.65.dq_ref) | copy-start | bytes 3145732
  262.2 5.0 %copy-start.16 = (f32[128,2048]{1,0:T(8,128)S(1)}, f32[128,2048]{1,0:T(8,128)}, u32[]{:S(2)}) copy-start(f32[128,2048]{1,0:T(8,128)} %get-tuple-element.66.dk_ref) | copy-start | bytes 3145732
  262.2 5.0 %copy-start.21 = (s32[6]{0:T(128)S(1)}, s32[6]{0:T(128)}, u32[]{:S(2)}) copy-start(s32[6]{0:T(128)} %stack.62.info_ref) | copy-start | bytes 76
  265.5 9.5 %copy-start.4 = (bf16[8,48,640]{2,1,0:T(8,128)(2,1)}, bf16[8,48,640]{2,1,0:T(8,128)(2,1)S(1)}, u32[]{:S(2)}) copy-start(bf16[8,48,640]{2,1,0:T(8,128)(2,1)S(1)} %add_convert_fusion.1.refs_0_) | copy-start | bytes 1474564
  267.2 7.9 %copy-start.2 = (bf16[8,48,768]{2,1,0:T(8,128)(2,1)}, bf16[8,48,768]{2,1,0:T(8,128)(2,1)S(1)}, u32[]{:S(2)}) copy-start(bf16[8,48,768]{2,1,0:T(8,128)(2,1)S(1)} %add_convert_fusion.refs_1_) | copy-start | bytes 1769476
  276.5 85.4 %reduce-scatter.6.cloned.1.call-start = ((), (), s32[]{:S(2)}) async-start(), calls=%async_computation.11 | async-start | bytes 3538944 | tf_op jit(solution)/shard_map/reduce_scatter | solution.py:801
  276.5 5.9 %copy-start.24 = (bf16[8,48,384]{2,1,0:T(8,128)(2,1)S(1)}, bf16[8,48,384]{2,1,0:T(8,128)(2,1)}, u32[]{:S(2)}) copy-start(bf16[8,48,384]{2,1,0:T(8,128)(2,1)} %copy-done.23) | copy-start | bytes 884740
  276.6 5.9 %copy-start.5 = (bf16[8,48,640]{2,1,0:T(8,128)(2,1)S(1)}, bf16[8,48,640]{2,1,0:T(8,128)(2,1)}, u32[]{:S(2)}) copy-start(bf16[8,48,640]{2,1,0:T(8,128)(2,1)} %copy-done.4) | copy-start | bytes 1474564
  276.6 7.8 %copy-start.3 = (bf16[8,48,768]{2,1,0:T(8,128)(2,1)S(1)}, bf16[8,48,768]{2,1,0:T(8,128)(2,1)}, u32[]{:S(2)}) copy-start(bf16[8,48,768]{2,1,0:T(8,128)(2,1)} %copy-done.2) | copy-start | bytes 1769476
  277.1 23.1 %copy-start.19 = (bf16[8,48,384]{2,1,0:T(8,128)(2,1)S(1)}, bf16[8,48,384]{2,1,0:T(8,128)(2,1)}, u32[]{:S(2)}) copy-start(bf16[8,48,384]{2,1,0:T(8,128)(2,1)} %copy-done.18) | copy-start | bytes 884740
  279.1 13.2 %collective-permute-start.4 = (bf16[256,384]{1,0:T(8,128)(2,1)S(1)}, bf16[256,384]{1,0:T(8,128)(2,1)S(1)}, u32[]{:S(2)}, u32[]{:S(2)}) collective-permute-start(bf16[256,384]{1,0:T(8,128)(2,1)S(1)} %dynamic-slice_select_fusion.1), channel_id=1, source_target_pairs={{0,8},{8,0},{16,24},{24,16},{1,9},{9,1},{17,25},{25,17},{2,10},{10... | collective-permute-start | bytes 589832 | tf_op jit(solution)/shard_map/ppermute | solution.py:811
  282.4 17.8 %collective-permute-start.5 = (bf16[8,48,384]{2,1,0:T(8,128)(2,1)S(1)}, bf16[8,48,384]{2,1,0:T(8,128)(2,1)S(1)}, u32[]{:S(2)}, u32[]{:S(2)}) collective-permute-start(bf16[8,48,384]{2,1,0:T(8,128)(2,1)S(1)} %copy-done.24), channel_id=1, source_target_pairs={{0,8},{8,0},{16,24},{24,16},{1,9},{9,1},{17,25},{25,17},{2,10},{10... | collective-permute-start | bytes 884744 | tf_op jit(solution)/shard_map/ppermute | solution.py:811
  282.5 12.3 %collective-permute-start.7 = (bf16[8,24,640]{2,1,0:T(8,128)(2,1)S(1)}, bf16[8,24,640]{2,1,0:T(8,128)(2,1)S(1)}, u32[]{:S(2)}, u32[]{:S(2)}) collective-permute-start(bf16[8,24,640]{2,1,0:T(8,128)(2,1)S(1)} %constant_dynamic-slice_fusion.1), channel_id=1, source_target_pairs={{0,16},{8,24},{16,0},{24,8},{1,17},{9,25},{17,1},{25,9},{2,18},{10... | collective-permute-start | bytes 737288 | tf_op jit(solution)/shard_map/ppermute | solution.py:811
  284.4 21.7 %collective-permute-start.8 = (bf16[8,24,768]{2,1,0:T(8,128)(2,1)S(1)}, bf16[8,24,768]{2,1,0:T(8,128)(2,1)S(1)}, u32[]{:S(2)}, u32[]{:S(2)}) collective-permute-start(bf16[8,24,768]{2,1,0:T(8,128)(2,1)S(1)} %constant_dynamic-slice_fusion), channel_id=1, source_target_pairs={{0,8},{8,0},{16,24},{24,16},{1,9},{9,1},{17,25},{25,17},{2,10},{10... | collective-permute-start | bytes 884744 | tf_op jit(solution)/shard_map/ppermute | solution.py:811
  300.3 11.6 %copy-start.34 = (bf16[512,384]{1,0:T(8,128)(2,1)S(1)}, bf16[512,384]{1,0:T(8,128)(2,1)}, u32[]{:S(2)}) copy-start(bf16[512,384]{1,0:T(8,128)(2,1)} %add_convert_fusion.3.refs_0_) | copy-start | bytes 1179652
  300.3 5.9 %collective-permute-start.6 = (bf16[8,24,384]{2,1,0:T(8,128)(2,1)S(1)}, bf16[8,24,384]{2,1,0:T(8,128)(2,1)S(1)}, u32[]{:S(2)}, u32[]{:S(2)}) collective-permute-start(bf16[8,24,384]{2,1,0:T(8,128)(2,1)S(1)} %constant_dynamic-slice_fusion.2), channel_id=1, source_target_pairs={{0,16},{8,24},{16,0},{24,8},{1,17},{9,25},{17,1},{25,9},{2,18},{10... | collective-permute-start | bytes 442376 | tf_op jit(solution)/shard_map/ppermute | solution.py:811
  307.2 20.9 %copy-start.46 = (bf16[96]{0:T(256)(128)(2,1)S(1)}, bf16[96]{0:T(256)(128)(2,1)}, u32[]{:S(2)}) copy-start(bf16[96]{0:T(256)(128)(2,1)} %param.22) | copy-start | bytes 580
  307.2 31.2 %all-to-all-start.3 = ((bf16[8,24,1792]{2,1,0:T(8,128)(2,1)}), bf16[8,24,1792]{2,1,0:T(8,128)(2,1)S(1)}, u32[]{:S(2)}, u32[]{:S(2)}) async-start(bf16[8,24,1792]{2,1,0:T(8,128)(2,1)} %pad_maximum_fusion), calls=%async_computation.6 | async-start | bytes 1376256 | tf_op jit(solution)/shard_map/all_to_all | solution.py:797
  312.0 7.4 %collective-permute-start.9 = (bf16[256,384]{1,0:T(8,128)(2,1)S(1)}, bf16[256,384]{1,0:T(8,128)(2,1)S(1)}, u32[]{:S(2)}, u32[]{:S(2)}) collective-permute-start(bf16[256,384]{1,0:T(8,128)(2,1)S(1)} %dynamic-slice_select_fusion), channel_id=1, source_target_pairs={{0,16},{8,24},{16,0},{24,8},{1,17},{9,25},{17,1},{25,9},{2,18},{10... | collective-permute-start | bytes 589832 | tf_op jit(solution)/shard_map/ppermute | solution.py:811
  314.8 7.1 %collective-permute-start.11 = (bf16[256,384]{1,0:T(8,128)(2,1)S(1)}, bf16[256,384]{1,0:T(8,128)(2,1)S(1)}, u32[]{:S(2)}, u32[]{:S(2)}) collective-permute-start(bf16[256,384]{1,0:T(8,128)(2,1)S(1)} %broadcast_select_fusion.1), channel_id=1, source_target_pairs={{0,8},{8,0},{16,24},{24,16},{1,9},{9,1},{17,25},{25,17},{2,10},{10... | collective-permute-start | bytes 589832 | tf_op jit(solution)/shard_map/ppermute | solution.py:811
  319.4 7.9 %collective-permute-start.10 = (bf16[256,384]{1,0:T(8,128)(2,1)S(1)}, bf16[256,384]{1,0:T(8,128)(2,1)S(1)}, u32[]{:S(2)}, u32[]{:S(2)}) collective-permute-start(bf16[256,384]{1,0:T(8,128)(2,1)S(1)} %fusion.35), channel_id=1, source_target_pairs={{0,16},{8,24},{16,0},{24,8},{1,17},{9,25},{17,1},{25,9},{2,18},{10... | collective-permute-start | bytes 589832 | tf_op jit(solution)/shard_map/ppermute | solution.py:811
  322.0 12.4 %collective-permute-start.13 = (bf16[512,384]{1,0:T(8,128)(2,1)S(1)}, bf16[512,384]{1,0:T(8,128)(2,1)S(1)}, u32[]{:S(2)}, u32[]{:S(2)}) collective-permute-start(bf16[512,384]{1,0:T(8,128)(2,1)S(1)} %maximum_select_fusion.3.refs_1_), channel_id=1, source_target_pairs={{0,16},{8,24},{16,0},{24,8},{1,17},{9,25},{17,1},{25,9},{2,18},{10... | collective-permute-start | bytes 1179656 | tf_op jit(solution)/shard_map/ppermute | solution.py:811
  327.4 8.6 %collective-permute-start.12 = (bf16[512,384]{1,0:T(8,128)(2,1)S(1)}, bf16[512,384]{1,0:T(8,128)(2,1)S(1)}, u32[]{:S(2)}, u32[]{:S(2)}) collective-permute-start(bf16[512,384]{1,0:T(8,128)(2,1)S(1)} %maximum_select_fusion.2.refs_0_), channel_id=1, source_target_pairs={{0,8},{8,0},{16,24},{24,16},{1,9},{9,1},{17,25},{25,17},{2,10},{10... | collective-permute-start | bytes 1179656 | tf_op jit(solution)/shard_map/ppermute | solution.py:811
  328.9 9.6 %copy-start.22 = (s32[2]{0:T(128)}, s32[2]{0:T(128)S(1)}, u32[]{:S(2)}) copy-start(s32[2]{0:T(128)S(1)} %pad_add_fusion.mine_ref) | copy-start | bytes 28
  341.7 7.9 %collective-permute-start.16 = (bf16[24,4352]{1,0:T(8,128)(2,1)}, bf16[24,4352]{1,0:T(8,128)(2,1)S(1)}, u32[]{:S(2)}, u32[]{:S(2)}) collective-permute-start(bf16[24,4352]{1,0:T(8,128)(2,1)} %get-tuple-element.79), channel_id=1, source_target_pairs={{0,8},{8,0},{16,24},{24,16},{1,9},{9,1},{17,25},{25,17},{2,10},{10... | collective-permute-start | bytes 626696 | tf_op jit(solution)/shard_map/ppermute | solution.py:811
  342.2 5.3 %collective-permute-start.14 = (bf16[24,2944]{1,0:T(8,128)(2,1)}, bf16[24,2944]{1,0:T(8,128)(2,1)S(1)}, u32[]{:S(2)}, u32[]{:S(2)}) collective-permute-start(bf16[24,2944]{1,0:T(8,128)(2,1)} %get-tuple-element.78), channel_id=1, source_target_pairs={{0,16},{8,24},{16,0},{24,8},{1,17},{9,25},{17,1},{25,9},{2,18},{10... | collective-permute-start | bytes 423944 | tf_op jit(solution)/shard_map/ppermute | solution.py:811
  343.7 3.8 %copy-start.42 = (bf16[24,2944]{1,0:T(8,128)(2,1)S(1)}, bf16[24,2944]{1,0:T(8,128)(2,1)}, u32[]{:S(2)}) copy-start(bf16[24,2944]{1,0:T(8,128)(2,1)} %get-tuple-element.78) | copy-start | bytes 423940
  343.7 5.8 %copy-start.41 = (bf16[24,4352]{1,0:T(8,128)(2,1)S(1)}, bf16[24,4352]{1,0:T(8,128)(2,1)}, u32[]{:S(2)}) copy-start(bf16[24,4352]{1,0:T(8,128)(2,1)} %get-tuple-element.79) | copy-start | bytes 626692
  343.7 7.6 %copy-start.32 = (bf16[768,1024]{1,0:T(8,128)(2,1)S(1)}, bf16[768,1024]{1,0:T(8,128)(2,1)}, u32[]{:S(2)}) copy-start(bf16[768,1024]{1,0:T(8,128)(2,1)} %get-tuple-element.93) | copy-start | bytes 4718596
  347.6 5.6 %copy-start.36 = (bf16[48,2944]{1,0:T(8,128)(2,1)}, bf16[48,2944]{1,0:T(8,128)(2,1)S(1)}, u32[]{:S(2)}) copy-start(bf16[48,2944]{1,0:T(8,128)(2,1)S(1)} %maximum_select_fusion.4.first_ref) | copy-start | bytes 847876
  347.6 6.7 %collective-permute-start.15 = (bf16[48,2944]{1,0:T(8,128)(2,1)S(1)}, bf16[48,2944]{1,0:T(8,128)(2,1)S(1)}, u32[]{:S(2)}, u32[]{:S(2)}) collective-permute-start(bf16[48,2944]{1,0:T(8,128)(2,1)S(1)} %maximum_select_fusion.4.first_ref), channel_id=1, source_target_pairs={{0,8},{8,0},{16,24},{24,16},{1,9},{9,1},{17,25},{25,17},{2,10},{10... | collective-permute-start | bytes 847880 | tf_op jit(solution)/shard_map/ppermute | solution.py:811
  349.6 3.6 copy-start.31
  349.6 8.1 %collective-permute-start.17 = (bf16[48,4352]{1,0:T(8,128)(2,1)S(1)}, bf16[48,4352]{1,0:T(8,128)(2,1)S(1)}, u32[]{:S(2)}, u32[]{:S(2)}) collective-permute-start(bf16[48,4352]{1,0:T(8,128)(2,1)S(1)} %maximum_select_fusion.1.last_ref), channel_id=1, source_target_pairs={{0,16},{8,24},{16,0},{24,8},{1,17},{9,25},{17,1},{25,9},{2,18},{10... | collective-permute-start | bytes 1253384 | tf_op jit(solution)/shard_map/ppermute | solution.py:811
  354.3 3.5 copy-start.40
  358.5 6.4 %copy-start.1 = (bf16[96,768]{1,0:T(8,128)(2,1)S(1)}, bf16[96,768]{1,0:T(8,128)(2,1)}, u32[]{:S(2)}) copy-start(bf16[96,768]{1,0:T(8,128)(2,1)} %param.27) | copy-start | bytes 442372
  (18 other events, 26.4 us)
Sparse Core Ops, SparseCore 0:
  10.5 42.8 all-gather.9
  55.6 40.2 all-gather.5
  100.0 37.1 all-gather.7
  174.0 43.9 reduce-scatter.3
  276.6 39.7 reduce-scatter.7
  318.5 40.1 reduce-scatter.5
Sparse Core Ops, SparseCore 1:
  63.2 69.1 all-reduce.4
  185.3 110.7 all-reduce.6
